TPU v7x, 512 devices: a whole 4x8x8 slice. The times are simulated.
512 devices in a mesh: section: 8 (over z), dom: 64 (over x, y, core).
Axes of the slice: x: 4, y: 8, z: 8, core: 2. Of those that a mesh axis runs over, the one named last changes fastest.
Arguments:
- initial_embed: bfloat16 [4, 24576, 256], P(None, 'dom'), may hold values from -6 to 6
- out_cotangent: bfloat16 [4, 24576, 256], P(None, 'dom'), may hold values from -6 to 6
- layer_weights: bfloat16 [8, 256, 256], P('section'), may hold values from -0.375 to 0.375
- stale_halo: bfloat16 [8, 4, 16384, 256], P('section', None, 'dom'), may hold values from -6 to 6
- tile_values: bfloat16 [4, 768, 128, 128], P(None, 'dom'), may hold values from -0.375 to 0.375
- tile_rows: int32 [4, 768], P(None, 'dom'), may hold values from 0 to 2
- tile_cols: int32 [4, 768], P(None, 'dom'), may hold values from 0 to 4
- tile_count: int32 [4, 64], P(None, 'dom'), may hold values from 3 to 12, as said below
- send_blocks: int32 [4, 128], P(None, 'dom'), may hold values from 0 to 2
Outputs:
- weight_grad: float32 [8, 256, 256], P('section')
- fresh_halo: bfloat16 [8, 4, 16384, 256], P('section', None, 'dom')
- initial_grad: float32 [4, 24576, 256], P(None, 'dom', 'section')
Inputs may be any that keep to these rules, and one draw needn't show every extreme that they name: `tile_count`: in every span some partition has all 12 slots live.
All inputs are finite; a program needn't handle non-finite values.
Results may differ from a plain program's by a relative error of at most 0.03.
Values may be sent and summed in bfloat16 or wider, within the bound.
No kernel may reach another device: no remote copies, remote signals or barrier semaphores. Data moves between devices by JAX's collectives and lax.ppermute only.
A program may use at most 64 MiB of HBM per device.

v0:
```python
import math

import jax
import jax.numpy as jnp
from jax import lax
from jax.sharding import PartitionSpec as P

ALPHA = 0.1
LAMBDA_RATE = 0.5


def padded(value, sides, width):
    for axis, dim in sides:
        size, length = (lax.axis_size(axis), value.shape[dim])
        up = [(i, (i + 1) % size) for i in range(size)]
        down = [(j, i) for i, j in up]
        last = lax.slice_in_dim(value, length - width, length, axis=dim)
        first = lax.slice_in_dim(value, 0, width, axis=dim)
        before = lax.ppermute(last, axis, up)
        after = lax.ppermute(first, axis, down)
        value = jnp.concatenate([before, value, after], axis=dim)
    return value


def shifted(value, axis, by):
    size = lax.axis_size(axis)
    pairs = [(i, i + by) for i in range(size) if 0 <= i + by < size]
    return lax.ppermute(value, axis, pairs)


def layer_rate(index):
    return jnp.log(LAMBDA_RATE / (jnp.asarray(index, jnp.float32) + 1.0) + 1.0)


def spread_forward(extended, values, row_ids, col_ids, count, nblocks):
    live_mask = (jnp.arange(values.shape[0]) < count).astype(jnp.float32)
    picker = jax.nn.one_hot(col_ids, extended.shape[0], dtype=jnp.bfloat16)
    picked = jnp.einsum("tn,nrh->trh", picker, extended, preferred_element_type=jnp.float32).astype(
        jnp.bfloat16
    )
    products = jnp.einsum("tij,tjh->tih", values, picked, preferred_element_type=jnp.float32)
    placer = jax.nn.one_hot(row_ids, nblocks, dtype=jnp.float32) * live_mask[:, None]
    return jnp.einsum("tb,tih->bih", placer, products, precision=lax.Precision.HIGHEST)


def spread_backward(gradient, values, row_ids, col_ids, count, nblocks):
    live_mask = (jnp.arange(values.shape[0]) < count).astype(jnp.float32)
    picker = jax.nn.one_hot(row_ids, nblocks, dtype=jnp.bfloat16)
    picked = jnp.einsum("tb,bih->tih", picker, gradient, preferred_element_type=jnp.float32).astype(
        jnp.bfloat16
    )
    products = jnp.einsum("tji,tjh->tih", values, picked, preferred_element_type=jnp.float32)
    placer = jax.nn.one_hot(col_ids, nblocks, dtype=jnp.float32) * live_mask[:, None]
    return jnp.einsum("tb,tih->bih", placer, products, precision=lax.Precision.HIGHEST)


def store_at(buffer, layer, slot_index, value, valid):
    previous = buffer[layer, slot_index]
    updated = jnp.where(valid, value, previous)
    starts = (jnp.int32(layer), slot_index) + tuple(
        (jnp.int32(0) for axis_pos in range(value.ndim))
    )
    return lax.dynamic_update_slice(buffer, updated[None, None], starts)


def shards(
    initial_embed,
    out_cotangent,
    layer_weights,
    stale_halo,
    tile_values,
    tile_rows,
    tile_cols,
    tile_count,
    send_blocks,
):
    section = lax.axis_index("section")
    sections = lax.axis_size("section")
    spans, row_count, width = initial_embed.shape
    depth = layer_weights.shape[0]
    tile_size = tile_values.shape[-1]
    nblocks = row_count // tile_size
    ticks = spans + sections - 1
    node_total = row_count * lax.axis_size("dom")
    mix_store = jnp.zeros((depth, spans, row_count, width), jnp.bfloat16)
    pre_store = jnp.zeros((depth, spans, row_count, width), jnp.float32)
    send_store = jnp.zeros((depth, spans, 2 * tile_size, width), jnp.bfloat16)
    fresh = jnp.zeros((depth, spans, 2 * tile_size, width), jnp.bfloat16)
    incoming = jnp.zeros((row_count, width), jnp.bfloat16)

    def forward_tick(tick, carry):
        incoming, mix_store, pre_store, send_store, fresh = carry
        span_now = tick - section
        valid = (span_now >= 0) & (span_now < spans)
        slot_index = jnp.clip(span_now, 0, spans - 1)
        layer_in = jnp.where(section == 0, initial_embed[slot_index], incoming)
        initial = initial_embed[slot_index]
        values = tile_values[slot_index]
        row_ids = tile_rows[slot_index]
        col_ids = tile_cols[slot_index]
        count = tile_count[slot_index, 0]
        blocks = layer_in.reshape(nblocks, tile_size, width)
        outgoing = jnp.take(blocks, send_blocks[slot_index], axis=0).reshape(2 * tile_size, width)
        rims = padded(outgoing, (("dom", 0),), tile_size)
        received = jnp.concatenate([rims[:tile_size], rims[3 * tile_size :]], axis=0)
        fresh = store_at(fresh, 0, slot_index, received, valid)
        beta_rate = layer_rate(section * depth + 0)
        halo_blocks = stale_halo[0, slot_index].reshape(2, tile_size, width)
        extended = jnp.concatenate([blocks, halo_blocks], axis=0)
        aggregate = spread_forward(extended, values, row_ids, col_ids, count, nblocks).reshape(
            row_count, width
        )
        mixed = ((1.0 - ALPHA) * aggregate + ALPHA * initial.astype(jnp.float32)).astype(
            jnp.bfloat16
        )
        preact = (1.0 - beta_rate) * mixed.astype(jnp.float32) + beta_rate * jnp.dot(
            mixed, layer_weights[0], preferred_element_type=jnp.float32
        )
        mix_store = store_at(mix_store, 0, slot_index, mixed, valid)
        pre_store = store_at(pre_store, 0, slot_index, preact, valid)
        layer_in = jax.nn.silu(preact).astype(jnp.bfloat16)
        incoming = shifted(layer_in, "section", 1)
        return (incoming, mix_store, pre_store, send_store, fresh)

    incoming, mix_store, pre_store, send_store, fresh = lax.fori_loop(
        0, ticks, forward_tick, (incoming, mix_store, pre_store, send_store, fresh)
    )
    weight_acc = jnp.zeros((depth, width, width), jnp.float32)
    initial_acc = jnp.zeros((spans, row_count, width), jnp.float32)
    incoming = jnp.zeros((row_count, width), jnp.bfloat16)

    def backward_tick(tick, carry):
        incoming, weight_acc, initial_acc = carry
        span_now = tick - (sections - 1 - section)
        valid = (span_now >= 0) & (span_now < spans)
        slot_index = jnp.clip(span_now, 0, spans - 1)
        grad_in = jnp.where(section == sections - 1, out_cotangent[slot_index], incoming)
        values = tile_values[slot_index]
        row_ids = tile_rows[slot_index]
        col_ids = tile_cols[slot_index]
        count = tile_count[slot_index, 0]
        weight_terms = []
        initial_term = jnp.zeros((row_count, width), jnp.float32)
        gathered = jnp.zeros((row_count, width), jnp.float32)
        for layer in reversed(range(depth)):
            beta_rate = layer_rate(section * depth + layer)
            preact = pre_store[layer, slot_index]
            mixed = mix_store[layer, slot_index]
            sigmoid = jax.nn.sigmoid(preact)
            delta = (
                grad_in.astype(jnp.float32) * sigmoid * (1.0 + preact * (1.0 - sigmoid))
            ).astype(jnp.bfloat16)
            weight_terms.insert(
                0,
                lax.dot_general(
                    mixed, delta, (((0,), (0,)), ((), ())), preferred_element_type=jnp.float32
                ),
            )
            dmixed = (1.0 - beta_rate) * delta.astype(jnp.float32) + beta_rate * lax.dot_general(
                delta,
                layer_weights[layer],
                (((1,), (1,)), ((), ())),
                preferred_element_type=jnp.float32,
            )
            initial_term = ALPHA * dmixed
            rounded = dmixed.astype(jnp.bfloat16).reshape(nblocks, tile_size, width)
            backward = spread_backward(rounded, values, row_ids, col_ids, count, nblocks).reshape(
                row_count, width
            )
            gathered = (1.0 - ALPHA) * backward
            grad_in = gathered.astype(jnp.bfloat16)
        initial_term = initial_term + jnp.where(section == 0, gathered, 0.0)
        weight_tick = jnp.where(valid, jnp.stack(weight_terms), 0.0)
        initial_term = jnp.where(valid, initial_term, 0.0)
        weight_acc = weight_acc + weight_tick
        current = lax.dynamic_index_in_dim(initial_acc, slot_index, 0, keepdims=False)
        initial_acc = lax.dynamic_update_index_in_dim(
            initial_acc, current + initial_term, slot_index, 0
        )
        incoming = shifted(grad_in, "section", -1)
        return (incoming, weight_acc, initial_acc)

    incoming, weight_acc, initial_acc = lax.fori_loop(
        0, ticks, backward_tick, (incoming, weight_acc, initial_acc)
    )
    weight_acc = lax.psum(weight_acc, "dom")
    weight_grad = weight_acc / math.sqrt(spans * node_total)
    initial_grad = lax.psum_scatter(initial_acc, "section", scatter_dimension=2, tiled=True)
    return (weight_grad, fresh, initial_grad)


def solution(mesh):
    placed = (
        P(None, "dom", None),
        P(None, "dom", None),
        P("section", None, None),
        P("section", None, "dom", None),
        P(None, "dom", None, None),
        P(None, "dom"),
        P(None, "dom"),
        P(None, "dom"),
        P(None, "dom"),
    )
    return jax.shard_map(
        shards,
        mesh=mesh,
        in_specs=placed,
        out_specs=(
            P("section", None, None),
            P("section", None, "dom", None),
            P(None, "dom", "section"),
        ),
        check_vma=False,
    )
```

profile of v0, /device:TPU:1, one launch (start us, length us, event | category | flops | bytes accessed | tf_op | source)
XLA Modules:
  0.0 683.9 jit_solution(3293949739717849479)
XLA Ops:
  11.0 288.4 %while.41 = (s32[]{:T(128)}, bf16[384,256]{1,0:T(8,128)(2,1)S(1)}, bf16[1,4,384,256]{3,2,1,0:T(8,128)(2,1)}, f32[1,4,384,256]{3,2,1,0:T(8,128)S(1)}, bf16[1,4,25...) while((s32[]{:T(128)}, bf16[384,256]{1,0:T(8,128)(2,1)S(1)}, ...), condition=%wide.region_1.2_spmd, body=%wide.region_0.1_spmd.sunk | while | flops 172983472 | bytes 16651110 | solution.py:125
  15.6 2.0 fusion.107
  19.8 4.8 collective-permute-start
  25.9 5.2 collective-permute-start.1
  42.4 2.0 fusion.107
  46.6 4.0 collective-permute-start
  52.0 8.4 %collective-permute-start.1 = (bf16[128,256]{1,0:T(8,128)(2,1)}, bf16[128,256]{1,0:T(8,128)(2,1)S(1)}, u32[]{:S(2)}, u32[]{:S(2)}) collective-permute-start(bf16[128,256]{1,0:T(8,128)(2,1)} %get-tuple-element.1114), channel_id=1, source_target_pairs={{1,0},{2,1},{3,2},{4,3},{5,4},{6,5},{7,6},{8,7},{9,8},{10,9},{11,1... | collective-permute-start | bytes 196616 | tf_op jit(solution)/shard_map/while/body/eval_jaxpr/ppermute | solution.py:20
  71.3 2.0 fusion.107
  75.5 4.0 collective-permute-start
  80.8 6.3 collective-permute-start.1
  98.1 2.0 fusion.107
  102.3 5.2 collective-permute-start
  108.8 6.3 collective-permute-start.1
  126.1 2.0 fusion.107
  130.3 3.1 collective-permute-start
  134.7 7.0 %collective-permute-start.1 = (bf16[128,256]{1,0:T(8,128)(2,1)}, bf16[128,256]{1,0:T(8,128)(2,1)S(1)}, u32[]{:S(2)}, u32[]{:S(2)}) collective-permute-start(bf16[128,256]{1,0:T(8,128)(2,1)} %get-tuple-element.1114), channel_id=1, source_target_pairs={{1,0},{2,1},{3,2},{4,3},{5,4},{6,5},{7,6},{8,7},{9,8},{10,9},{11,1... | collective-permute-start | bytes 196616 | tf_op jit(solution)/shard_map/while/body/eval_jaxpr/ppermute | solution.py:20
  151.6 2.0 fusion.107
  155.8 3.4 collective-permute-start
  160.5 7.0 %collective-permute-start.1 = (bf16[128,256]{1,0:T(8,128)(2,1)}, bf16[128,256]{1,0:T(8,128)(2,1)S(1)}, u32[]{:S(2)}, u32[]{:S(2)}) collective-permute-start(bf16[128,256]{1,0:T(8,128)(2,1)} %get-tuple-element.1114), channel_id=1, source_target_pairs={{1,0},{2,1},{3,2},{4,3},{5,4},{6,5},{7,6},{8,7},{9,8},{10,9},{11,1... | collective-permute-start | bytes 196616 | tf_op jit(solution)/shard_map/while/body/eval_jaxpr/ppermute | solution.py:20
  177.4 2.0 fusion.107
  181.6 3.1 collective-permute-start
  186.1 7.9 %collective-permute-start.1 = (bf16[128,256]{1,0:T(8,128)(2,1)}, bf16[128,256]{1,0:T(8,128)(2,1)S(1)}, u32[]{:S(2)}, u32[]{:S(2)}) collective-permute-start(bf16[128,256]{1,0:T(8,128)(2,1)} %get-tuple-element.1114), channel_id=1, source_target_pairs={{1,0},{2,1},{3,2},{4,3},{5,4},{6,5},{7,6},{8,7},{9,8},{10,9},{11,1... | collective-permute-start | bytes 196616 | tf_op jit(solution)/shard_map/while/body/eval_jaxpr/ppermute | solution.py:20
  203.9 2.0 fusion.107
  211.4 8.0 %collective-permute-start.1 = (bf16[128,256]{1,0:T(8,128)(2,1)}, bf16[128,256]{1,0:T(8,128)(2,1)S(1)}, u32[]{:S(2)}, u32[]{:S(2)}) collective-permute-start(bf16[128,256]{1,0:T(8,128)(2,1)} %get-tuple-element.1114), channel_id=1, source_target_pairs={{1,0},{2,1},{3,2},{4,3},{5,4},{6,5},{7,6},{8,7},{9,8},{10,9},{11,1... | collective-permute-start | bytes 196616 | tf_op jit(solution)/shard_map/while/body/eval_jaxpr/ppermute | solution.py:20
  229.2 2.0 fusion.107
  236.7 7.3 %collective-permute-start.1 = (bf16[128,256]{1,0:T(8,128)(2,1)}, bf16[128,256]{1,0:T(8,128)(2,1)S(1)}, u32[]{:S(2)}, u32[]{:S(2)}) collective-permute-start(bf16[128,256]{1,0:T(8,128)(2,1)} %get-tuple-element.1114), channel_id=1, source_target_pairs={{1,0},{2,1},{3,2},{4,3},{5,4},{6,5},{7,6},{8,7},{9,8},{10,9},{11,1... | collective-permute-start | bytes 196616 | tf_op jit(solution)/shard_map/while/body/eval_jaxpr/ppermute | solution.py:20
  253.9 2.0 fusion.107
  258.1 2.5 collective-permute-start
  261.9 7.3 %collective-permute-start.1 = (bf16[128,256]{1,0:T(8,128)(2,1)}, bf16[128,256]{1,0:T(8,128)(2,1)S(1)}, u32[]{:S(2)}, u32[]{:S(2)}) collective-permute-start(bf16[128,256]{1,0:T(8,128)(2,1)} %get-tuple-element.1114), channel_id=1, source_target_pairs={{1,0},{2,1},{3,2},{4,3},{5,4},{6,5},{7,6},{8,7},{9,8},{10,9},{11,1... | collective-permute-start | bytes 196616 | tf_op jit(solution)/shard_map/while/body/eval_jaxpr/ppermute | solution.py:20
  279.2 2.0 fusion.107
  286.7 7.3 %collective-permute-start.1 = (bf16[128,256]{1,0:T(8,128)(2,1)}, bf16[128,256]{1,0:T(8,128)(2,1)S(1)}, u32[]{:S(2)}, u32[]{:S(2)}) collective-permute-start(bf16[128,256]{1,0:T(8,128)(2,1)} %get-tuple-element.1114), channel_id=1, source_target_pairs={{1,0},{2,1},{3,2},{4,3},{5,4},{6,5},{7,6},{8,7},{9,8},{10,9},{11,1... | collective-permute-start | bytes 196616 | tf_op jit(solution)/shard_map/while/body/eval_jaxpr/ppermute | solution.py:20
  301.3 171.7 %while.42 = (s32[]{:T(128)}, bf16[384,256]{1,0:T(8,128)(2,1)}, f32[1,256,256]{2,1,0:T(8,128)}, f32[4,384,256]{1,2,0:T(8,128)}, s32[]{:T(128)}, /*index=5*/s32[4,...) while((s32[]{:T(128)}, bf16[384,256]{1,0:T(8,128)(2,1)}, ...), condition=%wide.region_3.4_spmd.clone, body=%wide.region_2.3_spmd.clone.sunk | while | flops 220692608 | bytes 17498900 | solution.py:183
  306.9 2.1 broadcast_select_fusion.5
  322.0 2.1 broadcast_select_fusion.5
  337.1 2.1 broadcast_select_fusion.5
  352.2 2.1 broadcast_select_fusion.5
  367.3 2.1 broadcast_select_fusion.5
  382.4 2.1 broadcast_select_fusion.5
  397.6 2.1 broadcast_select_fusion.5
  412.7 2.1 broadcast_select_fusion.5
  420.4 2.9 collective-permute-done.3
  428.8 2.1 broadcast_select_fusion.5
  436.6 3.0 collective-permute-done.3
  445.2 2.1 broadcast_select_fusion.5
  452.9 3.0 collective-permute-done.3
  461.5 2.1 broadcast_select_fusion.5
  469.2 3.8 collective-permute-done.3
  473.6 201.1 %all-reduce.2.cloned.1.call-done = f32[1,256,256]{2,1,0:T(8,128)} async-done(((f32[1,256,256]{2,1,0:T(8,128)}), f32[1,256,256]{2,1,0:T(8,128)}) %all-reduce.2.cloned.1.call-update) | async-done | bytes 262160 | tf_op jit(solution)/shard_map/psum | solution.py:186
  (549 shorter events, 297.5 us)
Async XLA Ops:
  8.0 666.7 %all-reduce.2.cloned.1.call-start = ((), (), s32[]{:S(2)}) async-start(), calls=%async_computation.1 | async-start | bytes 524288 | tf_op jit(solution)/shard_map/psum | solution.py:186
  19.8 18.1 %collective-permute-start = (bf16[384,256]{1,0:T(8,128)(2,1)}, bf16[384,256]{1,0:T(8,128)(2,1)S(1)}, u32[]{:S(2)}, u32[]{:S(2)}) collective-permute-start(bf16[384,256]{1,0:T(8,128)(2,1)} %get-tuple-element.1112), channel_id=1, source_target_pairs={{0,64},{64,128},{128,192},{192,256},{256,320},{320,384},{384,448},... | collective-permute-start | bytes 589832 | tf_op jit(solution)/shard_map/while/body/eval_jaxpr/ppermute | solution.py:28
  25.9 10.0 %collective-permute-start.1 = (bf16[128,256]{1,0:T(8,128)(2,1)}, bf16[128,256]{1,0:T(8,128)(2,1)S(1)}, u32[]{:S(2)}, u32[]{:S(2)}) collective-permute-start(bf16[128,256]{1,0:T(8,128)(2,1)} %get-tuple-element.1114), channel_id=1, source_target_pairs={{1,0},{2,1},{3,2},{4,3},{5,4},{6,5},{7,6},{8,7},{9,8},{10,9},{11,1... | collective-permute-start | bytes 196616 | tf_op jit(solution)/shard_map/while/body/eval_jaxpr/ppermute | solution.py:20
  31.2 5.1 collective-permute-start.2
  46.6 20.1 %collective-permute-start = (bf16[384,256]{1,0:T(8,128)(2,1)}, bf16[384,256]{1,0:T(8,128)(2,1)S(1)}, u32[]{:S(2)}, u32[]{:S(2)}) collective-permute-start(bf16[384,256]{1,0:T(8,128)(2,1)} %get-tuple-element.1112), channel_id=1, source_target_pairs={{0,64},{64,128},{128,192},{192,256},{256,320},{320,384},{384,448},... | collective-permute-start | bytes 589832 | tf_op jit(solution)/shard_map/while/body/eval_jaxpr/ppermute | solution.py:28
  52.0 13.2 %collective-permute-start.1 = (bf16[128,256]{1,0:T(8,128)(2,1)}, bf16[128,256]{1,0:T(8,128)(2,1)S(1)}, u32[]{:S(2)}, u32[]{:S(2)}) collective-permute-start(bf16[128,256]{1,0:T(8,128)(2,1)} %get-tuple-element.1114), channel_id=1, source_target_pairs={{1,0},{2,1},{3,2},{4,3},{5,4},{6,5},{7,6},{8,7},{9,8},{10,9},{11,1... | collective-permute-start | bytes 196616 | tf_op jit(solution)/shard_map/while/body/eval_jaxpr/ppermute | solution.py:20
  60.4 4.7 collective-permute-start.2
  75.5 18.0 %collective-permute-start = (bf16[384,256]{1,0:T(8,128)(2,1)}, bf16[384,256]{1,0:T(8,128)(2,1)S(1)}, u32[]{:S(2)}, u32[]{:S(2)}) collective-permute-start(bf16[384,256]{1,0:T(8,128)(2,1)} %get-tuple-element.1112), channel_id=1, source_target_pairs={{0,64},{64,128},{128,192},{192,256},{256,320},{320,384},{384,448},... | collective-permute-start | bytes 589832 | tf_op jit(solution)/shard_map/while/body/eval_jaxpr/ppermute | solution.py:28
  80.8 11.1 %collective-permute-start.1 = (bf16[128,256]{1,0:T(8,128)(2,1)}, bf16[128,256]{1,0:T(8,128)(2,1)S(1)}, u32[]{:S(2)}, u32[]{:S(2)}) collective-permute-start(bf16[128,256]{1,0:T(8,128)(2,1)} %get-tuple-element.1114), channel_id=1, source_target_pairs={{1,0},{2,1},{3,2},{4,3},{5,4},{6,5},{7,6},{8,7},{9,8},{10,9},{11,1... | collective-permute-start | bytes 196616 | tf_op jit(solution)/shard_map/while/body/eval_jaxpr/ppermute | solution.py:20
  87.2 4.7 collective-permute-start.2
  102.3 19.2 %collective-permute-start = (bf16[384,256]{1,0:T(8,128)(2,1)}, bf16[384,256]{1,0:T(8,128)(2,1)S(1)}, u32[]{:S(2)}, u32[]{:S(2)}) collective-permute-start(bf16[384,256]{1,0:T(8,128)(2,1)} %get-tuple-element.1112), channel_id=1, source_target_pairs={{0,64},{64,128},{128,192},{192,256},{256,320},{320,384},{384,448},... | collective-permute-start | bytes 589832 | tf_op jit(solution)/shard_map/while/body/eval_jaxpr/ppermute | solution.py:28
  108.8 11.1 %collective-permute-start.1 = (bf16[128,256]{1,0:T(8,128)(2,1)}, bf16[128,256]{1,0:T(8,128)(2,1)S(1)}, u32[]{:S(2)}, u32[]{:S(2)}) collective-permute-start(bf16[128,256]{1,0:T(8,128)(2,1)} %get-tuple-element.1114), channel_id=1, source_target_pairs={{1,0},{2,1},{3,2},{4,3},{5,4},{6,5},{7,6},{8,7},{9,8},{10,9},{11,1... | collective-permute-start | bytes 196616 | tf_op jit(solution)/shard_map/while/body/eval_jaxpr/ppermute | solution.py:20
  115.2 4.7 collective-permute-start.2
  130.3 16.7 %collective-permute-start = (bf16[384,256]{1,0:T(8,128)(2,1)}, bf16[384,256]{1,0:T(8,128)(2,1)S(1)}, u32[]{:S(2)}, u32[]{:S(2)}) collective-permute-start(bf16[384,256]{1,0:T(8,128)(2,1)} %get-tuple-element.1112), channel_id=1, source_target_pairs={{0,64},{64,128},{128,192},{192,256},{256,320},{320,384},{384,448},... | collective-permute-start | bytes 589832 | tf_op jit(solution)/shard_map/while/body/eval_jaxpr/ppermute | solution.py:28
  134.7 10.7 %collective-permute-start.1 = (bf16[128,256]{1,0:T(8,128)(2,1)}, bf16[128,256]{1,0:T(8,128)(2,1)S(1)}, u32[]{:S(2)}, u32[]{:S(2)}) collective-permute-start(bf16[128,256]{1,0:T(8,128)(2,1)} %get-tuple-element.1114), channel_id=1, source_target_pairs={{1,0},{2,1},{3,2},{4,3},{5,4},{6,5},{7,6},{8,7},{9,8},{10,9},{11,1... | collective-permute-start | bytes 196616 | tf_op jit(solution)/shard_map/while/body/eval_jaxpr/ppermute | solution.py:20
  141.7 3.7 collective-permute-start.2
  155.8 17.1 %collective-permute-start = (bf16[384,256]{1,0:T(8,128)(2,1)}, bf16[384,256]{1,0:T(8,128)(2,1)S(1)}, u32[]{:S(2)}, u32[]{:S(2)}) collective-permute-start(bf16[384,256]{1,0:T(8,128)(2,1)} %get-tuple-element.1112), channel_id=1, source_target_pairs={{0,64},{64,128},{128,192},{192,256},{256,320},{320,384},{384,448},... | collective-permute-start | bytes 589832 | tf_op jit(solution)/shard_map/while/body/eval_jaxpr/ppermute | solution.py:28
  160.5 10.7 %collective-permute-start.1 = (bf16[128,256]{1,0:T(8,128)(2,1)}, bf16[128,256]{1,0:T(8,128)(2,1)S(1)}, u32[]{:S(2)}, u32[]{:S(2)}) collective-permute-start(bf16[128,256]{1,0:T(8,128)(2,1)} %get-tuple-element.1114), channel_id=1, source_target_pairs={{1,0},{2,1},{3,2},{4,3},{5,4},{6,5},{7,6},{8,7},{9,8},{10,9},{11,1... | collective-permute-start | bytes 196616 | tf_op jit(solution)/shard_map/while/body/eval_jaxpr/ppermute | solution.py:20
  167.5 3.7 collective-permute-start.2
  181.6 17.7 %collective-permute-start = (bf16[384,256]{1,0:T(8,128)(2,1)}, bf16[384,256]{1,0:T(8,128)(2,1)S(1)}, u32[]{:S(2)}, u32[]{:S(2)}) collective-permute-start(bf16[384,256]{1,0:T(8,128)(2,1)} %get-tuple-element.1112), channel_id=1, source_target_pairs={{0,64},{64,128},{128,192},{192,256},{256,320},{320,384},{384,448},... | collective-permute-start | bytes 589832 | tf_op jit(solution)/shard_map/while/body/eval_jaxpr/ppermute | solution.py:28
  186.1 11.7 %collective-permute-start.1 = (bf16[128,256]{1,0:T(8,128)(2,1)}, bf16[128,256]{1,0:T(8,128)(2,1)S(1)}, u32[]{:S(2)}, u32[]{:S(2)}) collective-permute-start(bf16[128,256]{1,0:T(8,128)(2,1)} %get-tuple-element.1114), channel_id=1, source_target_pairs={{1,0},{2,1},{3,2},{4,3},{5,4},{6,5},{7,6},{8,7},{9,8},{10,9},{11,1... | collective-permute-start | bytes 196616 | tf_op jit(solution)/shard_map/while/body/eval_jaxpr/ppermute | solution.py:20
  194.0 3.7 collective-permute-start.2
  208.1 16.5 %collective-permute-start = (bf16[384,256]{1,0:T(8,128)(2,1)}, bf16[384,256]{1,0:T(8,128)(2,1)S(1)}, u32[]{:S(2)}, u32[]{:S(2)}) collective-permute-start(bf16[384,256]{1,0:T(8,128)(2,1)} %get-tuple-element.1112), channel_id=1, source_target_pairs={{0,64},{64,128},{128,192},{192,256},{256,320},{320,384},{384,448},... | collective-permute-start | bytes 589832 | tf_op jit(solution)/shard_map/while/body/eval_jaxpr/ppermute | solution.py:28
  211.4 11.7 %collective-permute-start.1 = (bf16[128,256]{1,0:T(8,128)(2,1)}, bf16[128,256]{1,0:T(8,128)(2,1)S(1)}, u32[]{:S(2)}, u32[]{:S(2)}) collective-permute-start(bf16[128,256]{1,0:T(8,128)(2,1)} %get-tuple-element.1114), channel_id=1, source_target_pairs={{1,0},{2,1},{3,2},{4,3},{5,4},{6,5},{7,6},{8,7},{9,8},{10,9},{11,1... | collective-permute-start | bytes 196616 | tf_op jit(solution)/shard_map/while/body/eval_jaxpr/ppermute | solution.py:20
  219.3 3.7 collective-permute-start.2
  233.4 15.9 %collective-permute-start = (bf16[384,256]{1,0:T(8,128)(2,1)}, bf16[384,256]{1,0:T(8,128)(2,1)S(1)}, u32[]{:S(2)}, u32[]{:S(2)}) collective-permute-start(bf16[384,256]{1,0:T(8,128)(2,1)} %get-tuple-element.1112), channel_id=1, source_target_pairs={{0,64},{64,128},{128,192},{192,256},{256,320},{320,384},{384,448},... | collective-permute-start | bytes 589832 | tf_op jit(solution)/shard_map/while/body/eval_jaxpr/ppermute | solution.py:28
  236.7 11.1 %collective-permute-start.1 = (bf16[128,256]{1,0:T(8,128)(2,1)}, bf16[128,256]{1,0:T(8,128)(2,1)S(1)}, u32[]{:S(2)}, u32[]{:S(2)}) collective-permute-start(bf16[128,256]{1,0:T(8,128)(2,1)} %get-tuple-element.1114), channel_id=1, source_target_pairs={{1,0},{2,1},{3,2},{4,3},{5,4},{6,5},{7,6},{8,7},{9,8},{10,9},{11,1... | collective-permute-start | bytes 196616 | tf_op jit(solution)/shard_map/while/body/eval_jaxpr/ppermute | solution.py:20
  244.0 3.7 collective-permute-start.2
  258.1 16.5 %collective-permute-start = (bf16[384,256]{1,0:T(8,128)(2,1)}, bf16[384,256]{1,0:T(8,128)(2,1)S(1)}, u32[]{:S(2)}, u32[]{:S(2)}) collective-permute-start(bf16[384,256]{1,0:T(8,128)(2,1)} %get-tuple-element.1112), channel_id=1, source_target_pairs={{0,64},{64,128},{128,192},{192,256},{256,320},{320,384},{384,448},... | collective-permute-start | bytes 589832 | tf_op jit(solution)/shard_map/while/body/eval_jaxpr/ppermute | solution.py:28
  261.9 11.1 %collective-permute-start.1 = (bf16[128,256]{1,0:T(8,128)(2,1)}, bf16[128,256]{1,0:T(8,128)(2,1)S(1)}, u32[]{:S(2)}, u32[]{:S(2)}) collective-permute-start(bf16[128,256]{1,0:T(8,128)(2,1)} %get-tuple-element.1114), channel_id=1, source_target_pairs={{1,0},{2,1},{3,2},{4,3},{5,4},{6,5},{7,6},{8,7},{9,8},{10,9},{11,1... | collective-permute-start | bytes 196616 | tf_op jit(solution)/shard_map/while/body/eval_jaxpr/ppermute | solution.py:20
  269.3 3.7 collective-permute-start.2
  283.4 16.0 %collective-permute-start = (bf16[384,256]{1,0:T(8,128)(2,1)}, bf16[384,256]{1,0:T(8,128)(2,1)S(1)}, u32[]{:S(2)}, u32[]{:S(2)}) collective-permute-start(bf16[384,256]{1,0:T(8,128)(2,1)} %get-tuple-element.1112), channel_id=1, source_target_pairs={{0,64},{64,128},{128,192},{192,256},{256,320},{320,384},{384,448},... | collective-permute-start | bytes 589832 | tf_op jit(solution)/shard_map/while/body/eval_jaxpr/ppermute | solution.py:28
  286.7 11.1 %collective-permute-start.1 = (bf16[128,256]{1,0:T(8,128)(2,1)}, bf16[128,256]{1,0:T(8,128)(2,1)S(1)}, u32[]{:S(2)}, u32[]{:S(2)}) collective-permute-start(bf16[128,256]{1,0:T(8,128)(2,1)} %get-tuple-element.1114), channel_id=1, source_target_pairs={{1,0},{2,1},{3,2},{4,3},{5,4},{6,5},{7,6},{8,7},{9,8},{10,9},{11,1... | collective-permute-start | bytes 196616 | tf_op jit(solution)/shard_map/while/body/eval_jaxpr/ppermute | solution.py:20
  294.0 3.7 collective-permute-start.2
  309.7 6.7 collective-permute-start.3
  324.8 6.7 collective-permute-start.3
  339.9 6.7 collective-permute-start.3
  355.0 6.7 collective-permute-start.3
  370.1 6.7 collective-permute-start.3
  385.2 6.7 collective-permute-start.3
  400.4 6.7 collective-permute-start.3
  415.5 7.8 %collective-permute-start.3 = (bf16[384,256]{1,0:T(8,128)(2,1)}, bf16[384,256]{1,0:T(8,128)(2,1)}, u32[]{:S(2)}, u32[]{:S(2)}) collective-permute-start(bf16[384,256]{1,0:T(8,128)(2,1)} %bitcast.201), channel_id=1, source_target_pairs={{64,0},{128,64},{192,128},{256,192},{320,256},{384,320},{448,384},... | collective-permute-start | bytes 589832 | tf_op jit(solution)/shard_map/while/body/eval_jaxpr/ppermute | solution.py:28
  431.6 7.9 %collective-permute-start.3 = (bf16[384,256]{1,0:T(8,128)(2,1)}, bf16[384,256]{1,0:T(8,128)(2,1)}, u32[]{:S(2)}, u32[]{:S(2)}) collective-permute-start(bf16[384,256]{1,0:T(8,128)(2,1)} %bitcast.201), channel_id=1, source_target_pairs={{64,0},{128,64},{192,128},{256,192},{320,256},{384,320},{448,384},... | collective-permute-start | bytes 589832 | tf_op jit(solution)/shard_map/while/body/eval_jaxpr/ppermute | solution.py:28
  436.6 3.0 copy-start.2
  448.0 7.9 %collective-permute-start.3 = (bf16[384,256]{1,0:T(8,128)(2,1)}, bf16[384,256]{1,0:T(8,128)(2,1)}, u32[]{:S(2)}, u32[]{:S(2)}) collective-permute-start(bf16[384,256]{1,0:T(8,128)(2,1)} %bitcast.201), channel_id=1, source_target_pairs={{64,0},{128,64},{192,128},{256,192},{320,256},{384,320},{448,384},... | collective-permute-start | bytes 589832 | tf_op jit(solution)/shard_map/while/body/eval_jaxpr/ppermute | solution.py:28
  464.3 8.7 %collective-permute-start.3 = (bf16[384,256]{1,0:T(8,128)(2,1)}, bf16[384,256]{1,0:T(8,128)(2,1)}, u32[]{:S(2)}, u32[]{:S(2)}) collective-permute-start(bf16[384,256]{1,0:T(8,128)(2,1)} %bitcast.201), channel_id=1, source_target_pairs={{64,0},{128,64},{192,128},{256,192},{320,256},{384,320},{448,384},... | collective-permute-start | bytes 589832 | tf_op jit(solution)/shard_map/while/body/eval_jaxpr/ppermute | solution.py:28
  469.2 3.8 copy-start.2
  473.0 203.4 %reduce-scatter.2.cloned.1.call-start = ((), (), s32[]{:S(2)}) async-start(), calls=%async_computation.2 | async-start | bytes 1769472 | tf_op jit(solution)/shard_map/reduce_scatter | solution.py:188
  (24 other events, 40.9 us)
Sparse Core Ops, SparseCore 0:
  473.1 201.5 all-reduce.1
Sparse Core Ops, SparseCore 1:
  477.2 53.6 reduce-scatter.1
where the time goes:
time: 689 us; the launch traced here: 684 us
  waiting for transfers between devices  227 us (33%)
  starting transfers between devices  149 us (22%)
  matrix products  137 us (20%)
  local copies, waits for them, and re-layouts  76.8 us (11%)
  other arithmetic  74.4 us (11%)
  between operations  15.7 us (2%)
    psum x1, waiting for transfers between devices, shards(): weight_acc = lax.psum(weight_acc, 'dom')  201 us
    ppermute x11, starting transfers between devices, padded(): after = lax.ppermute(first, axis, down)  78.2 us
    ppermute x22, starting transfers between devices, shifted(): return lax.ppermute(value, axis, pairs)  49.9 us
    dynamic_update_slice x33, other arithmetic, store_at(): return lax.dynamic_update_slice(buffer, updated[None, None], starts)  40.7 us
    ppermute x22, waiting for transfers between devices, shifted(): return lax.ppermute(value, axis, pairs)  25.1 us
    dot_general x11, matrix products, spread_backward(): jnp.einsum('tb,tih->bih', placer, products, precision=lax.Precision.HIGHEST)  23 us
    dot_general x11, matrix products, spread_forward(): jnp.einsum('tb,tih->bih', placer, products, precision=lax.Precision.HIGHEST)  22.3 us
    dot_general x11, matrix products, forward_tick(): jnp.dot(mixed, layer_weights[0], preferred_element_type=jnp.float32)  21.9 us
  transfers between devices with their start and end apart: 46, of which 13 were waited for; matrix products, arithmetic and copies ran while one was open for 14% of the time, Pallas kernels for 0%

commit v1 on v0

v1 whole, which is shorter than its diff:
```python
import functools
import math

import jax
import jax.numpy as jnp
from jax import lax
from jax.experimental import pallas as pl
from jax.experimental.pallas import tpu as pltpu
from jax.sharding import PartitionSpec as P

ALPHA = 0.1
LAMBDA_RATE = 0.5
CORES = 2
F32 = jnp.float32
BF16 = jnp.bfloat16


def vmem():
    return pl.BlockSpec(memory_space=pltpu.VMEM)


def smem():
    return pl.BlockSpec(memory_space=pltpu.SMEM)


def call(body, out_shape, in_specs, scratch, flops, moved):
    return pl.pallas_call(
        body,
        out_shape=out_shape,
        in_specs=in_specs,
        out_specs=jax.tree.map(lambda _: vmem(), out_shape),
        scratch_shapes=scratch,
        compiler_params=pltpu.CompilerParams(vmem_limit_bytes=24 * 1024 * 1024),
        cost_estimate=pl.CostEstimate(flops=flops, bytes_accessed=moved, transcendentals=0),
    )


def prepare_body(
    tiles_max, nblocks, info, own_x, got_x, own_g, got_g, own_t, got_t, dense, flipped, x0, g0, acc
):
    size = acc.shape[-1]
    core = info[2 * tiles_max + 3]
    mine = info[2 * tiles_max + 4] == 1
    acc[...] = jnp.zeros_like(acc)

    def add(slot, carry):
        row = info[slot]
        col = info[tiles_max + slot]
        col = jnp.where(col < nblocks, col, nblocks + jnp.where(col - nblocks == core, 0, 1))
        tile = jnp.where(mine, own_t[slot], got_t[slot])
        acc[row, col] += tile.astype(F32)
        return carry

    lax.fori_loop(0, info[2 * tiles_max], add, 0)
    for row in range(nblocks):
        for col in range(nblocks + 2):
            block = acc[row, col]
            dense[row * size : (row + 1) * size, col * size : (col + 1) * size] = block.astype(BF16)
            if col < nblocks:
                flipped[col * size : (col + 1) * size, row * size : (row + 1) * size] = (
                    block.T.astype(BF16)
                )
    x0[...] = jnp.where(mine, own_x[...], got_x[...])
    g0[...] = jnp.where(mine, own_g[...], got_g[...])


def weight_of(core, mine, got, layer):
    half = mine.shape[1] // 2
    own = mine[layer, half:, :]
    other = got[layer, half:, :]
    top = jnp.where(core == 0, own, other)
    bottom = jnp.where(core == 0, other, own)
    return jnp.concatenate([top, bottom], axis=0)


def forward_body(
    tiles_max, info, rates, dense, x0, mine, got, mix_out, slope_out, fresh, ext
):
    rows = x0.shape[0]
    size = fresh.shape[1]
    half = mine.shape[1] // 2
    core = info[2 * tiles_max + 3]
    send = jnp.where(core == 0, info[2 * tiles_max + 1], info[2 * tiles_max + 2])
    ext[0:rows, :] = x0[...]

    def step(layer, carry):
        rate = rates[layer]
        start = pl.multiple_of(send * size, size)
        fresh[layer] = ext[pl.ds(start, size), :]
        ext[rows : rows + half, :] = mine[layer, :half, :]
        ext[rows + half : rows + 2 * half, :] = got[layer, :half, :]
        agg = jnp.dot(dense[...], ext[...], preferred_element_type=F32)
        mix = ((1.0 - ALPHA) * agg + ALPHA * x0[...].astype(F32)).astype(BF16)
        mix_out[layer] = mix
        weight = weight_of(core, mine, got, layer)
        pre = (1.0 - rate) * mix.astype(F32) + rate * jnp.dot(
            mix, weight, preferred_element_type=F32
        )
        gate = jax.nn.sigmoid(pre)
        slope_out[layer] = gate * (1.0 + pre * (1.0 - gate))
        ext[0:rows, :] = (pre * gate).astype(BF16)
        return carry

    lax.fori_loop(0, mine.shape[0], step, 0)


def backward_body(
    tiles_max, info, rates, flipped, g0, mine, got, mix, slope, dweight, dinput, grad, acc, last
):
    depth = mine.shape[0]
    half = dweight.shape[1]
    core = info[2 * tiles_max + 3]
    grad[...] = g0[...]
    acc[...] = jnp.zeros_like(acc)

    def step(index, carry):
        layer = depth - 1 - index
        rate = rates[layer]
        delta = (grad[...].astype(F32) * slope[layer]).astype(BF16)
        start = pl.multiple_of(core * half, half)
        part = mix[layer, :, pl.ds(start, half)]
        dweight[layer] = lax.dot_general(
            part, delta, (((0,), (0,)), ((), ())), preferred_element_type=F32
        ).astype(BF16)
        weight = weight_of(core, mine, got, layer)
        dmix = (1.0 - rate) * delta.astype(F32) + rate * lax.dot_general(
            delta, weight, (((1,), (1,)), ((), ())), preferred_element_type=F32
        )
        acc[...] += ALPHA * dmix
        back = jnp.dot(flipped[...], dmix.astype(BF16), preferred_element_type=F32)
        gx = (1.0 - ALPHA) * back
        last[...] = gx
        grad[...] = gx.astype(BF16)
        return carry

    lax.fori_loop(0, depth, step, 0)
    dinput[...] = (acc[...] + last[...]).T.astype(BF16)


def swap(value):
    size = lax.axis_size("dom")
    return lax.ppermute(value, "dom", [(i, i ^ 1) for i in range(size)])


def exchange(value, axis, groups=None):
    return lax.all_to_all(value, axis, 0, 0, tiled=True, axis_index_groups=groups)


def shards(
    initial_embed,
    out_cotangent,
    layer_weights,
    stale_halo,
    tile_values,
    tile_rows,
    tile_cols,
    tile_count,
    send_blocks,
):
    section = lax.axis_index("section")
    depth = lax.axis_size("section")
    doms = lax.axis_size("dom")
    core = lax.axis_index("dom") % CORES
    spans, rows, width = initial_embed.shape
    tiles_max, size = tile_values.shape[1], tile_values.shape[-1]
    nblocks = rows // size
    half = width // 2
    chips = doms // CORES
    span = section % spans
    parity = section // spans
    rates = jnp.log(LAMBDA_RATE / (jnp.arange(depth, dtype=F32) + 1.0) + 1.0)

    halo = stale_halo[0].reshape(spans, 2, size, width)
    kept = lax.dynamic_index_in_dim(halo, core, 1, keepdims=False)
    given = lax.dynamic_index_in_dim(halo, 1 - core, 1, keepdims=False)
    taken = swap(given)
    choose = (jnp.arange(CORES) == core)[:, None, None, None]
    halo_slots = jnp.where(choose, kept[None], taken[None]).reshape(depth, size, width)
    own_weight = lax.dynamic_slice_in_dim(layer_weights[0], core * half, half, 0)
    weight_slots = jnp.broadcast_to(own_weight[None], (depth, half, width))
    mine = exchange(jnp.concatenate([halo_slots, weight_slots], axis=1), "section")
    got = swap(mine)

    def of_span(value):
        return lax.dynamic_index_in_dim(value, span, 0, keepdims=False)

    own_x, own_g, own_t = of_span(initial_embed), of_span(out_cotangent), of_span(tile_values)
    own_info = jnp.concatenate(
        [of_span(tile_rows), of_span(tile_cols), of_span(tile_count), of_span(send_blocks)]
    )
    is_mine = parity == core
    info = jnp.where(is_mine, own_info, swap(own_info))
    info = jnp.concatenate(
        [info, core.astype(jnp.int32)[None], is_mine.astype(jnp.int32)[None]]
    )
    dense, flipped, x0, g0 = call(
        functools.partial(prepare_body, tiles_max, nblocks),
        (
            jax.ShapeDtypeStruct((rows, rows + 2 * size), BF16),
            jax.ShapeDtypeStruct((rows, rows), BF16),
            jax.ShapeDtypeStruct((rows, width), BF16),
            jax.ShapeDtypeStruct((rows, width), BF16),
        ),
        [smem()] + [vmem()] * 6,
        [pltpu.VMEM((nblocks, nblocks + 2, size, size), F32)],
        10**6,
        4 * 10**6,
    )(info, own_x, swap(own_x), own_g, swap(own_g), own_t, swap(own_t))

    mix, slope, fresh_out = call(
        functools.partial(forward_body, tiles_max),
        (
            jax.ShapeDtypeStruct((depth, rows, width), BF16),
            jax.ShapeDtypeStruct((depth, rows, width), F32),
            jax.ShapeDtypeStruct((depth, size, width), BF16),
        ),
        [smem()] * 2 + [vmem()] * 4,
        [pltpu.VMEM((rows + 2 * size, width), BF16)],
        1400 * 10**6,
        10**7,
    )(info, rates, dense, x0, mine, got)

    fresh_in = exchange(fresh_out, "section").reshape(CORES, spans, size, width)
    stays = lax.dynamic_index_in_dim(fresh_in, 1 - core, 0, keepdims=False)
    leaves = lax.dynamic_index_in_dim(fresh_in, core, 0, keepdims=False)
    comes = lax.ppermute(
        leaves, "dom", [(i, (i - 1) % doms if i % 2 == 0 else (i + 1) % doms) for i in range(doms)]
    )
    lower = jnp.where(core == 0, comes, stays)
    upper = jnp.where(core == 0, stays, comes)
    fresh = jnp.concatenate([lower, upper], axis=1)[None]

    dweight, dinput = call(
        functools.partial(backward_body, tiles_max),
        (
            jax.ShapeDtypeStruct((depth, half, width), BF16),
            jax.ShapeDtypeStruct((width, rows), BF16),
        ),
        [smem()] * 2 + [vmem()] * 6,
        [
            pltpu.VMEM((rows, width), BF16),
            pltpu.VMEM((rows, width), F32),
            pltpu.VMEM((rows, width), F32),
        ],
        1400 * 10**6,
        10**7,
    )(info, rates, flipped, g0, mine, got, mix, slope)

    scale = 1.0 / math.sqrt(spans * rows * doms)
    terms = exchange(dweight, "section")
    partial = terms.astype(F32).sum(axis=0).reshape(chips, half // chips, width)
    groups = [[CORES * i + j for i in range(chips)] for j in range(CORES)]
    pieces = exchange(partial, "dom", groups)
    piece = (pieces.sum(axis=0) * scale).astype(BF16)
    spread = exchange(jnp.broadcast_to(piece[None], (doms,) + piece.shape), "dom")
    weight_grad = (
        spread.reshape(chips, CORES, half // chips, width)
        .transpose(1, 0, 2, 3)
        .reshape(1, width, width)
        .astype(F32)
    )

    arrived = exchange(dinput.reshape(depth, width // depth, rows), "section")
    arrived = arrived.reshape(CORES, spans, width // depth, rows)
    picked = lax.dynamic_index_in_dim(arrived, core, 0, keepdims=False)
    initial_grad = picked.transpose(0, 2, 1).astype(F32)
    return (weight_grad, fresh, initial_grad)


def solution(mesh):
    placed = (
        P(None, "dom", None),
        P(None, "dom", None),
        P("section", None, None),
        P("section", None, "dom", None),
        P(None, "dom", None, None),
        P(None, "dom"),
        P(None, "dom"),
        P(None, "dom"),
        P(None, "dom"),
    )
    return jax.shard_map(
        shards,
        mesh=mesh,
        in_specs=placed,
        out_specs=(
            P("section", None, None),
            P("section", None, "dom", None),
            P(None, "dom", "section"),
        ),
        check_vma=False,
    )
```

time: 689 us -> 165 us (0.24)
  waiting for transfers between devices: 227 us -> 25.4 us
  matrix products: 137 us -> 0 us
  starting transfers between devices: 149 us -> 51.5 us
  other arithmetic: 74.4 us -> 2.72 us
  local copies, waits for them, and re-layouts: 76.8 us -> 7.88 us
  blocking collectives: 0 us -> 62.7 us
  between operations: 15.7 us -> 0.96 us
  Pallas kernels: 0 us -> 13.4 us
    psum x1 -> x0, waiting for transfers between devices: 201 us -> none  [shards(): weight_acc = lax.psum(weight_acc, 'dom')]
    dot_general x99 -> x0, matrix products: 137 us -> none  [the longest x11 23 us: spread_backward(): jnp.einsum('tb,tih->bih', placer, products, precision=lax.Precision.HIGHEST)]
    ppermute x44 -> x7, starting transfers between devices: 149 us -> 28.7 us  [the longest x6 21.1 us: swap(): return lax.ppermute(value, 'dom', [(i, i ^ 1) for i in range(size)])]
    all_to_all x0 -> x3, blocking collectives: none -> 62.7 us  [exchange(): lax.all_to_all(value, axis, 0, 0, tiled=True, axis_index_groups=groups)]
    dynamic_update_slice x33 -> x0, other arithmetic: 40.7 us -> none  [store_at(): return lax.dynamic_update_slice(buffer, updated[None, None], starts)]
    dynamic_slice x66 -> x2, local copies, waits for them, and re-layouts: 36.5 us -> 0.77 us  [of_span(): return lax.dynamic_index_in_dim(value, span, 0, keepdims=False)]
    convert_element_type x55 -> x3, other arithmetic: 29.3 us -> 0.73 us  [the longest x1 0.7 us: shards(): initial_grad = picked.transpose(0, 2, 1).astype(F32)]
    ppermute x44 -> x7, waiting for transfers between devices: 25.5 us -> 1.44 us  [the longest x6 1.44 us: swap(): return lax.ppermute(value, 'dom', [(i, i ^ 1) for i in range(size)])]
  transfers between devices with their start and end apart: 46 -> 10, of which waited for: 13 -> 5; matrix products, arithmetic and copies ran while one was open for 14% -> 5% of each run, Pallas kernels for 0% -> 1%
where the time goes in v1:
time: 165 us; the launch traced here: 164 us
  blocking collectives  62.7 us (38%)
  starting transfers between devices  51.5 us (31%)
  waiting for transfers between devices  25.4 us (15%)
  Pallas kernels  13.4 us (8%)
  local copies, waits for them, and re-layouts  7.88 us (5%)
  other arithmetic  2.72 us (2%)
    all_to_all x3, blocking collectives, exchange(): lax.all_to_all(value, axis, 0, 0, tiled=True, axis_index_groups=groups)  62.7 us
    all_to_all x3, waiting for transfers between devices, exchange(): lax.all_to_all(value, axis, 0, 0, tiled=True, axis_index_groups=groups)  23.9 us
    all_to_all x3, starting transfers between devices, exchange(): lax.all_to_all(value, axis, 0, 0, tiled=True, axis_index_groups=groups)  22.8 us
    ppermute x6, starting transfers between devices, swap(): return lax.ppermute(value, 'dom', [(i, i ^ 1) for i in range(size)])  21.1 us
    ppermute x1, starting transfers between devices, shards(): lax.ppermute(leaves, 'dom', [(i, (i - 1) % doms if i % 2 == 0 else (i + 1...  7.6 us
    pallas_call x1, Pallas kernels, shards(): call(functools.partial(forward_body, tiles_max), (jax.ShapeDtypeStruct((d...  6.04 us
    pallas_call x1, Pallas kernels, shards(): call(functools.partial(backward_body, tiles_max), (jax.ShapeDtypeStruct((...  5.84 us
  transfers between devices with their start and end apart: 10, of which 5 were waited for; matrix products, arithmetic and copies ran while one was open for 5% of the time, Pallas kernels for 1%

profile of v1, /device:TPU:1, one launch (start us, length us, event | category | flops | bytes accessed | tf_op | source)
XLA Modules:
  0.0 164.5 jit_solution(14921042057834103056)
XLA Ops:
  0.6 0.0 copy-start
  0.7 1.2 dynamic-slice_bitcast_fusion.3
  1.9 8.8 %collective-permute-start.4 = (bf16[4,128,256]{2,1,0:T(8,128)(2,1)S(1)}, bf16[4,128,256]{2,1,0:T(8,128)(2,1)S(1)}, u32[]{:S(2)}, u32[]{:S(2)}) collective-permute-start(bf16[4,128,256]{2,1,0:T(8,128)(2,1)S(1)} %get-tuple-element.24), channel_id=1, source_target_pairs={{0,1},{1,0},{2,3},{3,2},{4,5},{5,4},{6,7},{7,6},{8,9},{9,8},{10,11... | collective-permute-start | bytes 786440 | tf_op jit(solution)/shard_map/ppermute | solution.py:142
  10.7 0.1 broadcast_in_dim.66
  10.7 0.1 broadcast_in_dim.67
  10.8 0.8 dynamic-slice_bitcast_fusion.6
  11.7 0.1 collective-permute-done.4
  11.8 0.1 bitcast_select_fusion
  12.0 0.0 copy-start.2
  12.0 0.0 copy-start.1
  12.0 0.1 pad_maximum_fusion
  12.1 32.4 %all_to_all.30.mine = bf16[8,256,256]{2,1,0:T(8,128)(2,1)S(1)} all-to-all(bf16[8,256,256]{2,1,0:T(8,128)(2,1)S(1)} %pad_maximum_fusion), channel_id=1, replica_groups=mesh['section'=8,'dom'=64] {'section'}, dimensions={0} | all-to-all | bytes 2097152 | tf_op jit(solution)/shard_map/all_to_all | solution.py:146
  44.5 3.6 %collective-permute-start.5 = (bf16[8,256,256]{2,1,0:T(8,128)(2,1)S(1)}, bf16[8,256,256]{2,1,0:T(8,128)(2,1)}, u32[]{:S(2)}, u32[]{:S(2)}) collective-permute-start(bf16[8,256,256]{2,1,0:T(8,128)(2,1)S(1)} %all_to_all.30.mine), channel_id=1, source_target_pairs={{0,1},{1,0},{2,3},{3,2},{4,5},{5,4},{6,7},{7,6},{8,9},{9,8},{10,11... | collective-permute-start | bytes 3145736 | tf_op jit(solution)/shard_map/ppermute | solution.py:142
  48.1 0.6 constant_dynamic-slice_fusion.1
  48.7 0.2 fusion
  48.9 0.7 fusion.1
  49.6 0.7 pad_add_fusion
  50.3 1.9 %collective-permute-start = (s32[27]{0:T(128)S(1)}, s32[27]{0:T(128)S(1)}, u32[]{:S(2)}, u32[]{:S(2)}) collective-permute-start(s32[27]{0:T(128)S(1)} %pad_add_fusion), channel_id=1, source_target_pairs={{0,1},{1,0},{2,3},{3,2},{4,5},{5,4},{6,7},{7,6},{8,9},{9,8},{10,11... | collective-permute-start | bytes 332 | tf_op jit(solution)/shard_map/ppermute | solution.py:142
  52.3 0.9 dynamic-slice_bitcast_fusion.4.own_g
  53.2 2.4 %collective-permute-start.2 = (bf16[384,256]{1,0:T(8,128)(2,1)S(1)}, bf16[384,256]{1,0:T(8,128)(2,1)}, u32[]{:S(2)}, u32[]{:S(2)}) collective-permute-start(bf16[384,256]{1,0:T(8,128)(2,1)S(1)} %dynamic-slice_bitcast_fusion.4.own_g), channel_id=1, source_target_pairs={{0,1},{1,0},{2,3},{3,2},{4,5},{5,4},{6,7},{7,6},{8,9},{9,8},{10,11... | collective-permute-start | bytes 589832 | tf_op jit(solution)/shard_map/ppermute | solution.py:142
  55.6 0.9 dynamic-slice_bitcast_fusion.5.own_x
  56.6 1.9 %collective-permute-start.1 = (bf16[384,256]{1,0:T(8,128)(2,1)S(1)}, bf16[384,256]{1,0:T(8,128)(2,1)}, u32[]{:S(2)}, u32[]{:S(2)}) collective-permute-start(bf16[384,256]{1,0:T(8,128)(2,1)S(1)} %dynamic-slice_bitcast_fusion.5.own_x), channel_id=1, source_target_pairs={{0,1},{1,0},{2,3},{3,2},{4,5},{5,4},{6,7},{7,6},{8,9},{9,8},{10,11... | collective-permute-start | bytes 589832 | tf_op jit(solution)/shard_map/ppermute | solution.py:142
  58.6 2.4 %collective-permute-start.3 = (bf16[12,128,128]{2,1,0:T(8,128)(2,1)S(1)}, bf16[12,128,128]{2,1,0:T(8,128)(2,1)}, u32[]{:S(2)}, u32[]{:S(2)}) collective-permute-start(bf16[12,128,128]{2,1,0:T(8,128)(2,1)S(1)} %dynamic-slice_bitcast_fusion.own_t), channel_id=1, source_target_pairs={{0,1},{1,0},{2,3},{3,2},{4,5},{5,4},{6,7},{7,6},{8,9},{9,8},{10,11... | collective-permute-start | bytes 1179656 | tf_op jit(solution)/shard_map/ppermute | solution.py:142
  61.0 0.0 collective-permute-done
  61.0 0.1 pad_add_fusion.1.info
  61.1 0.0 collective-permute-done.2.got_g
  61.1 0.0 collective-permute-done.1.got_x
  61.1 1.3 collective-permute-done.3.got_t
  62.4 1.5 shard_map.112
  63.9 0.0 collective-permute-done.5.got
  64.0 6.0 %shard_map.113 = (bf16[8,384,256]{2,1,0:T(8,128)(2,1)S(1)}, f32[8,384,256]{2,1,0:T(8,128)S(1)}, bf16[8,128,256]{2,1,0:T(8,128)(2,1)}) custom-call(s32[29]{0:T(128)S(1)} %pad_add_fusion.1.info, f32[8]{0:T(128)S(1)} %add_log_fusion.rates, bf16[384,640]{1,0:T(8,128)(2,1)S(1)} %get-tuple-element.14.dense, bf16[384,256]{1,0:T(8,128)(2,1)S(1)} %get-tuple-element.15.x0, ...), custom_call_target="tpu_custom_call" | custom-call | flops 1400000000 | bytes 10000000 | tf_op jit(solution)/shard_map/pallas_call | solution.py:210
  70.0 5.8 %shard_map.114 = (bf16[8,128,256]{2,1,0:T(8,128)(2,1)S(1)}, bf16[256,384]{1,0:T(8,128)(2,1)S(1)}) custom-call(s32[29]{0:T(128)S(1)} %pad_add_fusion.1.info, f32[8]{0:T(128)S(1)} %add_log_fusion.rates, bf16[384,384]{1,0:T(8,128)(2,1)S(1)} %get-tuple-element.12.flipped, bf16[384,256]{1,0:T(8,128)(2,1)S(1)} %get-tuple-element.13.g0, ...), custom_call_target="tpu_custom_call" | custom-call | flops 1400000000 | bytes 10000000 | tf_op jit(solution)/shard_map/pallas_call | solution.py:233
  75.8 12.4 %all_to_all.31 = bf16[8,32,384]{2,1,0:T(8,128)(2,1)S(1)} all-to-all(bf16[8,32,384]{2,1,0:T(8,128)(2,1)S(1)} %bitcast.43), channel_id=1, replica_groups=mesh['section'=8,'dom'=64] {'section'}, dimensions={0} | all-to-all | bytes 393216 | tf_op jit(solution)/shard_map/all_to_all | solution.py:146
  88.3 17.8 %all_to_all.32 = bf16[8,128,256]{2,1,0:T(8,128)(2,1)S(1)} all-to-all(bf16[8,128,256]{2,1,0:T(8,128)(2,1)S(1)} %get-tuple-element.18), channel_id=1, replica_groups=mesh['section'=8,'dom'=64] {'section'}, dimensions={0} | all-to-all | bytes 1048576 | tf_op jit(solution)/shard_map/all_to_all | solution.py:146
  106.1 3.5 %all-to-all-start.4 = ((bf16[8,128,256]{2,1,0:T(8,128)(2,1)}), bf16[8,128,256]{2,1,0:T(8,128)(2,1)S(1)}, u32[]{:S(2)}, u32[]{:S(2)}) async-start(bf16[8,128,256]{2,1,0:T(8,128)(2,1)} %get-tuple-element.19), calls=%async_computation.4 | async-start | bytes 1048576 | tf_op jit(solution)/shard_map/all_to_all | solution.py:146
  109.6 0.1 convert_reduce_fusion
  109.7 0.7 reshape.55
  110.4 13.6 %all-to-all-done.4 = bf16[8,128,256]{2,1,0:T(8,128)(2,1)S(1)} async-done(((bf16[8,128,256]{2,1,0:T(8,128)(2,1)}), bf16[8,128,256]{2,1,0:T(8,128)(2,1)S(1)}, u32[]{:S(2)}, u32[]{:S(2)}) %all-to-all-start.4) | async-done | bytes 524320 | tf_op jit(solution)/shard_map/all_to_all | solution.py:146
  123.9 9.7 %all-to-all-start.2 = ((f32[32,4,256]{2,1,0:T(4,128)}), f32[32,4,256]{2,1,0:T(4,128)S(1)}, u32[]{:S(2)}, u32[]{:S(2)}) async-start(f32[32,4,256]{2,1,0:T(4,128)} %reshape.55), calls=%async_computation.2 | async-start | bytes 262144 | tf_op jit(solution)/shard_map/all_to_all | solution.py:146
  133.7 7.6 %collective-permute-start.6 = (bf16[4,128,256]{2,1,0:T(8,128)(2,1)S(1)}, bf16[4,128,256]{2,1,0:T(8,128)(2,1)S(1)}, u32[]{:S(2)}, u32[]{:S(2)}) collective-permute-start(bf16[4,128,256]{2,1,0:T(8,128)(2,1)S(1)} %dynamic-slice_bitcast_fusion.1), channel_id=1, source_target_pairs={{0,63},{1,2},{2,1},{3,4},{4,3},{5,6},{6,5},{7,8},{8,7},{9,10},{10,... | collective-permute-start | bytes 786440 | tf_op jit(solution)/shard_map/ppermute | solution.py:226
  141.3 0.7 convert_bitcast_fusion.1
  142.0 0.8 all-to-all-done.2
  142.9 0.7 broadcast_in_dim.76
  143.6 9.5 %all-to-all-start.3 = ((bf16[64,4,256]{2,1,0:T(4,128)(2,1)}), bf16[64,4,256]{2,1,0:T(4,128)(2,1)S(1)}, u32[]{:S(2)}, u32[]{:S(2)}) async-start(bf16[64,4,256]{2,1,0:T(4,128)(2,1)} %broadcast_in_dim.76), calls=%async_computation.3 | async-start | bytes 262144 | tf_op jit(solution)/shard_map/all_to_all | solution.py:146
  153.1 0.0 collective-permute-done.6
  153.2 0.8 maximum_bitcast_fusion
  154.0 9.6 %all-to-all-done.3 = bf16[64,4,256]{2,1,0:T(4,128)(2,1)S(1)} async-done(((bf16[64,4,256]{2,1,0:T(4,128)(2,1)}), bf16[64,4,256]{2,1,0:T(4,128)(2,1)S(1)}, u32[]{:S(2)}, u32[]{:S(2)}) %all-to-all-start.3) | async-done | bytes 131104 | tf_op jit(solution)/shard_map/all_to_all | solution.py:146
  163.7 0.8 reshape.60
  (14 shorter events, 0.3 us)
Async XLA Ops:
  0.6 57.9 %copy-start = (bf16[4,12,128,128]{3,2,1,0:T(8,128)(2,1)S(1)}, bf16[4,12,128,128]{3,2,1,0:T(8,128)(2,1)}, u32[]{:S(2)}) copy-start(bf16[4,12,128,128]{3,2,1,0:T(8,128)(2,1)} %param.13) | copy-start | bytes 4718596
  1.9 9.9 %collective-permute-start.4 = (bf16[4,128,256]{2,1,0:T(8,128)(2,1)S(1)}, bf16[4,128,256]{2,1,0:T(8,128)(2,1)S(1)}, u32[]{:S(2)}, u32[]{:S(2)}) collective-permute-start(bf16[4,128,256]{2,1,0:T(8,128)(2,1)S(1)} %get-tuple-element.24), channel_id=1, source_target_pairs={{0,1},{1,0},{2,3},{3,2},{4,5},{5,4},{6,7},{7,6},{8,9},{9,8},{10,11... | collective-permute-start | bytes 786440 | tf_op jit(solution)/shard_map/ppermute | solution.py:142
  12.0 36.2 %copy-start.2 = (s32[4,1]{0,1:T(1,128)S(1)}, s32[4,1]{0,1:T(1,128)}, u32[]{:S(2)}) copy-start(s32[4,1]{0,1:T(1,128)} %param.16) | copy-start | bytes 52
  12.0 36.8 %copy-start.1 = (s32[4,2]{0,1:T(2,128)S(1)}, s32[4,2]{0,1:T(2,128)}, u32[]{:S(2)}) copy-start(s32[4,2]{0,1:T(2,128)} %param.17) | copy-start | bytes 100
  44.5 19.5 %collective-permute-start.5 = (bf16[8,256,256]{2,1,0:T(8,128)(2,1)S(1)}, bf16[8,256,256]{2,1,0:T(8,128)(2,1)}, u32[]{:S(2)}, u32[]{:S(2)}) collective-permute-start(bf16[8,256,256]{2,1,0:T(8,128)(2,1)S(1)} %all_to_all.30.mine), channel_id=1, source_target_pairs={{0,1},{1,0},{2,3},{3,2},{4,5},{5,4},{6,7},{7,6},{8,9},{9,8},{10,11... | collective-permute-start | bytes 3145736 | tf_op jit(solution)/shard_map/ppermute | solution.py:142
  50.3 10.7 %collective-permute-start = (s32[27]{0:T(128)S(1)}, s32[27]{0:T(128)S(1)}, u32[]{:S(2)}, u32[]{:S(2)}) collective-permute-start(s32[27]{0:T(128)S(1)} %pad_add_fusion), channel_id=1, source_target_pairs={{0,1},{1,0},{2,3},{3,2},{4,5},{5,4},{6,7},{7,6},{8,9},{9,8},{10,11... | collective-permute-start | bytes 332 | tf_op jit(solution)/shard_map/ppermute | solution.py:142
  53.2 7.9 %collective-permute-start.2 = (bf16[384,256]{1,0:T(8,128)(2,1)S(1)}, bf16[384,256]{1,0:T(8,128)(2,1)}, u32[]{:S(2)}, u32[]{:S(2)}) collective-permute-start(bf16[384,256]{1,0:T(8,128)(2,1)S(1)} %dynamic-slice_bitcast_fusion.4.own_g), channel_id=1, source_target_pairs={{0,1},{1,0},{2,3},{3,2},{4,5},{5,4},{6,7},{7,6},{8,9},{9,8},{10,11... | collective-permute-start | bytes 589832 | tf_op jit(solution)/shard_map/ppermute | solution.py:142
  56.6 4.5 %collective-permute-start.1 = (bf16[384,256]{1,0:T(8,128)(2,1)S(1)}, bf16[384,256]{1,0:T(8,128)(2,1)}, u32[]{:S(2)}, u32[]{:S(2)}) collective-permute-start(bf16[384,256]{1,0:T(8,128)(2,1)S(1)} %dynamic-slice_bitcast_fusion.5.own_x), channel_id=1, source_target_pairs={{0,1},{1,0},{2,3},{3,2},{4,5},{5,4},{6,7},{7,6},{8,9},{9,8},{10,11... | collective-permute-start | bytes 589832 | tf_op jit(solution)/shard_map/ppermute | solution.py:142
  58.6 3.9 %collective-permute-start.3 = (bf16[12,128,128]{2,1,0:T(8,128)(2,1)S(1)}, bf16[12,128,128]{2,1,0:T(8,128)(2,1)}, u32[]{:S(2)}, u32[]{:S(2)}) collective-permute-start(bf16[12,128,128]{2,1,0:T(8,128)(2,1)S(1)} %dynamic-slice_bitcast_fusion.own_t), channel_id=1, source_target_pairs={{0,1},{1,0},{2,3},{3,2},{4,5},{5,4},{6,7},{7,6},{8,9},{9,8},{10,11... | collective-permute-start | bytes 1179656 | tf_op jit(solution)/shard_map/ppermute | solution.py:142
  106.1 17.8 %all-to-all-start.4 = ((bf16[8,128,256]{2,1,0:T(8,128)(2,1)}), bf16[8,128,256]{2,1,0:T(8,128)(2,1)S(1)}, u32[]{:S(2)}, u32[]{:S(2)}) async-start(bf16[8,128,256]{2,1,0:T(8,128)(2,1)} %get-tuple-element.19), calls=%async_computation.4 | async-start | bytes 1048576 | tf_op jit(solution)/shard_map/all_to_all | solution.py:146
  123.9 18.9 %all-to-all-start.2 = ((f32[32,4,256]{2,1,0:T(4,128)}), f32[32,4,256]{2,1,0:T(4,128)S(1)}, u32[]{:S(2)}, u32[]{:S(2)}) async-start(f32[32,4,256]{2,1,0:T(4,128)} %reshape.55), calls=%async_computation.2 | async-start | bytes 262144 | tf_op jit(solution)/shard_map/all_to_all | solution.py:146
  133.7 19.4 %collective-permute-start.6 = (bf16[4,128,256]{2,1,0:T(8,128)(2,1)S(1)}, bf16[4,128,256]{2,1,0:T(8,128)(2,1)S(1)}, u32[]{:S(2)}, u32[]{:S(2)}) collective-permute-start(bf16[4,128,256]{2,1,0:T(8,128)(2,1)S(1)} %dynamic-slice_bitcast_fusion.1), channel_id=1, source_target_pairs={{0,63},{1,2},{2,1},{3,4},{4,3},{5,6},{6,5},{7,8},{8,7},{9,10},{10,... | collective-permute-start | bytes 786440 | tf_op jit(solution)/shard_map/ppermute | solution.py:226
  143.6 20.0 %all-to-all-start.3 = ((bf16[64,4,256]{2,1,0:T(4,128)(2,1)}), bf16[64,4,256]{2,1,0:T(4,128)(2,1)S(1)}, u32[]{:S(2)}, u32[]{:S(2)}) async-start(bf16[64,4,256]{2,1,0:T(4,128)(2,1)} %broadcast_in_dim.76), calls=%async_computation.3 | async-start | bytes 262144 | tf_op jit(solution)/shard_map/all_to_all | solution.py:146

commit v2 on v1

--- a/solution.py
+++ b/solution.py
@@ -40,7 +40,7 @@
 ):
     size = acc.shape[-1]
     core = info[2 * tiles_max + 3]
-    mine = info[2 * tiles_max + 4] == 1
+    mine = info[2 * tiles_max + 4] == core
     acc[...] = jnp.zeros_like(acc)
 
     def add(slot, carry):
@@ -64,10 +64,9 @@
     g0[...] = jnp.where(mine, own_g[...], got_g[...])
 
 
-def weight_of(core, mine, got, layer):
-    half = mine.shape[1] // 2
-    own = mine[layer, half:, :]
-    other = got[layer, half:, :]
+def weight_of(core, parity, mine, got, layer):
+    own = mine[CORES * layer + 1 - parity]
+    other = got[CORES * layer + 1 - parity]
     top = jnp.where(core == 0, own, other)
     bottom = jnp.where(core == 0, other, own)
     return jnp.concatenate([top, bottom], axis=0)
@@ -78,8 +77,9 @@
 ):
     rows = x0.shape[0]
     size = fresh.shape[1]
-    half = mine.shape[1] // 2
+    half = mine.shape[1]
     core = info[2 * tiles_max + 3]
+    parity = info[2 * tiles_max + 4]
     send = jnp.where(core == 0, info[2 * tiles_max + 1], info[2 * tiles_max + 2])
     ext[0:rows, :] = x0[...]
 
@@ -87,12 +87,12 @@
         rate = rates[layer]
         start = pl.multiple_of(send * size, size)
         fresh[layer] = ext[pl.ds(start, size), :]
-        ext[rows : rows + half, :] = mine[layer, :half, :]
-        ext[rows + half : rows + 2 * half, :] = got[layer, :half, :]
+        ext[rows : rows + half, :] = mine[CORES * layer + parity]
+        ext[rows + half : rows + 2 * half, :] = got[CORES * layer + parity]
         agg = jnp.dot(dense[...], ext[...], preferred_element_type=F32)
         mix = ((1.0 - ALPHA) * agg + ALPHA * x0[...].astype(F32)).astype(BF16)
         mix_out[layer] = mix
-        weight = weight_of(core, mine, got, layer)
+        weight = weight_of(core, parity, mine, got, layer)
         pre = (1.0 - rate) * mix.astype(F32) + rate * jnp.dot(
             mix, weight, preferred_element_type=F32
         )
@@ -101,15 +101,19 @@
         ext[0:rows, :] = (pre * gate).astype(BF16)
         return carry
 
-    lax.fori_loop(0, mine.shape[0], step, 0)
+    lax.fori_loop(0, fresh.shape[0], step, 0)
 
 
 def backward_body(
-    tiles_max, info, rates, flipped, g0, mine, got, mix, slope, dweight, dinput, grad, acc, last
+    tiles_max, info, rates, flipped, g0, mine, got, mix, slope, fresh, terms, parcel, grad, acc, last,
+    dweight, sorted_rows
 ):
-    depth = mine.shape[0]
+    depth, size, width = fresh.shape
     half = dweight.shape[1]
+    chips = terms.shape[0]
+    few = half // chips
     core = info[2 * tiles_max + 3]
+    parity = info[2 * tiles_max + 4]
     grad[...] = g0[...]
     acc[...] = jnp.zeros_like(acc)
 
@@ -121,8 +125,8 @@
         part = mix[layer, :, pl.ds(start, half)]
         dweight[layer] = lax.dot_general(
             part, delta, (((0,), (0,)), ((), ())), preferred_element_type=F32
-        ).astype(BF16)
-        weight = weight_of(core, mine, got, layer)
+        )
+        weight = weight_of(core, parity, mine, got, layer)
         dmix = (1.0 - rate) * delta.astype(F32) + rate * lax.dot_general(
             delta, weight, (((1,), (1,)), ((), ())), preferred_element_type=F32
         )
@@ -134,7 +138,72 @@
         return carry
 
     lax.fori_loop(0, depth, step, 0)
-    dinput[...] = (acc[...] + last[...]).T.astype(BF16)
+    for chip in range(chips):
+        for layer in range(depth):
+            sorted_rows[chip, layer * few : (layer + 1) * few, :] = dweight[
+                layer, chip * few : (chip + 1) * few, :
+            ]
+    terms[...] = sorted_rows[...].astype(BF16)
+    dinput = (acc[...] + last[...]).T.astype(BF16)
+    share = width // depth
+    hop = share // 2
+    for part in range(depth):
+        piece = dinput[part * share : (part + 1) * share]
+        parcel[part, :size, :] = fresh[part]
+        parcel[part, size : size + share, :] = piece[:, :width]
+        parcel[part, size + share : size + share + hop, : width // 2] = piece[:hop, width:]
+        parcel[part, size + share : size + share + hop, width // 2 :] = piece[hop:, width:]
+        rest = parcel.shape[1] - (size + share + hop)
+        parcel[part, size + share + hop :, :] = jnp.zeros((rest, width), BF16)
+
+
+def merge_body(tail, pieces, parcel_in, parcel):
+    depth, deep, _ = parcel.shape
+    few = pieces.shape[1] // depth
+    total = pieces[0].astype(F32)
+    for chip in range(1, pieces.shape[0]):
+        total += pieces[chip].astype(F32)
+    parcel[...] = parcel_in[...]
+    for layer in range(depth):
+        part = total[layer * few : (layer + 1) * few]
+        if few < tail:
+            pad = jnp.zeros((tail - few, part.shape[1]), F32)
+            part = jnp.concatenate([part, pad], axis=0)
+        parcel[layer, deep - tail :, :] = part.astype(BF16)
+
+
+def unpack_body(size, core_ref, arrived, out, stays, leaves):
+    spans, share, _ = out.shape
+    width = arrived.shape[-1]
+    hop = share // 2
+    base = core_ref[0] * spans
+    away = (1 - core_ref[0]) * spans
+    for span in range(spans):
+        leaves[span] = arrived[base + span, :size, :]
+        stays[span] = arrived[away + span, :size, :]
+        top = arrived[base + span, size : size + share, :].astype(F32)
+        low = arrived[base + span, size + share : size + share + hop, :].astype(F32)
+        tail = jnp.concatenate([low[:, : width // 2], low[:, width // 2 :]], axis=0)
+        out[span, :, :width] = top
+        out[span, :, width:] = tail
+
+
+def fresh_body(core_ref, stays, comes, out):
+    size = stays.shape[1]
+    first = core_ref[0] == 0
+    for span in range(stays.shape[0]):
+        own, other = stays[span], comes[span]
+        out[0, span, :size, :] = jnp.where(first, other, own)
+        out[0, span, size:, :] = jnp.where(first, own, other)
+
+
+def assemble_body(spread, out):
+    doms, few, _ = spread.shape
+    chips = doms // CORES
+    for core in range(CORES):
+        for chip in range(chips):
+            row = (core * chips + chip) * few
+            out[0, row : row + few, :] = spread[CORES * chip + core]
 
 
 def swap(value):
@@ -170,16 +239,14 @@
     parity = section // spans
     rates = jnp.log(LAMBDA_RATE / (jnp.arange(depth, dtype=F32) + 1.0) + 1.0)
 
-    halo = stale_halo[0].reshape(spans, 2, size, width)
-    kept = lax.dynamic_index_in_dim(halo, core, 1, keepdims=False)
-    given = lax.dynamic_index_in_dim(halo, 1 - core, 1, keepdims=False)
-    taken = swap(given)
-    choose = (jnp.arange(CORES) == core)[:, None, None, None]
-    halo_slots = jnp.where(choose, kept[None], taken[None]).reshape(depth, size, width)
-    own_weight = lax.dynamic_slice_in_dim(layer_weights[0], core * half, half, 0)
-    weight_slots = jnp.broadcast_to(own_weight[None], (depth, half, width))
-    mine = exchange(jnp.concatenate([halo_slots, weight_slots], axis=1), "section")
-    got = swap(mine)
+    halo = stale_halo[0].reshape(1, spans, CORES, size, width)
+    weight = layer_weights[0].reshape(1, 1, CORES, half, width)
+    choose = (jnp.arange(CORES) == core)[:, None, None, None, None]
+    slots = jnp.where(choose, halo, weight).reshape(depth * CORES, size, width)
+    column = [
+        [z * doms + CORES * i + j for z in range(depth) for j in range(CORES)] for i in range(chips)
+    ]
+    mine = exchange(slots, ("section", "dom"), column)
 
     def of_span(value):
         return lax.dynamic_index_in_dim(value, span, 0, keepdims=False)
@@ -191,7 +258,7 @@
     is_mine = parity == core
     info = jnp.where(is_mine, own_info, swap(own_info))
     info = jnp.concatenate(
-        [info, core.astype(jnp.int32)[None], is_mine.astype(jnp.int32)[None]]
+        [info, core.astype(jnp.int32)[None], parity.astype(jnp.int32)[None]]
     )
     dense, flipped, x0, g0 = call(
         functools.partial(prepare_body, tiles_max, nblocks),
@@ -207,6 +274,9 @@
         4 * 10**6,
     )(info, own_x, swap(own_x), own_g, swap(own_g), own_t, swap(own_t))
 
+    mine, dense = lax.optimization_barrier((mine, dense))
+    got = swap(mine)
+
     mix, slope, fresh_out = call(
         functools.partial(forward_body, tiles_max),
         (
@@ -220,51 +290,77 @@
         10**7,
     )(info, rates, dense, x0, mine, got)
 
-    fresh_in = exchange(fresh_out, "section").reshape(CORES, spans, size, width)
-    stays = lax.dynamic_index_in_dim(fresh_in, 1 - core, 0, keepdims=False)
-    leaves = lax.dynamic_index_in_dim(fresh_in, core, 0, keepdims=False)
-    comes = lax.ppermute(
-        leaves, "dom", [(i, (i - 1) % doms if i % 2 == 0 else (i + 1) % doms) for i in range(doms)]
-    )
-    lower = jnp.where(core == 0, comes, stays)
-    upper = jnp.where(core == 0, stays, comes)
-    fresh = jnp.concatenate([lower, upper], axis=1)[None]
-
-    dweight, dinput = call(
+    few = half // chips
+    tail = max(16, few)
+    deep = size + width // depth + width // depth // 2 + tail
+    terms, parcel = call(
         functools.partial(backward_body, tiles_max),
         (
-            jax.ShapeDtypeStruct((depth, half, width), BF16),
-            jax.ShapeDtypeStruct((width, rows), BF16),
-        ),
-        [smem()] * 2 + [vmem()] * 6,
+            jax.ShapeDtypeStruct((chips, depth * few, width), BF16),
+            jax.ShapeDtypeStruct((depth, deep, width), BF16),
+        ),
+        [smem()] * 2 + [vmem()] * 7,
         [
             pltpu.VMEM((rows, width), BF16),
             pltpu.VMEM((rows, width), F32),
             pltpu.VMEM((rows, width), F32),
+            pltpu.VMEM((depth, half, width), F32),
+            pltpu.VMEM((chips, depth * few, width), F32),
         ],
         1400 * 10**6,
         10**7,
-    )(info, rates, flipped, g0, mine, got, mix, slope)
-
+    )(info, rates, flipped, g0, mine, got, mix, slope, fresh_out)
+
+    groups = [[CORES * i + j for i in range(chips)] for j in range(CORES)]
+    pieces = exchange(terms, "dom", groups)
+    parcel = call(
+        functools.partial(merge_body, tail),
+        jax.ShapeDtypeStruct((depth, deep, width), BF16),
+        [vmem()] * 2,
+        [],
+        10**6,
+        10**6,
+    )(pieces, parcel)
+
+    arrived = exchange(parcel, "section")
     scale = 1.0 / math.sqrt(spans * rows * doms)
-    terms = exchange(dweight, "section")
-    partial = terms.astype(F32).sum(axis=0).reshape(chips, half // chips, width)
-    groups = [[CORES * i + j for i in range(chips)] for j in range(CORES)]
-    pieces = exchange(partial, "dom", groups)
-    piece = (pieces.sum(axis=0) * scale).astype(BF16)
-    spread = exchange(jnp.broadcast_to(piece[None], (doms,) + piece.shape), "dom")
-    weight_grad = (
-        spread.reshape(chips, CORES, half // chips, width)
-        .transpose(1, 0, 2, 3)
-        .reshape(1, width, width)
-        .astype(F32)
-    )
-
-    arrived = exchange(dinput.reshape(depth, width // depth, rows), "section")
-    arrived = arrived.reshape(CORES, spans, width // depth, rows)
-    picked = lax.dynamic_index_in_dim(arrived, core, 0, keepdims=False)
-    initial_grad = picked.transpose(0, 2, 1).astype(F32)
-    return (weight_grad, fresh, initial_grad)
+    piece = arrived[:, deep - tail : deep - tail + few, :].astype(F32).sum(axis=0) * scale
+    copies = jnp.broadcast_to(piece[None], (doms,) + piece.shape)
+    copies, arrived = lax.optimization_barrier((copies, arrived))
+    spread = exchange(copies, "dom")
+    weight_grad = call(
+        assemble_body,
+        jax.ShapeDtypeStruct((1, width, width), F32),
+        [vmem()],
+        [],
+        10**5,
+        10**6,
+    )(spread)
+
+    initial_grad, stays, leaves = call(
+        functools.partial(unpack_body, size),
+        (
+            jax.ShapeDtypeStruct((spans, width // depth, rows), F32),
+            jax.ShapeDtypeStruct((spans, size, width), BF16),
+            jax.ShapeDtypeStruct((spans, size, width), BF16),
+        ),
+        [smem(), vmem()],
+        [],
+        100,
+        100,
+    )(core.astype(jnp.int32)[None], arrived)
+    comes = lax.ppermute(
+        leaves, "dom", [(i, (i - 1) % doms if i % 2 == 0 else (i + 1) % doms) for i in range(doms)]
+    )
+    fresh = call(
+        fresh_body,
+        jax.ShapeDtypeStruct((1, spans, 2 * size, width), BF16),
+        [smem(), vmem(), vmem()],
+        [],
+        100,
+        100,
+    )(core.astype(jnp.int32)[None], stays, comes)
+    return (weight_grad, fresh, initial_grad.transpose(0, 2, 1))
 
 
 def solution(mesh):

time: 165 us -> 133 us (0.81)
  blocking collectives: 62.7 us -> 45.4 us
  starting transfers between devices: 51.5 us -> 39.4 us
  waiting for transfers between devices: 25.4 us -> 20.4 us
    all_to_all x3 -> x2, blocking collectives: 62.7 us -> 45.4 us  [exchange(): lax.all_to_all(value, axis, 0, 0, tiled=True, axis_index_groups=groups)]
    all_to_all x3 -> x2, waiting for transfers between devices: 23.9 us -> 10.1 us  [exchange(): lax.all_to_all(value, axis, 0, 0, tiled=True, axis_index_groups=groups)]
    ppermute x6 -> x5, starting transfers between devices: 21.1 us -> 10.6 us  [swap(): return lax.ppermute(value, 'dom', [(i, i ^ 1) for i in range(size)])]
    ppermute x1, waiting for transfers between devices: 0.01 us -> 6.63 us  [shards(): lax.ppermute(leaves, 'dom', [(i, (i - 1) % doms if i % 2 == 0 else (i + 1...]
    unnamed x6 -> x22, local copies, waits for them, and re-layouts: 0.02 us -> 4.82 us
    ppermute x1, starting transfers between devices: 7.6 us -> 3.53 us  [shards(): lax.ppermute(leaves, 'dom', [(i, (i - 1) % doms if i % 2 == 0 else (i + 1...]
    all_to_all x3 -> x2, starting transfers between devices: 22.8 us -> 25.4 us  [exchange(): lax.all_to_all(value, axis, 0, 0, tiled=True, axis_index_groups=groups)]
    pallas_call x0 -> x4, Pallas kernels: none -> 2.43 us  [the longest x1 0.83 us: shards(): call(fresh_body, jax.ShapeDtypeStruct((1, spans, 2 * size, width), BF16),...]
  transfers between devices with their start and end apart: 10 -> 8, of which waited for: 5 -> 5; matrix products, arithmetic and copies ran while one was open for 5% -> 3% of each run, Pallas kernels for 1% -> 2%
where the time goes in v2:
time: 133 us; the launch traced here: 132 us
  blocking collectives  45.4 us (34%)
  starting transfers between devices  39.4 us (30%)
  waiting for transfers between devices  20.4 us (15%)
  Pallas kernels  13.9 us (10%)
  local copies, waits for them, and re-layouts  9.13 us (7%)
  other arithmetic  3.19 us (2%)
    all_to_all x2, blocking collectives, exchange(): lax.all_to_all(value, axis, 0, 0, tiled=True, axis_index_groups=groups)  45.4 us
    all_to_all x2, starting transfers between devices, exchange(): lax.all_to_all(value, axis, 0, 0, tiled=True, axis_index_groups=groups)  25.4 us
    ppermute x5, starting transfers between devices, swap(): return lax.ppermute(value, 'dom', [(i, i ^ 1) for i in range(size)])  10.6 us
    all_to_all x2, waiting for transfers between devices, exchange(): lax.all_to_all(value, axis, 0, 0, tiled=True, axis_index_groups=groups)  10.1 us
    ppermute x1, waiting for transfers between devices, shards(): lax.ppermute(leaves, 'dom', [(i, (i - 1) % doms if i % 2 == 0 else (i + 1...  6.63 us
    pallas_call x1, Pallas kernels, shards(): call(functools.partial(backward_body, tiles_max), (jax.ShapeDtypeStruct((...  5.28 us
    unnamed x22, local copies, waits for them, and re-layouts  4.82 us
    pallas_call x1, Pallas kernels, shards(): call(functools.partial(forward_body, tiles_max), (jax.ShapeDtypeStruct((d...  4.66 us
  transfers between devices with their start and end apart: 8, of which 5 were waited for; matrix products, arithmetic and copies ran while one was open for 3% of the time, Pallas kernels for 2%

profile of v2, /device:TPU:1, one launch (start us, length us, event | category | flops | bytes accessed | tf_op | source)
XLA Modules:
  0.0 132.3 jit_solution(1583197110854600777)
XLA Ops:
  0.6 0.0 copy-start
  0.7 0.1 broadcast_in_dim.53
  0.7 0.1 broadcast_in_dim.54
  0.8 0.0 copy-start.9
  0.8 2.3 %bitcast_select_fusion = bf16[16,128,256]{2,1,0:T(8,128)(2,1)} fusion(pred[16]{0:T(512)(128)(4,1)S(1)} %broadcast_in_dim.54, bf16[2,128,256]{2,1,0:T(8,128)(2,1)} %bitcast.21, bf16[4,2,128,256]{3,2,1,0:T(8,128)(2,1)} %bitcast.20), kind=kLoop, calls=%fused_computation | loop fusion | flops 524288 | bytes 1703952 | tf_op jit(solution)/shard_map/jit(_where)/select_n | solution.py:245
  3.2 11.8 %all-to-all-start = ((bf16[16,128,256]{2,1,0:T(8,128)(2,1)}), bf16[16,128,256]{2,1,0:T(8,128)(2,1)S(1)}, u32[]{:S(2)}, u32[]{:S(2)}) async-start(bf16[16,128,256]{2,1,0:T(8,128)(2,1)} %bitcast_select_fusion), calls=%async_computation | async-start | bytes 2097152 | tf_op jit(solution)/shard_map/all_to_all | solution.py:215
  15.0 0.0 copy-done.10
  15.0 0.6 constant_dynamic-slice_fusion.1
  15.6 0.0 copy-done.9
  15.6 0.2 fusion
  15.8 0.7 fusion.1
  16.5 0.7 pad_add_fusion
  17.2 2.0 %collective-permute-start = (s32[27]{0:T(128)S(1)}, s32[27]{0:T(128)S(1)}, u32[]{:S(2)}, u32[]{:S(2)}) collective-permute-start(s32[27]{0:T(128)S(1)} %pad_add_fusion), channel_id=1, source_target_pairs={{0,1},{1,0},{2,3},{3,2},{4,5},{5,4},{6,7},{7,6},{8,9},{9,8},{10,11... | collective-permute-start | bytes 332 | tf_op jit(solution)/shard_map/ppermute | solution.py:211
  19.3 0.9 dynamic-slice_bitcast_fusion.1.own_g
  20.2 2.3 %collective-permute-start.2 = (bf16[384,256]{1,0:T(8,128)(2,1)S(1)}, bf16[384,256]{1,0:T(8,128)(2,1)}, u32[]{:S(2)}, u32[]{:S(2)}) collective-permute-start(bf16[384,256]{1,0:T(8,128)(2,1)S(1)} %dynamic-slice_bitcast_fusion.1.own_g), channel_id=1, source_target_pairs={{0,1},{1,0},{2,3},{3,2},{4,5},{5,4},{6,7},{7,6},{8,9},{9,8},{10,11... | collective-permute-start | bytes 589832 | tf_op jit(solution)/shard_map/ppermute | solution.py:211
  22.5 0.0 copy-done
  22.6 2.0 %collective-permute-start.3 = (bf16[12,128,128]{2,1,0:T(8,128)(2,1)S(1)}, bf16[12,128,128]{2,1,0:T(8,128)(2,1)}, u32[]{:S(2)}, u32[]{:S(2)}) collective-permute-start(bf16[12,128,128]{2,1,0:T(8,128)(2,1)S(1)} %dynamic-slice_bitcast_fusion.own_t), channel_id=1, source_target_pairs={{0,1},{1,0},{2,3},{3,2},{4,5},{5,4},{6,7},{7,6},{8,9},{9,8},{10,11... | collective-permute-start | bytes 1179656 | tf_op jit(solution)/shard_map/ppermute | solution.py:211
  24.6 0.9 dynamic-slice_bitcast_fusion.2.own_x
  25.6 2.3 %collective-permute-start.1 = (bf16[384,256]{1,0:T(8,128)(2,1)S(1)}, bf16[384,256]{1,0:T(8,128)(2,1)}, u32[]{:S(2)}, u32[]{:S(2)}) collective-permute-start(bf16[384,256]{1,0:T(8,128)(2,1)S(1)} %dynamic-slice_bitcast_fusion.2.own_x), channel_id=1, source_target_pairs={{0,1},{1,0},{2,3},{3,2},{4,5},{5,4},{6,7},{7,6},{8,9},{9,8},{10,11... | collective-permute-start | bytes 589832 | tf_op jit(solution)/shard_map/ppermute | solution.py:211
  27.9 0.0 collective-permute-done
  27.9 0.1 pad_add_fusion.1.info
  28.0 0.0 collective-permute-done.2.got_g
  28.0 1.1 collective-permute-done.1.got_x
  29.0 0.0 collective-permute-done.3.got_t
  29.0 1.5 %shard_map.112 = (bf16[384,640]{1,0:T(8,128)(2,1)S(1)}, bf16[384,384]{1,0:T(8,128)(2,1)S(1)}, bf16[384,256]{1,0:T(8,128)(2,1)S(1)}, bf16[384,256]{1,0:T(8,128)(2,1)S(1)}) custom-call(s32[29]{0:T(128)S(1)} %pad_add_fusion.1.info, bf16[384,256]{1,0:T(8,128)(2,1)S(1)} %dynamic-slice_bitcast_fusion.2.own_x, bf16[384,256]{1,0:T(8,128)(2,1)} %collective-permute-done.1.got_x, ...), custom_call_target="tpu_custom_call" | custom-call | flops 1000000 | bytes 4000000 | tf_op jit(solution)/shard_map/pallas_call | solution.py:263
  30.6 0.0 copy-start.1
  30.6 0.7 copy-done.1
  31.3 0.7 copy-done.3
  32.0 0.8 copy-done.5
  32.7 0.7 copy-done.7
  33.4 9.5 %all-to-all-done.mine = bf16[16,128,256]{2,1,0:T(8,128)(2,1)S(1)} async-done(((bf16[16,128,256]{2,1,0:T(8,128)(2,1)}), bf16[16,128,256]{2,1,0:T(8,128)(2,1)S(1)}, u32[]{:S(2)}, u32[]{:S(2)}) %all-to-all-start) | async-done | bytes 1048608 | tf_op jit(solution)/shard_map/all_to_all | solution.py:215
  43.0 1.9 %collective-permute-start.4 = (bf16[16,128,256]{2,1,0:T(8,128)(2,1)S(1)}, bf16[16,128,256]{2,1,0:T(8,128)(2,1)S(1)}, u32[]{:S(2)}, u32[]{:S(2)}) collective-permute-start(bf16[16,128,256]{2,1,0:T(8,128)(2,1)S(1)} %all-to-all-done.mine), channel_id=1, source_target_pairs={{0,1},{1,0},{2,3},{3,2},{4,5},{5,4},{6,7},{7,6},{8,9},{9,8},{10,11... | collective-permute-start | bytes 3145736 | tf_op jit(solution)/shard_map/ppermute | solution.py:211
  44.9 2.6 %collective-permute-done.4.got = bf16[16,128,256]{2,1,0:T(8,128)(2,1)S(1)} collective-permute-done((bf16[16,128,256]{2,1,0:T(8,128)(2,1)S(1)}, bf16[16,128,256]{2,1,0:T(8,128)(2,1)S(1)}, u32[]{:S(2)}, u32[]{:S(2)}) %collective-permute-start.4) | collective-permute-done | bytes 1048608 | tf_op jit(solution)/shard_map/ppermute | solution.py:211
  47.5 1.0 copy-done.6
  48.5 0.9 copy-done.8
  49.5 4.7 %shard_map.113 = (bf16[8,384,256]{2,1,0:T(8,128)(2,1)S(1)}, f32[8,384,256]{2,1,0:T(8,128)S(1)}, bf16[8,128,256]{2,1,0:T(8,128)(2,1)S(1)}) custom-call(s32[29]{0:T(128)S(1)} %pad_add_fusion.1.info, f32[8]{0:T(128)S(1)} %add_log_fusion.rates, bf16[384,640]{1,0:T(8,128)(2,1)S(1)} %copy-done.6, bf16[384,256]{1,0:T(8,128)(2,1)S(1)} %copy-done.8, ...), custom_call_target="tpu_custom_call" | custom-call | flops 1400000000 | bytes 10000000 | tf_op jit(solution)/shard_map/pallas_call | solution.py:280
  54.2 5.3 %shard_map.114 = (bf16[32,32,256]{2,1,0:T(8,128)(2,1)S(1)}, bf16[8,192,256]{2,1,0:T(8,128)(2,1)S(1)}) custom-call(s32[29]{0:T(128)S(1)} %pad_add_fusion.1.info, f32[8]{0:T(128)S(1)} %add_log_fusion.rates, bf16[384,384]{1,0:T(8,128)(2,1)S(1)} %copy-done.2, bf16[384,256]{1,0:T(8,128)(2,1)S(1)} %copy-done.4, bf16[16,128,256]{2,1,0:T(8,128)(2,1)S(1)} %all-to-all-done.mine, ...), custom_call_target="tpu_custom_call" | custom-call | flops 1400000000 | bytes 10000000 | tf_op jit(solution)/shard_map/pallas_call | solution.py:296
  59.4 24.3 %all_to_all.20.pieces = bf16[32,32,256]{2,1,0:T(8,128)(2,1)S(1)} all-to-all(bf16[32,32,256]{2,1,0:T(8,128)(2,1)S(1)} %get-tuple-element.28), channel_id=1, replica_groups={{0,2,4,6,8,10,12,14,16,18,20,22,24,26,28,30,32,34,36,38,40,42,44,46,48,..., dimensions={0} | all-to-all | bytes 1048576 | tf_op jit(solution)/shard_map/all_to_all | solution.py:215
  83.7 0.1 shard_map.115
  83.8 21.1 %all_to_all.21.arrived = bf16[8,192,256]{2,1,0:T(8,128)(2,1)S(1)} all-to-all(bf16[8,192,256]{2,1,0:T(8,128)(2,1)S(1)} %shard_map.115), channel_id=1, replica_groups=mesh['section'=8,'dom'=64] {'section'}, dimensions={0} | all-to-all | bytes 1572864 | tf_op jit(solution)/shard_map/all_to_all | solution.py:215
  105.0 0.7 broadcast_in_dim.62
  105.7 13.5 %all-to-all-start.3 = ((f32[64,4,256]{2,1,0:T(4,128)}), f32[64,4,256]{2,1,0:T(4,128)S(1)}, u32[]{:S(2)}, u32[]{:S(2)}) async-start(f32[64,4,256]{2,1,0:T(4,128)} %broadcast_in_dim.62), calls=%async_computation.3 | async-start | bytes 524288 | tf_op jit(solution)/shard_map/all_to_all | solution.py:215
  119.3 0.7 shard_map.117
  120.0 3.5 %collective-permute-start.5 = (bf16[4,128,256]{2,1,0:T(8,128)(2,1)S(1)}, bf16[4,128,256]{2,1,0:T(8,128)(2,1)S(1)}, u32[]{:S(2)}, u32[]{:S(2)}) collective-permute-start(bf16[4,128,256]{2,1,0:T(8,128)(2,1)S(1)} %get-tuple-element.33), channel_id=1, source_target_pairs={{0,63},{1,2},{2,1},{3,4},{4,3},{5,6},{6,5},{7,8},{8,7},{9,10},{10,... | collective-permute-start | bytes 786440 | tf_op jit(solution)/shard_map/ppermute | solution.py:352
  123.5 6.6 %collective-permute-done.5.comes = bf16[4,128,256]{2,1,0:T(8,128)(2,1)S(1)} collective-permute-done((bf16[4,128,256]{2,1,0:T(8,128)(2,1)S(1)}, bf16[4,128,256]{2,1,0:T(8,128)(2,1)S(1)}, u32[]{:S(2)}, u32[]{:S(2)}) %collective-permute-start.5) | collective-permute-done | bytes 262176 | tf_op jit(solution)/shard_map/ppermute | solution.py:352
  130.2 0.8 shard_map.118
  131.0 0.6 all-to-all-done.3.spread
  131.5 0.7 shard_map.116
  (16 shorter events, 0.1 us)
Async XLA Ops:
  0.6 21.9 %copy-start = (bf16[4,12,128,128]{3,2,1,0:T(8,128)(2,1)S(1)}, bf16[4,12,128,128]{3,2,1,0:T(8,128)(2,1)}, u32[]{:S(2)}) copy-start(bf16[4,12,128,128]{3,2,1,0:T(8,128)(2,1)} %param.13) | copy-start | bytes 4718596
  0.8 14.2 %copy-start.10 = (s32[4,1]{0,1:T(1,128)S(1)}, s32[4,1]{0,1:T(1,128)}, u32[]{:S(2)}) copy-start(s32[4,1]{0,1:T(1,128)} %param.16) | copy-start | bytes 52
  0.8 14.8 %copy-start.9 = (s32[4,2]{0,1:T(2,128)S(1)}, s32[4,2]{0,1:T(2,128)}, u32[]{:S(2)}) copy-start(s32[4,2]{0,1:T(2,128)} %param.17) | copy-start | bytes 100
  3.2 39.8 %all-to-all-start = ((bf16[16,128,256]{2,1,0:T(8,128)(2,1)}), bf16[16,128,256]{2,1,0:T(8,128)(2,1)S(1)}, u32[]{:S(2)}, u32[]{:S(2)}) async-start(bf16[16,128,256]{2,1,0:T(8,128)(2,1)} %bitcast_select_fusion), calls=%async_computation | async-start | bytes 2097152 | tf_op jit(solution)/shard_map/all_to_all | solution.py:215
  17.2 10.7 %collective-permute-start = (s32[27]{0:T(128)S(1)}, s32[27]{0:T(128)S(1)}, u32[]{:S(2)}, u32[]{:S(2)}) collective-permute-start(s32[27]{0:T(128)S(1)} %pad_add_fusion), channel_id=1, source_target_pairs={{0,1},{1,0},{2,3},{3,2},{4,5},{5,4},{6,7},{7,6},{8,9},{9,8},{10,11... | collective-permute-start | bytes 332 | tf_op jit(solution)/shard_map/ppermute | solution.py:211
  20.2 7.8 %collective-permute-start.2 = (bf16[384,256]{1,0:T(8,128)(2,1)S(1)}, bf16[384,256]{1,0:T(8,128)(2,1)}, u32[]{:S(2)}, u32[]{:S(2)}) collective-permute-start(bf16[384,256]{1,0:T(8,128)(2,1)S(1)} %dynamic-slice_bitcast_fusion.1.own_g), channel_id=1, source_target_pairs={{0,1},{1,0},{2,3},{3,2},{4,5},{5,4},{6,7},{7,6},{8,9},{9,8},{10,11... | collective-permute-start | bytes 589832 | tf_op jit(solution)/shard_map/ppermute | solution.py:211
  22.6 6.5 %collective-permute-start.3 = (bf16[12,128,128]{2,1,0:T(8,128)(2,1)S(1)}, bf16[12,128,128]{2,1,0:T(8,128)(2,1)}, u32[]{:S(2)}, u32[]{:S(2)}) collective-permute-start(bf16[12,128,128]{2,1,0:T(8,128)(2,1)S(1)} %dynamic-slice_bitcast_fusion.own_t), channel_id=1, source_target_pairs={{0,1},{1,0},{2,3},{3,2},{4,5},{5,4},{6,7},{7,6},{8,9},{9,8},{10,11... | collective-permute-start | bytes 1179656 | tf_op jit(solution)/shard_map/ppermute | solution.py:211
  25.6 3.5 %collective-permute-start.1 = (bf16[384,256]{1,0:T(8,128)(2,1)S(1)}, bf16[384,256]{1,0:T(8,128)(2,1)}, u32[]{:S(2)}, u32[]{:S(2)}) collective-permute-start(bf16[384,256]{1,0:T(8,128)(2,1)S(1)} %dynamic-slice_bitcast_fusion.2.own_x), channel_id=1, source_target_pairs={{0,1},{1,0},{2,3},{3,2},{4,5},{5,4},{6,7},{7,6},{8,9},{9,8},{10,11... | collective-permute-start | bytes 589832 | tf_op jit(solution)/shard_map/ppermute | solution.py:211
  30.6 0.7 copy-start.1
  31.3 0.7 copy-start.3
  32.0 0.8 copy-start.5
  32.7 0.7 copy-start.7
  43.0 4.5 %collective-permute-start.4 = (bf16[16,128,256]{2,1,0:T(8,128)(2,1)S(1)}, bf16[16,128,256]{2,1,0:T(8,128)(2,1)S(1)}, u32[]{:S(2)}, u32[]{:S(2)}) collective-permute-start(bf16[16,128,256]{2,1,0:T(8,128)(2,1)S(1)} %all-to-all-done.mine), channel_id=1, source_target_pairs={{0,1},{1,0},{2,3},{3,2},{4,5},{5,4},{6,7},{7,6},{8,9},{9,8},{10,11... | collective-permute-start | bytes 3145736 | tf_op jit(solution)/shard_map/ppermute | solution.py:211
  47.5 1.0 copy-start.6
  48.5 0.9 copy-start.8
  49.5 4.7 %copy-start.2 = (bf16[384,384]{1,0:T(8,128)(2,1)S(1)}, bf16[384,384]{1,0:T(8,128)(2,1)}, u32[]{:S(2)}) copy-start(bf16[384,384]{1,0:T(8,128)(2,1)} %copy-done.1) | copy-start | bytes 884740
  49.5 4.7 %copy-start.4 = (bf16[384,256]{1,0:T(8,128)(2,1)S(1)}, bf16[384,256]{1,0:T(8,128)(2,1)}, u32[]{:S(2)}) copy-start(bf16[384,256]{1,0:T(8,128)(2,1)} %copy-done.3) | copy-start | bytes 589828
  105.7 25.8 %all-to-all-start.3 = ((f32[64,4,256]{2,1,0:T(4,128)}), f32[64,4,256]{2,1,0:T(4,128)S(1)}, u32[]{:S(2)}, u32[]{:S(2)}) async-start(f32[64,4,256]{2,1,0:T(4,128)} %broadcast_in_dim.62), calls=%async_computation.3 | async-start | bytes 524288 | tf_op jit(solution)/shard_map/all_to_all | solution.py:215
  120.0 10.2 %collective-permute-start.5 = (bf16[4,128,256]{2,1,0:T(8,128)(2,1)S(1)}, bf16[4,128,256]{2,1,0:T(8,128)(2,1)S(1)}, u32[]{:S(2)}, u32[]{:S(2)}) collective-permute-start(bf16[4,128,256]{2,1,0:T(8,128)(2,1)S(1)} %get-tuple-element.33), channel_id=1, source_target_pairs={{0,63},{1,2},{2,1},{3,4},{4,3},{5,6},{6,5},{7,8},{8,7},{9,10},{10,... | collective-permute-start | bytes 786440 | tf_op jit(solution)/shard_map/ppermute | solution.py:352

commit v3 on v2

--- a/solution.py
+++ b/solution.py
@@ -11,6 +11,7 @@
 ALPHA = 0.1
 LAMBDA_RATE = 0.5
 CORES = 2
+CHIPS_X = 4
 F32 = jnp.float32
 BF16 = jnp.bfloat16
 
@@ -33,6 +34,19 @@
         compiler_params=pltpu.CompilerParams(vmem_limit_bytes=24 * 1024 * 1024),
         cost_estimate=pl.CostEstimate(flops=flops, bytes_accessed=moved, transcendentals=0),
     )
+
+
+def slots_body(core_ref, halo, weight, out):
+    spans, _, _ = halo.shape
+    size = out.shape[1]
+    core = core_ref[0]
+    for parity in range(CORES):
+        mine = core == parity
+        for span in range(spans):
+            for half in range(CORES):
+                slot = (parity * spans + span) * CORES + half
+                block = slice(half * size, (half + 1) * size)
+                out[slot] = jnp.where(mine, halo[span, block, :], weight[block, :])
 
 
 def prepare_body(
@@ -105,13 +119,12 @@
 
 
 def backward_body(
-    tiles_max, info, rates, flipped, g0, mine, got, mix, slope, fresh, terms, parcel, grad, acc, last,
-    dweight, sorted_rows
+    tiles_max, info, rates, flipped, g0, mine, got, mix, slope, terms, columns, grad, acc, last
 ):
-    depth, size, width = fresh.shape
-    half = dweight.shape[1]
-    chips = terms.shape[0]
-    few = half // chips
+    depth, _, width = columns.shape
+    parts = terms.shape[0]
+    few = terms.shape[1] // depth
+    half = parts * few
     core = info[2 * tiles_max + 3]
     parity = info[2 * tiles_max + 4]
     grad[...] = g0[...]
@@ -123,9 +136,12 @@
         delta = (grad[...].astype(F32) * slope[layer]).astype(BF16)
         start = pl.multiple_of(core * half, half)
         part = mix[layer, :, pl.ds(start, half)]
-        dweight[layer] = lax.dot_general(
+        dweight = lax.dot_general(
             part, delta, (((0,), (0,)), ((), ())), preferred_element_type=F32
-        )
+        ).astype(BF16)
+        row = pl.multiple_of(layer * few, few)
+        for piece in range(parts):
+            terms[piece, pl.ds(row, few), :] = dweight[piece * few : (piece + 1) * few]
         weight = weight_of(core, parity, mine, got, layer)
         dmix = (1.0 - rate) * delta.astype(F32) + rate * lax.dot_general(
             delta, weight, (((1,), (1,)), ((), ())), preferred_element_type=F32
@@ -138,38 +154,28 @@
         return carry
 
     lax.fori_loop(0, depth, step, 0)
-    for chip in range(chips):
-        for layer in range(depth):
-            sorted_rows[chip, layer * few : (layer + 1) * few, :] = dweight[
-                layer, chip * few : (chip + 1) * few, :
-            ]
-    terms[...] = sorted_rows[...].astype(BF16)
     dinput = (acc[...] + last[...]).T.astype(BF16)
     share = width // depth
     hop = share // 2
     for part in range(depth):
         piece = dinput[part * share : (part + 1) * share]
-        parcel[part, :size, :] = fresh[part]
-        parcel[part, size : size + share, :] = piece[:, :width]
-        parcel[part, size + share : size + share + hop, : width // 2] = piece[:hop, width:]
-        parcel[part, size + share : size + share + hop, width // 2 :] = piece[hop:, width:]
-        rest = parcel.shape[1] - (size + share + hop)
-        parcel[part, size + share + hop :, :] = jnp.zeros((rest, width), BF16)
-
-
-def merge_body(tail, pieces, parcel_in, parcel):
-    depth, deep, _ = parcel.shape
+        columns[part, :share, :] = piece[:, :width]
+        columns[part, share:, : width // 2] = piece[:hop, width:]
+        columns[part, share:, width // 2 :] = piece[hop:, width:]
+
+
+def merge_body(pieces, fresh, columns, parcel):
+    depth, size, _ = fresh.shape
     few = pieces.shape[1] // depth
-    total = pieces[0].astype(F32)
-    for chip in range(1, pieces.shape[0]):
-        total += pieces[chip].astype(F32)
-    parcel[...] = parcel_in[...]
+    middle = size + columns.shape[1]
     for layer in range(depth):
-        part = total[layer * few : (layer + 1) * few]
-        if few < tail:
-            pad = jnp.zeros((tail - few, part.shape[1]), F32)
-            part = jnp.concatenate([part, pad], axis=0)
-        parcel[layer, deep - tail :, :] = part.astype(BF16)
+        parcel[layer, :size, :] = fresh[layer]
+        parcel[layer, size:middle, :] = columns[layer]
+        rows = slice(layer * few, (layer + 1) * few)
+        total = pieces[0, rows, :].astype(F32)
+        for chip in range(1, pieces.shape[0]):
+            total += pieces[chip, rows, :].astype(F32)
+        parcel[layer, middle:, :] = total.astype(BF16)
 
 
 def unpack_body(size, core_ref, arrived, out, stays, leaves):
@@ -195,15 +201,6 @@
         own, other = stays[span], comes[span]
         out[0, span, :size, :] = jnp.where(first, other, own)
         out[0, span, size:, :] = jnp.where(first, own, other)
-
-
-def assemble_body(spread, out):
-    doms, few, _ = spread.shape
-    chips = doms // CORES
-    for core in range(CORES):
-        for chip in range(chips):
-            row = (core * chips + chip) * few
-            out[0, row : row + few, :] = spread[CORES * chip + core]
 
 
 def swap(value):
@@ -239,10 +236,14 @@
     parity = section // spans
     rates = jnp.log(LAMBDA_RATE / (jnp.arange(depth, dtype=F32) + 1.0) + 1.0)
 
-    halo = stale_halo[0].reshape(1, spans, CORES, size, width)
-    weight = layer_weights[0].reshape(1, 1, CORES, half, width)
-    choose = (jnp.arange(CORES) == core)[:, None, None, None, None]
-    slots = jnp.where(choose, halo, weight).reshape(depth * CORES, size, width)
+    slots = call(
+        slots_body,
+        jax.ShapeDtypeStruct((depth * CORES, size, width), BF16),
+        [smem(), vmem(), vmem()],
+        [],
+        10**5,
+        10**6,
+    )(core.astype(jnp.int32)[None], stale_halo[0], layer_weights[0])
     column = [
         [z * doms + CORES * i + j for z in range(depth) for j in range(CORES)] for i in range(chips)
     ]
@@ -290,52 +291,55 @@
         10**7,
     )(info, rates, dense, x0, mine, got)
 
-    few = half // chips
-    tail = max(16, few)
-    deep = size + width // depth + width // depth // 2 + tail
-    terms, parcel = call(
+    few = half // CHIPS_X
+    spare = width // depth + width // depth // 2
+    terms, columns = call(
         functools.partial(backward_body, tiles_max),
         (
-            jax.ShapeDtypeStruct((chips, depth * few, width), BF16),
-            jax.ShapeDtypeStruct((depth, deep, width), BF16),
-        ),
-        [smem()] * 2 + [vmem()] * 7,
+            jax.ShapeDtypeStruct((CHIPS_X, depth * few, width), BF16),
+            jax.ShapeDtypeStruct((depth, spare, width), BF16),
+        ),
+        [smem()] * 2 + [vmem()] * 6,
         [
             pltpu.VMEM((rows, width), BF16),
             pltpu.VMEM((rows, width), F32),
             pltpu.VMEM((rows, width), F32),
-            pltpu.VMEM((depth, half, width), F32),
-            pltpu.VMEM((chips, depth * few, width), F32),
         ],
         1400 * 10**6,
         10**7,
-    )(info, rates, flipped, g0, mine, got, mix, slope, fresh_out)
-
-    groups = [[CORES * i + j for i in range(chips)] for j in range(CORES)]
-    pieces = exchange(terms, "dom", groups)
+    )(info, rates, flipped, g0, mine, got, mix, slope)
+
+    chips_y = chips // CHIPS_X
+    along_x = [
+        [(x * chips_y + y) * CORES + j for x in range(CHIPS_X)]
+        for y in range(chips_y)
+        for j in range(CORES)
+    ]
+    along_y = [
+        [(x * chips_y + y) * CORES + j for y in range(chips_y)]
+        for x in range(CHIPS_X)
+        for j in range(CORES)
+    ]
+    pairs = [[CORES * i + j for j in range(CORES)] for i in range(chips)]
+    pieces = exchange(terms, "dom", along_x)
     parcel = call(
-        functools.partial(merge_body, tail),
-        jax.ShapeDtypeStruct((depth, deep, width), BF16),
-        [vmem()] * 2,
+        merge_body,
+        jax.ShapeDtypeStruct((depth, size + spare + few, width), BF16),
+        [vmem()] * 3,
         [],
         10**6,
         10**6,
-    )(pieces, parcel)
+    )(pieces, fresh_out, columns)
 
     arrived = exchange(parcel, "section")
     scale = 1.0 / math.sqrt(spans * rows * doms)
-    piece = arrived[:, deep - tail : deep - tail + few, :].astype(F32).sum(axis=0) * scale
-    copies = jnp.broadcast_to(piece[None], (doms,) + piece.shape)
+    piece = arrived[:, size + spare :, :].astype(F32).sum(axis=0).astype(BF16)
+    copies = jnp.broadcast_to(piece[None], (chips_y,) + piece.shape)
     copies, arrived = lax.optimization_barrier((copies, arrived))
-    spread = exchange(copies, "dom")
-    weight_grad = call(
-        assemble_body,
-        jax.ShapeDtypeStruct((1, width, width), F32),
-        [vmem()],
-        [],
-        10**5,
-        10**6,
-    )(spread)
+    piece = exchange(copies, "dom", along_y).astype(F32).sum(axis=0) * scale
+    copies = jnp.broadcast_to(piece[None], (CHIPS_X,) + piece.shape)
+    piece = exchange(copies, "dom", along_x).reshape(half, width)
+    weight_grad = lax.all_gather(piece, "dom", axis_index_groups=pairs, tiled=True)[None]
 
     initial_grad, stays, leaves = call(
         functools.partial(unpack_body, size),

time: 133 us -> 131 us (0.985)
  waiting for transfers between devices: 20.4 us -> 17.1 us
  local copies, waits for them, and re-layouts: 9.13 us -> 12.3 us
  other arithmetic: 3.19 us -> 0.87 us
    all_to_all x2, blocking collectives: 45.4 us -> 36.9 us  [exchange(): lax.all_to_all(value, axis, 0, 0, tiled=True, axis_index_groups=groups)]
    all_gather x0 -> x1, blocking collectives: none -> 7.69 us  [shards(): lax.all_gather(piece, 'dom', axis_index_groups=pairs, tiled=True)[None]]
    ppermute x1, waiting for transfers between devices: 6.63 us -> 0.37 us  [shards(): lax.ppermute(leaves, 'dom', [(i, (i - 1) % doms if i % 2 == 0 else (i + 1...]
    ppermute x1, starting transfers between devices: 3.53 us -> 7.63 us  [shards(): lax.ppermute(leaves, 'dom', [(i, (i - 1) % doms if i % 2 == 0 else (i + 1...]
    all_to_all x2 -> x3, starting transfers between devices: 25.4 us -> 22.1 us  [exchange(): lax.all_to_all(value, axis, 0, 0, tiled=True, axis_index_groups=groups)]
    all_to_all x2 -> x3, waiting for transfers between devices: 10.1 us -> 13.1 us  [exchange(): lax.all_to_all(value, axis, 0, 0, tiled=True, axis_index_groups=groups)]
    unnamed x22 -> x27, local copies, waits for them, and re-layouts: 4.82 us -> 7.57 us
    select_n x1 -> x0, other arithmetic: 2.35 us -> none  [shards(): slots = jnp.where(choose, halo, weight).reshape(depth * CORES, size, width)]
  transfers between devices with their start and end apart: 8 -> 9, of which waited for: 5 -> 5; matrix products, arithmetic and copies ran while one was open for 3% -> 4% of each run, Pallas kernels for 2% -> 2%
where the time goes in v3:
time: 131 us; the launch traced here: 130 us
  blocking collectives  44.5 us (34%)
  starting transfers between devices  40.3 us (31%)
  waiting for transfers between devices  17.1 us (13%)
  Pallas kernels  14 us (11%)
  local copies, waits for them, and re-layouts  12.3 us (9%)
    all_to_all x2, blocking collectives, exchange(): lax.all_to_all(value, axis, 0, 0, tiled=True, axis_index_groups=groups)  36.9 us
    all_to_all x3, starting transfers between devices, exchange(): lax.all_to_all(value, axis, 0, 0, tiled=True, axis_index_groups=groups)  22.1 us
    all_to_all x3, waiting for transfers between devices, exchange(): lax.all_to_all(value, axis, 0, 0, tiled=True, axis_index_groups=groups)  13.1 us
    ppermute x5, starting transfers between devices, swap(): return lax.ppermute(value, 'dom', [(i, i ^ 1) for i in range(size)])  10.6 us
    all_gather x1, blocking collectives, shards(): lax.all_gather(piece, 'dom', axis_index_groups=pairs, tiled=True)[None]  7.69 us
    ppermute x1, starting transfers between devices, shards(): lax.ppermute(leaves, 'dom', [(i, (i - 1) % doms if i % 2 == 0 else (i + 1...  7.63 us
    unnamed x27, local copies, waits for them, and re-layouts  7.57 us
    pallas_call x1, Pallas kernels, shards(): call(functools.partial(backward_body, tiles_max), (jax.ShapeDtypeStruct((...  5.08 us
  transfers between devices with their start and end apart: 9, of which 5 were waited for; matrix products, arithmetic and copies ran while one was open for 4% of the time, Pallas kernels for 2%

profile of v3, /device:TPU:1, one launch (start us, length us, event | category | flops | bytes accessed | tf_op | source)
XLA Modules:
  0.0 130.0 jit_solution(3218365212903284847)
XLA Ops:
  0.6 0.0 copy-start
  0.7 1.1 copy-done.1
  1.8 0.9 copy-done.6
  2.7 1.1 shard_map.113
  3.8 11.8 %all-to-all-start = ((bf16[16,128,256]{2,1,0:T(8,128)(2,1)}), bf16[16,128,256]{2,1,0:T(8,128)(2,1)S(1)}, u32[]{:S(2)}, u32[]{:S(2)}) async-start(bf16[16,128,256]{2,1,0:T(8,128)(2,1)} %shard_map.113), calls=%async_computation | async-start | bytes 2097152 | tf_op jit(solution)/shard_map/all_to_all | solution.py:212
  15.6 0.0 copy-done.12
  15.6 0.6 constant_dynamic-slice_fusion.1
  16.2 0.2 fusion
  16.4 0.7 fusion.1
  17.1 0.7 pad_add_fusion
  17.8 2.0 %collective-permute-start = (s32[27]{0:T(128)S(1)}, s32[27]{0:T(128)S(1)}, u32[]{:S(2)}, u32[]{:S(2)}) collective-permute-start(s32[27]{0:T(128)S(1)} %pad_add_fusion), channel_id=1, source_target_pairs={{0,1},{1,0},{2,3},{3,2},{4,5},{5,4},{6,7},{7,6},{8,9},{9,8},{10,11... | collective-permute-start | bytes 332 | tf_op jit(solution)/shard_map/ppermute | solution.py:208
  19.9 0.9 dynamic-slice_bitcast_fusion.1.own_g
  20.8 2.3 %collective-permute-start.2 = (bf16[384,256]{1,0:T(8,128)(2,1)S(1)}, bf16[384,256]{1,0:T(8,128)(2,1)}, u32[]{:S(2)}, u32[]{:S(2)}) collective-permute-start(bf16[384,256]{1,0:T(8,128)(2,1)S(1)} %dynamic-slice_bitcast_fusion.1.own_g), channel_id=1, source_target_pairs={{0,1},{1,0},{2,3},{3,2},{4,5},{5,4},{6,7},{7,6},{8,9},{9,8},{10,11... | collective-permute-start | bytes 589832 | tf_op jit(solution)/shard_map/ppermute | solution.py:208
  23.2 2.0 %collective-permute-start.3 = (bf16[12,128,128]{2,1,0:T(8,128)(2,1)S(1)}, bf16[12,128,128]{2,1,0:T(8,128)(2,1)}, u32[]{:S(2)}, u32[]{:S(2)}) collective-permute-start(bf16[12,128,128]{2,1,0:T(8,128)(2,1)S(1)} %dynamic-slice_bitcast_fusion.own_t), channel_id=1, source_target_pairs={{0,1},{1,0},{2,3},{3,2},{4,5},{5,4},{6,7},{7,6},{8,9},{9,8},{10,11... | collective-permute-start | bytes 1179656 | tf_op jit(solution)/shard_map/ppermute | solution.py:208
  25.2 0.9 dynamic-slice_bitcast_fusion.2.own_x
  26.2 2.3 %collective-permute-start.1 = (bf16[384,256]{1,0:T(8,128)(2,1)S(1)}, bf16[384,256]{1,0:T(8,128)(2,1)}, u32[]{:S(2)}, u32[]{:S(2)}) collective-permute-start(bf16[384,256]{1,0:T(8,128)(2,1)S(1)} %dynamic-slice_bitcast_fusion.2.own_x), channel_id=1, source_target_pairs={{0,1},{1,0},{2,3},{3,2},{4,5},{5,4},{6,7},{7,6},{8,9},{9,8},{10,11... | collective-permute-start | bytes 589832 | tf_op jit(solution)/shard_map/ppermute | solution.py:208
  28.5 0.0 collective-permute-done
  28.5 0.1 pad_add_fusion.1.info
  28.6 0.0 collective-permute-done.2.got_g
  28.6 1.1 collective-permute-done.1.got_x
  29.6 0.0 collective-permute-done.3.got_t
  29.6 1.6 %shard_map.112 = (bf16[384,640]{1,0:T(8,128)(2,1)S(1)}, bf16[384,384]{1,0:T(8,128)(2,1)S(1)}, bf16[384,256]{1,0:T(8,128)(2,1)S(1)}, bf16[384,256]{1,0:T(8,128)(2,1)S(1)}) custom-call(s32[29]{0:T(128)S(1)} %pad_add_fusion.1.info, bf16[384,256]{1,0:T(8,128)(2,1)S(1)} %dynamic-slice_bitcast_fusion.2.own_x, bf16[384,256]{1,0:T(8,128)(2,1)} %collective-permute-done.1.got_x, ...), custom_call_target="tpu_custom_call" | custom-call | flops 1000000 | bytes 4000000 | tf_op jit(solution)/shard_map/pallas_call | solution.py:264
  31.2 0.7 copy-done.2
  31.9 0.7 copy-done.4
  32.6 0.8 copy-done.7
  33.4 0.7 copy-done.9
  34.1 9.5 %all-to-all-done.mine = bf16[16,128,256]{2,1,0:T(8,128)(2,1)S(1)} async-done(((bf16[16,128,256]{2,1,0:T(8,128)(2,1)}), bf16[16,128,256]{2,1,0:T(8,128)(2,1)S(1)}, u32[]{:S(2)}, u32[]{:S(2)}) %all-to-all-start) | async-done | bytes 1048608 | tf_op jit(solution)/shard_map/all_to_all | solution.py:212
  43.6 1.9 %collective-permute-start.4 = (bf16[16,128,256]{2,1,0:T(8,128)(2,1)S(1)}, bf16[16,128,256]{2,1,0:T(8,128)(2,1)S(1)}, u32[]{:S(2)}, u32[]{:S(2)}) collective-permute-start(bf16[16,128,256]{2,1,0:T(8,128)(2,1)S(1)} %all-to-all-done.mine), channel_id=1, source_target_pairs={{0,1},{1,0},{2,3},{3,2},{4,5},{5,4},{6,7},{7,6},{8,9},{9,8},{10,11... | collective-permute-start | bytes 3145736 | tf_op jit(solution)/shard_map/ppermute | solution.py:208
  45.5 2.6 %collective-permute-done.4.got = bf16[16,128,256]{2,1,0:T(8,128)(2,1)S(1)} collective-permute-done((bf16[16,128,256]{2,1,0:T(8,128)(2,1)S(1)}, bf16[16,128,256]{2,1,0:T(8,128)(2,1)S(1)}, u32[]{:S(2)}, u32[]{:S(2)}) %collective-permute-start.4) | collective-permute-done | bytes 1048608 | tf_op jit(solution)/shard_map/ppermute | solution.py:208
  48.1 1.0 copy-done.8
  49.1 0.9 copy-done.10
  50.1 4.7 %shard_map.114 = (bf16[8,384,256]{2,1,0:T(8,128)(2,1)S(1)}, f32[8,384,256]{2,1,0:T(8,128)S(1)}, bf16[8,128,256]{2,1,0:T(8,128)(2,1)S(1)}) custom-call(s32[29]{0:T(128)S(1)} %pad_add_fusion.1.info, f32[8]{0:T(128)S(1)} %add_log_fusion.rates, bf16[384,640]{1,0:T(8,128)(2,1)S(1)} %copy-done.8, bf16[384,256]{1,0:T(8,128)(2,1)S(1)} %copy-done.10, ...), custom_call_target="tpu_custom_call" | custom-call | flops 1400000000 | bytes 10000000 | tf_op jit(solution)/shard_map/pallas_call | solution.py:281
  54.8 5.1 %shard_map.115 = (bf16[4,256,256]{2,1,0:T(8,128)(2,1)S(1)}, bf16[8,48,256]{2,1,0:T(8,128)(2,1)S(1)}) custom-call(s32[29]{0:T(128)S(1)} %pad_add_fusion.1.info, f32[8]{0:T(128)S(1)} %add_log_fusion.rates, bf16[384,384]{1,0:T(8,128)(2,1)S(1)} %copy-done.3, bf16[384,256]{1,0:T(8,128)(2,1)S(1)} %copy-done.5, bf16[16,128,256]{2,1,0:T(8,128)(2,1)S(1)} %all-to-all-done.mine, ...), custom_call_target="tpu_custom_call" | custom-call | flops 1400000000 | bytes 10000000 | tf_op jit(solution)/shard_map/pallas_call | solution.py:296
  59.9 12.9 %all_to_all.25.pieces = bf16[4,256,256]{2,1,0:T(8,128)(2,1)S(1)} all-to-all(bf16[4,256,256]{2,1,0:T(8,128)(2,1)S(1)} %get-tuple-element.27), channel_id=1, replica_groups={{0,16,32,48},{1,17,33,49},{2,18,34,50},{3,19,35,51},{4,20,36,52},{5,21,..., dimensions={0} | all-to-all | bytes 1048576 | tf_op jit(solution)/shard_map/all_to_all | solution.py:212
  72.8 0.1 shard_map.116
  72.9 23.9 %all_to_all.26.arrived = bf16[8,208,256]{2,1,0:T(8,128)(2,1)S(1)} all-to-all(bf16[8,208,256]{2,1,0:T(8,128)(2,1)S(1)} %shard_map.116), channel_id=1, replica_groups=mesh['section'=8,'dom'=64] {'section'}, dimensions={0} | all-to-all | bytes 1703936 | tf_op jit(solution)/shard_map/all_to_all | solution.py:212
  96.8 0.7 broadcast_in_dim.12
  97.5 6.9 %all-to-all-start.3 = ((bf16[8,32,256]{2,1,0:T(8,128)(2,1)}), bf16[8,32,256]{2,1,0:T(8,128)(2,1)S(1)}, u32[]{:S(2)}, u32[]{:S(2)}) async-start(bf16[8,32,256]{2,1,0:T(8,128)(2,1)} %broadcast_in_dim.12), calls=%async_computation.3 | async-start | bytes 262144 | tf_op jit(solution)/shard_map/all_to_all | solution.py:212
  104.4 0.7 shard_map.117
  105.2 7.6 %collective-permute-start.5 = (bf16[4,128,256]{2,1,0:T(8,128)(2,1)S(1)}, bf16[4,128,256]{2,1,0:T(8,128)(2,1)S(1)}, u32[]{:S(2)}, u32[]{:S(2)}) collective-permute-start(bf16[4,128,256]{2,1,0:T(8,128)(2,1)S(1)} %get-tuple-element.33), channel_id=1, source_target_pairs={{0,63},{1,2},{2,1},{3,4},{4,3},{5,6},{6,5},{7,8},{8,7},{9,10},{10,... | collective-permute-start | bytes 786440 | tf_op jit(solution)/shard_map/ppermute | solution.py:356
  112.8 0.0 all-to-all-done.3
  112.8 0.7 broadcast_in_dim.13
  113.5 3.3 %all-to-all-start.4 = ((f32[4,32,256]{2,1,0:T(8,128)}), f32[4,32,256]{2,1,0:T(8,128)S(1)}, u32[]{:S(2)}, u32[]{:S(2)}) async-start(f32[4,32,256]{2,1,0:T(8,128)} %broadcast_in_dim.13), calls=%async_computation.4 | async-start | bytes 262144 | tf_op jit(solution)/shard_map/all_to_all | solution.py:212
  116.8 0.4 collective-permute-done.5.comes
  117.2 0.8 shard_map.118
  118.0 3.6 %all-to-all-done.4 = f32[4,32,256]{2,1,0:T(8,128)S(1)} async-done(((f32[4,32,256]{2,1,0:T(8,128)}), f32[4,32,256]{2,1,0:T(8,128)S(1)}, u32[]{:S(2)}, u32[]{:S(2)}) %all-to-all-start.4) | async-done | bytes 131104 | tf_op jit(solution)/shard_map/all_to_all | solution.py:212
  121.6 7.7 %all_gather.3 = f32[256,256]{1,0:T(8,128)S(1)} all-gather(f32[128,256]{1,0:T(8,128)S(1)} %bitcast.21), channel_id=1, replica_groups={{0,1},{2,3},{4,5},{6,7},{8,9},{10,11},{12,13},{14,15},{16,17},{18,19},{..., dimensions={0}, use_global_device_ids=true | all-gather | bytes 393216 | tf_op jit(solution)/shard_map/all_gather | solution.py:342
  129.3 0.7 copy.13
  (22 shorter events, 0.1 us)
Async XLA Ops:
  0.6 22.5 %copy-start = (bf16[4,12,128,128]{3,2,1,0:T(8,128)(2,1)S(1)}, bf16[4,12,128,128]{3,2,1,0:T(8,128)(2,1)}, u32[]{:S(2)}) copy-start(bf16[4,12,128,128]{3,2,1,0:T(8,128)(2,1)} %param.13) | copy-start | bytes 4718596
  0.7 1.2 copy-start.1
  1.8 0.9 copy-start.6
  2.7 12.9 %copy-start.12 = (s32[4,1]{0,1:T(1,128)S(1)}, s32[4,1]{0,1:T(1,128)}, u32[]{:S(2)}) copy-start(s32[4,1]{0,1:T(1,128)} %param.16) | copy-start | bytes 52
  2.7 13.5 %copy-start.11 = (s32[4,2]{0,1:T(2,128)S(1)}, s32[4,2]{0,1:T(2,128)}, u32[]{:S(2)}) copy-start(s32[4,2]{0,1:T(2,128)} %param.17) | copy-start | bytes 100
  3.8 39.8 %all-to-all-start = ((bf16[16,128,256]{2,1,0:T(8,128)(2,1)}), bf16[16,128,256]{2,1,0:T(8,128)(2,1)S(1)}, u32[]{:S(2)}, u32[]{:S(2)}) async-start(bf16[16,128,256]{2,1,0:T(8,128)(2,1)} %shard_map.113), calls=%async_computation | async-start | bytes 2097152 | tf_op jit(solution)/shard_map/all_to_all | solution.py:212
  17.8 10.7 %collective-permute-start = (s32[27]{0:T(128)S(1)}, s32[27]{0:T(128)S(1)}, u32[]{:S(2)}, u32[]{:S(2)}) collective-permute-start(s32[27]{0:T(128)S(1)} %pad_add_fusion), channel_id=1, source_target_pairs={{0,1},{1,0},{2,3},{3,2},{4,5},{5,4},{6,7},{7,6},{8,9},{9,8},{10,11... | collective-permute-start | bytes 332 | tf_op jit(solution)/shard_map/ppermute | solution.py:208
  20.8 7.8 %collective-permute-start.2 = (bf16[384,256]{1,0:T(8,128)(2,1)S(1)}, bf16[384,256]{1,0:T(8,128)(2,1)}, u32[]{:S(2)}, u32[]{:S(2)}) collective-permute-start(bf16[384,256]{1,0:T(8,128)(2,1)S(1)} %dynamic-slice_bitcast_fusion.1.own_g), channel_id=1, source_target_pairs={{0,1},{1,0},{2,3},{3,2},{4,5},{5,4},{6,7},{7,6},{8,9},{9,8},{10,11... | collective-permute-start | bytes 589832 | tf_op jit(solution)/shard_map/ppermute | solution.py:208
  23.2 6.5 %collective-permute-start.3 = (bf16[12,128,128]{2,1,0:T(8,128)(2,1)S(1)}, bf16[12,128,128]{2,1,0:T(8,128)(2,1)}, u32[]{:S(2)}, u32[]{:S(2)}) collective-permute-start(bf16[12,128,128]{2,1,0:T(8,128)(2,1)S(1)} %dynamic-slice_bitcast_fusion.own_t), channel_id=1, source_target_pairs={{0,1},{1,0},{2,3},{3,2},{4,5},{5,4},{6,7},{7,6},{8,9},{9,8},{10,11... | collective-permute-start | bytes 1179656 | tf_op jit(solution)/shard_map/ppermute | solution.py:208
  26.2 3.5 %collective-permute-start.1 = (bf16[384,256]{1,0:T(8,128)(2,1)S(1)}, bf16[384,256]{1,0:T(8,128)(2,1)}, u32[]{:S(2)}, u32[]{:S(2)}) collective-permute-start(bf16[384,256]{1,0:T(8,128)(2,1)S(1)} %dynamic-slice_bitcast_fusion.2.own_x), channel_id=1, source_target_pairs={{0,1},{1,0},{2,3},{3,2},{4,5},{5,4},{6,7},{7,6},{8,9},{9,8},{10,11... | collective-permute-start | bytes 589832 | tf_op jit(solution)/shard_map/ppermute | solution.py:208
  31.2 0.7 copy-start.2
  31.9 0.7 copy-start.4
  32.6 0.8 copy-start.7
  33.4 0.7 copy-start.9
  43.6 4.5 %collective-permute-start.4 = (bf16[16,128,256]{2,1,0:T(8,128)(2,1)S(1)}, bf16[16,128,256]{2,1,0:T(8,128)(2,1)S(1)}, u32[]{:S(2)}, u32[]{:S(2)}) collective-permute-start(bf16[16,128,256]{2,1,0:T(8,128)(2,1)S(1)} %all-to-all-done.mine), channel_id=1, source_target_pairs={{0,1},{1,0},{2,3},{3,2},{4,5},{5,4},{6,7},{7,6},{8,9},{9,8},{10,11... | collective-permute-start | bytes 3145736 | tf_op jit(solution)/shard_map/ppermute | solution.py:208
  48.1 1.0 copy-start.8
  49.1 0.9 copy-start.10
  50.1 4.7 %copy-start.3 = (bf16[384,384]{1,0:T(8,128)(2,1)S(1)}, bf16[384,384]{1,0:T(8,128)(2,1)}, u32[]{:S(2)}) copy-start(bf16[384,384]{1,0:T(8,128)(2,1)} %copy-done.2) | copy-start | bytes 884740
  50.1 4.7 %copy-start.5 = (bf16[384,256]{1,0:T(8,128)(2,1)S(1)}, bf16[384,256]{1,0:T(8,128)(2,1)}, u32[]{:S(2)}) copy-start(bf16[384,256]{1,0:T(8,128)(2,1)} %copy-done.4) | copy-start | bytes 589828
  97.5 15.3 %all-to-all-start.3 = ((bf16[8,32,256]{2,1,0:T(8,128)(2,1)}), bf16[8,32,256]{2,1,0:T(8,128)(2,1)S(1)}, u32[]{:S(2)}, u32[]{:S(2)}) async-start(bf16[8,32,256]{2,1,0:T(8,128)(2,1)} %broadcast_in_dim.12), calls=%async_computation.3 | async-start | bytes 262144 | tf_op jit(solution)/shard_map/all_to_all | solution.py:212
  105.2 12.1 %collective-permute-start.5 = (bf16[4,128,256]{2,1,0:T(8,128)(2,1)S(1)}, bf16[4,128,256]{2,1,0:T(8,128)(2,1)S(1)}, u32[]{:S(2)}, u32[]{:S(2)}) collective-permute-start(bf16[4,128,256]{2,1,0:T(8,128)(2,1)S(1)} %get-tuple-element.33), channel_id=1, source_target_pairs={{0,63},{1,2},{2,1},{3,4},{4,3},{5,6},{6,5},{7,8},{8,7},{9,10},{10,... | collective-permute-start | bytes 786440 | tf_op jit(solution)/shard_map/ppermute | solution.py:356
  113.5 8.1 %all-to-all-start.4 = ((f32[4,32,256]{2,1,0:T(8,128)}), f32[4,32,256]{2,1,0:T(8,128)S(1)}, u32[]{:S(2)}, u32[]{:S(2)}) async-start(f32[4,32,256]{2,1,0:T(8,128)} %broadcast_in_dim.13), calls=%async_computation.4 | async-start | bytes 262144 | tf_op jit(solution)/shard_map/all_to_all | solution.py:212

commit v4 on v3

--- a/solution.py
+++ b/solution.py
@@ -24,29 +24,34 @@
     return pl.BlockSpec(memory_space=pltpu.SMEM)
 
 
-def call(body, out_shape, in_specs, scratch, flops, moved):
+def hbm():
+    return pl.BlockSpec(memory_space=pltpu.HBM)
+
+
+def call(body, out_shape, in_specs, scratch, flops, moved, place=vmem):
     return pl.pallas_call(
         body,
         out_shape=out_shape,
         in_specs=in_specs,
-        out_specs=jax.tree.map(lambda _: vmem(), out_shape),
+        out_specs=jax.tree.map(lambda _: place(), out_shape),
         scratch_shapes=scratch,
         compiler_params=pltpu.CompilerParams(vmem_limit_bytes=24 * 1024 * 1024),
         cost_estimate=pl.CostEstimate(flops=flops, bytes_accessed=moved, transcendentals=0),
     )
 
 
-def slots_body(core_ref, halo, weight, out):
-    spans, _, _ = halo.shape
-    size = out.shape[1]
+def slots_body(core_ref, halo, weight, out, sems):
+    spans = halo.shape[0]
     core = core_ref[0]
-    for parity in range(CORES):
-        mine = core == parity
-        for span in range(spans):
-            for half in range(CORES):
-                slot = (parity * spans + span) * CORES + half
-                block = slice(half * size, (half + 1) * size)
-                out[slot] = jnp.where(mine, halo[span, block, :], weight[block, :])
+    copies = [pltpu.make_async_copy(halo, out.at[core], sems.at[0])]
+    for span in range(spans):
+        copies.append(
+            pltpu.make_async_copy(weight.at[0], out.at[1 - core, span], sems.at[1 + span])
+        )
+    for copy in copies:
+        copy.start()
+    for copy in copies:
+        copy.wait()
 
 
 def prepare_body(
@@ -87,15 +92,25 @@
 
 
 def forward_body(
-    tiles_max, info, rates, dense, x0, mine, got, mix_out, slope_out, fresh, ext
+    tiles_max, info, rates, dense_far, x0_far, mine, got, mix_out, slope_out, fresh,
+    ext, dense, x0, base, sems
 ):
+    fetches = [
+        pltpu.make_async_copy(x0_far, x0, sems.at[0]),
+        pltpu.make_async_copy(dense_far, dense, sems.at[1]),
+    ]
+    for fetch in fetches:
+        fetch.start()
     rows = x0.shape[0]
     size = fresh.shape[1]
     half = mine.shape[1]
     core = info[2 * tiles_max + 3]
     parity = info[2 * tiles_max + 4]
     send = jnp.where(core == 0, info[2 * tiles_max + 1], info[2 * tiles_max + 2])
+    fetches[0].wait()
     ext[0:rows, :] = x0[...]
+    base[...] = ALPHA * x0[...].astype(F32)
+    fetches[1].wait()
 
     def step(layer, carry):
         rate = rates[layer]
@@ -104,27 +119,29 @@
         ext[rows : rows + half, :] = mine[CORES * layer + parity]
         ext[rows + half : rows + 2 * half, :] = got[CORES * layer + parity]
         agg = jnp.dot(dense[...], ext[...], preferred_element_type=F32)
-        mix = ((1.0 - ALPHA) * agg + ALPHA * x0[...].astype(F32)).astype(BF16)
+        mix = ((1.0 - ALPHA) * agg + base[...]).astype(BF16)
         mix_out[layer] = mix
         weight = weight_of(core, parity, mine, got, layer)
         pre = (1.0 - rate) * mix.astype(F32) + rate * jnp.dot(
             mix, weight, preferred_element_type=F32
         )
-        gate = jax.nn.sigmoid(pre)
-        slope_out[layer] = gate * (1.0 + pre * (1.0 - gate))
-        ext[0:rows, :] = (pre * gate).astype(BF16)
+        gate = 0.5 * jnp.tanh(0.5 * pre) + 0.5
+        silu = pre * gate
+        slope_out[layer] = gate + silu * (1.0 - gate)
+        ext[0:rows, :] = silu.astype(BF16)
         return carry
 
     lax.fori_loop(0, fresh.shape[0], step, 0)
 
 
 def backward_body(
-    tiles_max, info, rates, flipped, g0, mine, got, mix, slope, terms, columns, grad, acc, last
+    tiles_max, info, rates, flipped, g0, mine, got, mix, slope, *rest
 ):
+    terms, (columns, grad, acc, last, chunk) = rest[:CHIPS_X], rest[CHIPS_X:]
     depth, _, width = columns.shape
-    parts = terms.shape[0]
-    few = terms.shape[1] // depth
-    half = parts * few
+    few = terms[0].shape[0] // depth
+    half = CHIPS_X * few
+    spot = info[2 * tiles_max + 5]
     core = info[2 * tiles_max + 3]
     parity = info[2 * tiles_max + 4]
     grad[...] = g0[...]
@@ -136,25 +153,30 @@
         delta = (grad[...].astype(F32) * slope[layer]).astype(BF16)
         start = pl.multiple_of(core * half, half)
         part = mix[layer, :, pl.ds(start, half)]
-        dweight = lax.dot_general(
+        chunk[...] = lax.dot_general(
             part, delta, (((0,), (0,)), ((), ())), preferred_element_type=F32
         ).astype(BF16)
         row = pl.multiple_of(layer * few, few)
-        for piece in range(parts):
-            terms[piece, pl.ds(row, few), :] = dweight[piece * few : (piece + 1) * few]
+        for away in range(CHIPS_X):
+            piece = pl.multiple_of(lax.rem(spot + away, CHIPS_X) * few, few)
+            terms[away][pl.ds(row, few), :] = chunk[pl.ds(piece, few), :]
         weight = weight_of(core, parity, mine, got, layer)
         dmix = (1.0 - rate) * delta.astype(F32) + rate * lax.dot_general(
             delta, weight, (((1,), (1,)), ((), ())), preferred_element_type=F32
         )
-        acc[...] += ALPHA * dmix
+        acc[...] += dmix
         back = jnp.dot(flipped[...], dmix.astype(BF16), preferred_element_type=F32)
         gx = (1.0 - ALPHA) * back
-        last[...] = gx
+
+        @pl.when(layer == 0)
+        def _():
+            last[...] = gx
+
         grad[...] = gx.astype(BF16)
         return carry
 
     lax.fori_loop(0, depth, step, 0)
-    dinput = (acc[...] + last[...]).T.astype(BF16)
+    dinput = (ALPHA * acc[...] + last[...]).T.astype(BF16)
     share = width // depth
     hop = share // 2
     for part in range(depth):
@@ -164,34 +186,38 @@
         columns[part, share:, width // 2 :] = piece[hop:, width:]
 
 
-def merge_body(pieces, fresh, columns, parcel):
-    depth, size, _ = fresh.shape
-    few = pieces.shape[1] // depth
-    middle = size + columns.shape[1]
+def merge_body(*refs):
+    pieces, (columns, parcel) = refs[:CHIPS_X], refs[CHIPS_X:]
+    depth, spare, _ = columns.shape
+    few = pieces[0].shape[0] // depth
     for layer in range(depth):
-        parcel[layer, :size, :] = fresh[layer]
-        parcel[layer, size:middle, :] = columns[layer]
+        parcel[layer, :spare, :] = columns[layer]
         rows = slice(layer * few, (layer + 1) * few)
-        total = pieces[0, rows, :].astype(F32)
-        for chip in range(1, pieces.shape[0]):
-            total += pieces[chip, rows, :].astype(F32)
-        parcel[layer, middle:, :] = total.astype(BF16)
-
-
-def unpack_body(size, core_ref, arrived, out, stays, leaves):
+        total = pieces[0][rows, :].astype(F32)
+        for piece in pieces[1:]:
+            total += piece[rows, :].astype(F32)
+        parcel[layer, spare:, :] = total.astype(BF16)
+
+
+def unpack_body(core_ref, arrived, out):
     spans, share, _ = out.shape
     width = arrived.shape[-1]
     hop = share // 2
     base = core_ref[0] * spans
-    away = (1 - core_ref[0]) * spans
     for span in range(spans):
-        leaves[span] = arrived[base + span, :size, :]
-        stays[span] = arrived[away + span, :size, :]
-        top = arrived[base + span, size : size + share, :].astype(F32)
-        low = arrived[base + span, size + share : size + share + hop, :].astype(F32)
-        tail = jnp.concatenate([low[:, : width // 2], low[:, width // 2 :]], axis=0)
+        top = arrived[base + span, :share, :].astype(F32)
+        low = arrived[base + span, share : share + hop, :].astype(F32)
         out[span, :, :width] = top
-        out[span, :, width:] = tail
+        out[span, :hop, width:] = low[:, : width // 2]
+        out[span, hop:, width:] = low[:, width // 2 :]
+
+
+def part_body(core_ref, arrived, stays, leaves):
+    spans = stays.shape[0]
+    core = core_ref[0]
+    for span in range(spans):
+        leaves[span] = arrived[core * spans + span]
+        stays[span] = arrived[(1 - core) * spans + span]
 
 
 def fresh_body(core_ref, stays, comes, out):
@@ -232,18 +258,26 @@
     nblocks = rows // size
     half = width // 2
     chips = doms // CORES
+    chips_y = chips // CHIPS_X
+    spot = lax.axis_index("dom") // (CORES * chips_y)
+    core_ref = core.astype(jnp.int32)[None]
     span = section % spans
     parity = section // spans
     rates = jnp.log(LAMBDA_RATE / (jnp.arange(depth, dtype=F32) + 1.0) + 1.0)
 
     slots = call(
         slots_body,
-        jax.ShapeDtypeStruct((depth * CORES, size, width), BF16),
-        [smem(), vmem(), vmem()],
-        [],
+        jax.ShapeDtypeStruct((CORES, spans, CORES, size, width), BF16),
+        [smem(), hbm(), hbm()],
+        [pltpu.SemaphoreType.DMA((1 + spans,))],
         10**5,
         10**6,
-    )(core.astype(jnp.int32)[None], stale_halo[0], layer_weights[0])
+        hbm,
+    )(
+        core.astype(jnp.int32)[None],
+        stale_halo.reshape(spans, CORES, size, width),
+        layer_weights.reshape(1, CORES, half, width),
+    ).reshape(depth * CORES, size, width)
     column = [
         [z * doms + CORES * i + j for z in range(depth) for j in range(CORES)] for i in range(chips)
     ]
@@ -259,7 +293,7 @@
     is_mine = parity == core
     info = jnp.where(is_mine, own_info, swap(own_info))
     info = jnp.concatenate(
-        [info, core.astype(jnp.int32)[None], parity.astype(jnp.int32)[None]]
+        [info, core.astype(jnp.int32)[None], parity.astype(jnp.int32)[None], spot.astype(jnp.int32)[None]]
     )
     dense, flipped, x0, g0 = call(
         functools.partial(prepare_body, tiles_max, nblocks),
@@ -285,31 +319,65 @@
             jax.ShapeDtypeStruct((depth, rows, width), F32),
             jax.ShapeDtypeStruct((depth, size, width), BF16),
         ),
-        [smem()] * 2 + [vmem()] * 4,
-        [pltpu.VMEM((rows + 2 * size, width), BF16)],
+        [smem()] * 2 + [hbm()] * 2 + [vmem()] * 2,
+        [
+            pltpu.VMEM((rows + 2 * size, width), BF16),
+            pltpu.VMEM((rows, rows + 2 * size), BF16),
+            pltpu.VMEM((rows, width), BF16),
+            pltpu.VMEM((rows, width), F32),
+            pltpu.SemaphoreType.DMA((2,)),
+        ],
         1400 * 10**6,
         10**7,
     )(info, rates, dense, x0, mine, got)
 
+    fresh_in = exchange(fresh_out, "section")
+
     few = half // CHIPS_X
     spare = width // depth + width // depth // 2
-    terms, columns = call(
+    *terms, columns = call(
         functools.partial(backward_body, tiles_max),
-        (
-            jax.ShapeDtypeStruct((CHIPS_X, depth * few, width), BF16),
-            jax.ShapeDtypeStruct((depth, spare, width), BF16),
-        ),
+        (jax.ShapeDtypeStruct((depth * few, width), BF16),) * CHIPS_X
+        + (jax.ShapeDtypeStruct((depth, spare, width), BF16),),
         [smem()] * 2 + [vmem()] * 6,
         [
             pltpu.VMEM((rows, width), BF16),
             pltpu.VMEM((rows, width), F32),
             pltpu.VMEM((rows, width), F32),
+            pltpu.VMEM((half, width), BF16),
         ],
-        1400 * 10**6,
-        10**7,
+        100,
+        100,
     )(info, rates, flipped, g0, mine, got, mix, slope)
 
-    chips_y = chips // CHIPS_X
+    hop = CORES * chips_y
+    pieces = [terms[0]] + [
+        lax.ppermute(terms[k], "dom", [(i, (i + k * hop) % doms) for i in range(doms)])
+        for k in range(1, CHIPS_X)
+    ]
+    parcel = call(
+        merge_body,
+        jax.ShapeDtypeStruct((depth, spare + few, width), BF16),
+        [vmem()] * (CHIPS_X + 1),
+        [],
+        100,
+        100,
+    )(*pieces, columns)
+    parcel, fresh_in = lax.optimization_barrier((parcel, fresh_in))
+
+    arrived = exchange(parcel, "section")
+
+    stays, leaves = call(
+        part_body,
+        (jax.ShapeDtypeStruct((spans, size, width), BF16),) * 2,
+        [smem(), vmem()],
+        [],
+        100,
+        100,
+    )(core_ref, fresh_in)
+    comes = lax.ppermute(
+        leaves, "dom", [(i, (i - 1) % doms if i % 2 == 0 else (i + 1) % doms) for i in range(doms)]
+    )
     along_x = [
         [(x * chips_y + y) * CORES + j for x in range(CHIPS_X)]
         for y in range(chips_y)
@@ -321,41 +389,15 @@
         for j in range(CORES)
     ]
     pairs = [[CORES * i + j for j in range(CORES)] for i in range(chips)]
-    pieces = exchange(terms, "dom", along_x)
-    parcel = call(
-        merge_body,
-        jax.ShapeDtypeStruct((depth, size + spare + few, width), BF16),
-        [vmem()] * 3,
-        [],
-        10**6,
-        10**6,
-    )(pieces, fresh_out, columns)
-
-    arrived = exchange(parcel, "section")
     scale = 1.0 / math.sqrt(spans * rows * doms)
-    piece = arrived[:, size + spare :, :].astype(F32).sum(axis=0).astype(BF16)
+    piece = arrived[:, spare:, :].astype(F32).sum(axis=0).astype(BF16)
     copies = jnp.broadcast_to(piece[None], (chips_y,) + piece.shape)
-    copies, arrived = lax.optimization_barrier((copies, arrived))
+    copies, arrived, comes = lax.optimization_barrier((copies, arrived, comes))
     piece = exchange(copies, "dom", along_y).astype(F32).sum(axis=0) * scale
     copies = jnp.broadcast_to(piece[None], (CHIPS_X,) + piece.shape)
     piece = exchange(copies, "dom", along_x).reshape(half, width)
     weight_grad = lax.all_gather(piece, "dom", axis_index_groups=pairs, tiled=True)[None]
 
-    initial_grad, stays, leaves = call(
-        functools.partial(unpack_body, size),
-        (
-            jax.ShapeDtypeStruct((spans, width // depth, rows), F32),
-            jax.ShapeDtypeStruct((spans, size, width), BF16),
-            jax.ShapeDtypeStruct((spans, size, width), BF16),
-        ),
-        [smem(), vmem()],
-        [],
-        100,
-        100,
-    )(core.astype(jnp.int32)[None], arrived)
-    comes = lax.ppermute(
-        leaves, "dom", [(i, (i - 1) % doms if i % 2 == 0 else (i + 1) % doms) for i in range(doms)]
-    )
     fresh = call(
         fresh_body,
         jax.ShapeDtypeStruct((1, spans, 2 * size, width), BF16),
@@ -363,7 +405,16 @@
         [],
         100,
         100,
-    )(core.astype(jnp.int32)[None], stays, comes)
+    )(core_ref, stays, comes)
+
+    initial_grad = call(
+        unpack_body,
+        jax.ShapeDtypeStruct((spans, width // depth, rows), F32),
+        [smem(), vmem()],
+        [],
+        100,
+        100,
+    )(core_ref, arrived)
     return (weight_grad, fresh, initial_grad.transpose(0, 2, 1))
 
 

time: 131 us -> 139 us (1.061)
  blocking collectives: 44.5 us -> 21.8 us
  starting transfers between devices: 40.3 us -> 53.3 us
  local copies, waits for them, and re-layouts: 12.3 us -> 21 us
  waiting for transfers between devices: 17.1 us -> 24 us
  Pallas kernels: 14 us -> 15.5 us
    all_to_all x2 -> x1, blocking collectives: 36.9 us -> 14.6 us  [exchange(): lax.all_to_all(value, axis, 0, 0, tiled=True, axis_index_groups=groups)]
    ppermute x0 -> x3, starting transfers between devices: none -> 10.6 us  [shards(): lax.ppermute(terms[k], 'dom', [(i, (i + k * hop) % doms) for i in range(d...]
    unnamed x27 -> x41, local copies, waits for them, and re-layouts: 7.57 us -> 16.9 us
    all_to_all x3 -> x4, starting transfers between devices: 22.1 us -> 26.6 us  [exchange(): lax.all_to_all(value, axis, 0, 0, tiled=True, axis_index_groups=groups)]
    all_to_all x3 -> x4, waiting for transfers between devices: 13.1 us -> 17.2 us  [exchange(): lax.all_to_all(value, axis, 0, 0, tiled=True, axis_index_groups=groups)]
    ppermute x0 -> x3, waiting for transfers between devices: none -> 3.07 us  [shards(): lax.ppermute(terms[k], 'dom', [(i, (i + k * hop) % doms) for i in range(d...]
    ppermute x1, starting transfers between devices: 7.63 us -> 5.51 us  [shards(): lax.ppermute(leaves, 'dom', [(i, (i - 1) % doms if i % 2 == 0 else (i + 1...]
  transfers between devices with their start and end apart: 9 -> 13, of which waited for: 5 -> 7; matrix products, arithmetic and copies ran while one was open for 4% -> 3% of each run, Pallas kernels for 2% -> 7%
where the time goes in v4:
time: 139 us; the launch traced here: 137 us
  starting transfers between devices  53.3 us (38%)
  waiting for transfers between devices  24 us (17%)
  blocking collectives  21.8 us (16%)
  local copies, waits for them, and re-layouts  21 us (15%)
  Pallas kernels  15.5 us (11%)
    all_to_all x4, starting transfers between devices, exchange(): lax.all_to_all(value, axis, 0, 0, tiled=True, axis_index_groups=groups)  26.6 us
    all_to_all x4, waiting for transfers between devices, exchange(): lax.all_to_all(value, axis, 0, 0, tiled=True, axis_index_groups=groups)  17.2 us
    unnamed x41, local copies, waits for them, and re-layouts  16.9 us
    all_to_all x1, blocking collectives, exchange(): lax.all_to_all(value, axis, 0, 0, tiled=True, axis_index_groups=groups)  14.6 us
    ppermute x3, starting transfers between devices, shards(): lax.ppermute(terms[k], 'dom', [(i, (i + k * hop) % doms) for i in range(d...  10.6 us
    ppermute x5, starting transfers between devices, swap(): return lax.ppermute(value, 'dom', [(i, i ^ 1) for i in range(size)])  10.6 us
    all_gather x1, blocking collectives, shards(): lax.all_gather(piece, 'dom', axis_index_groups=pairs, tiled=True)[None]  7.28 us
    ppermute x1, starting transfers between devices, shards(): lax.ppermute(leaves, 'dom', [(i, (i - 1) % doms if i % 2 == 0 else (i + 1...  5.51 us
  transfers between devices with their start and end apart: 13, of which 7 were waited for; matrix products, arithmetic and copies ran while one was open for 3% of the time, Pallas kernels for 7%

profile of v4, /device:TPU:1, one launch (start us, length us, event | category | flops | bytes accessed | tf_op | source)
XLA Modules:
  0.0 137.5 jit_solution(6691451647451583634)
XLA Ops:
  0.7 1.1 copy-done.7
  1.8 0.9 copy-done.13
  2.7 1.0 shard_map.113
  3.8 11.8 %all-to-all-start = ((bf16[16,128,256]{2,1,0:T(8,128)(2,1)}), bf16[16,128,256]{2,1,0:T(8,128)(2,1)S(1)}, u32[]{:S(2)}, u32[]{:S(2)}) async-start(bf16[16,128,256]{2,1,0:T(8,128)(2,1)} %bitcast.11), calls=%async_computation | async-start | bytes 2097152 | tf_op jit(solution)/shard_map/all_to_all | solution.py:238
  16.4 0.7 fusion.1
  17.1 0.7 pad_add_fusion
  17.8 2.0 %collective-permute-start = (s32[27]{0:T(128)S(1)}, s32[27]{0:T(128)S(1)}, u32[]{:S(2)}, u32[]{:S(2)}) collective-permute-start(s32[27]{0:T(128)S(1)} %pad_add_fusion), channel_id=1, source_target_pairs={{0,1},{1,0},{2,3},{3,2},{4,5},{5,4},{6,7},{7,6},{8,9},{9,8},{10,11... | collective-permute-start | bytes 332 | tf_op jit(solution)/shard_map/ppermute | solution.py:234
  19.8 0.9 dynamic-slice_bitcast_fusion.1.own_g
  20.8 2.3 %collective-permute-start.2 = (bf16[384,256]{1,0:T(8,128)(2,1)S(1)}, bf16[384,256]{1,0:T(8,128)(2,1)}, u32[]{:S(2)}, u32[]{:S(2)}) collective-permute-start(bf16[384,256]{1,0:T(8,128)(2,1)S(1)} %dynamic-slice_bitcast_fusion.1.own_g), channel_id=1, source_target_pairs={{0,1},{1,0},{2,3},{3,2},{4,5},{5,4},{6,7},{7,6},{8,9},{9,8},{10,11... | collective-permute-start | bytes 589832 | tf_op jit(solution)/shard_map/ppermute | solution.py:234
  23.1 2.0 %collective-permute-start.3 = (bf16[12,128,128]{2,1,0:T(8,128)(2,1)S(1)}, bf16[12,128,128]{2,1,0:T(8,128)(2,1)}, u32[]{:S(2)}, u32[]{:S(2)}) collective-permute-start(bf16[12,128,128]{2,1,0:T(8,128)(2,1)S(1)} %dynamic-slice_bitcast_fusion.own_t), channel_id=1, source_target_pairs={{0,1},{1,0},{2,3},{3,2},{4,5},{5,4},{6,7},{7,6},{8,9},{9,8},{10,11... | collective-permute-start | bytes 1179656 | tf_op jit(solution)/shard_map/ppermute | solution.py:234
  25.2 0.9 dynamic-slice_bitcast_fusion.2.own_x
  26.1 2.3 %collective-permute-start.1 = (bf16[384,256]{1,0:T(8,128)(2,1)S(1)}, bf16[384,256]{1,0:T(8,128)(2,1)}, u32[]{:S(2)}, u32[]{:S(2)}) collective-permute-start(bf16[384,256]{1,0:T(8,128)(2,1)S(1)} %dynamic-slice_bitcast_fusion.2.own_x), channel_id=1, source_target_pairs={{0,1},{1,0},{2,3},{3,2},{4,5},{5,4},{6,7},{7,6},{8,9},{9,8},{10,11... | collective-permute-start | bytes 589832 | tf_op jit(solution)/shard_map/ppermute | solution.py:234
  28.6 1.0 collective-permute-done.1.got_x
  29.6 1.5 %shard_map.112 = (bf16[384,640]{1,0:T(8,128)(2,1)S(1)}, bf16[384,384]{1,0:T(8,128)(2,1)S(1)}, bf16[384,256]{1,0:T(8,128)(2,1)S(1)}, bf16[384,256]{1,0:T(8,128)(2,1)S(1)}) custom-call(s32[30]{0:T(128)S(1)} %pad_add_fusion.1.info, bf16[384,256]{1,0:T(8,128)(2,1)S(1)} %dynamic-slice_bitcast_fusion.2.own_x, bf16[384,256]{1,0:T(8,128)(2,1)} %collective-permute-done.1.got_x, ...), custom_call_target="tpu_custom_call" | custom-call | flops 1000000 | bytes 4000000 | tf_op jit(solution)/shard_map/pallas_call | solution.py:298
  31.1 0.7 copy-done.9
  31.9 0.7 copy-done.11
  32.5 0.8 copy-done.14
  34.0 9.5 %all-to-all-done.mine = bf16[16,128,256]{2,1,0:T(8,128)(2,1)S(1)} async-done(((bf16[16,128,256]{2,1,0:T(8,128)(2,1)}), bf16[16,128,256]{2,1,0:T(8,128)(2,1)S(1)}, u32[]{:S(2)}, u32[]{:S(2)}) %all-to-all-start) | async-done | bytes 1048608 | tf_op jit(solution)/shard_map/all_to_all | solution.py:238
  43.5 1.9 %collective-permute-start.4 = (bf16[16,128,256]{2,1,0:T(8,128)(2,1)S(1)}, bf16[16,128,256]{2,1,0:T(8,128)(2,1)S(1)}, u32[]{:S(2)}, u32[]{:S(2)}) collective-permute-start(bf16[16,128,256]{2,1,0:T(8,128)(2,1)S(1)} %all-to-all-done.mine), channel_id=1, source_target_pairs={{0,1},{1,0},{2,3},{3,2},{4,5},{5,4},{6,7},{7,6},{8,9},{9,8},{10,11... | collective-permute-start | bytes 3145736 | tf_op jit(solution)/shard_map/ppermute | solution.py:234
  45.5 2.6 %collective-permute-done.4.got = bf16[16,128,256]{2,1,0:T(8,128)(2,1)S(1)} collective-permute-done((bf16[16,128,256]{2,1,0:T(8,128)(2,1)S(1)}, bf16[16,128,256]{2,1,0:T(8,128)(2,1)S(1)}, u32[]{:S(2)}, u32[]{:S(2)}) %collective-permute-start.4) | collective-permute-done | bytes 1048608 | tf_op jit(solution)/shard_map/ppermute | solution.py:234
  48.1 1.4 copy-done.15
  49.4 0.9 copy-done.17
  50.4 5.4 %shard_map.114 = (bf16[8,384,256]{2,1,0:T(8,128)(2,1)S(1)}, f32[8,384,256]{2,1,0:T(8,128)S(1)}, bf16[8,128,256]{2,1,0:T(8,128)(2,1)S(1)}) custom-call(s32[30]{0:T(128)S(1)} %pad_add_fusion.1.info, f32[8]{0:T(128)S(1)} %add_log_fusion.rates, bf16[384,640]{1,0:T(8,128)(2,1)S(1)} %copy-done.15, bf16[384,256]{1,0:T(8,128)(2,1)S(1)} %copy-done.17, ...), custom_call_target="tpu_custom_call" | custom-call | flops 1400000000 | bytes 10000000 | tf_op jit(solution)/shard_map/pallas_call | solution.py:315
  55.8 1.6 %copy-done.1 = f32[8,384,256]{2,1,0:T(8,128)} copy-done((f32[8,384,256]{2,1,0:T(8,128)}, f32[8,384,256]{2,1,0:T(8,128)S(1)}, u32[]{:S(2)}) %copy-start.1) | copy-done | bytes 3145752
  57.4 1.2 copy-done.3
  58.5 0.8 copy-done.8
  59.3 3.5 %all-to-all-start.1 = ((bf16[8,128,256]{2,1,0:T(8,128)(2,1)}), bf16[8,128,256]{2,1,0:T(8,128)(2,1)S(1)}, u32[]{:S(2)}, u32[]{:S(2)}) async-start(bf16[8,128,256]{2,1,0:T(8,128)(2,1)} %copy-done.8), calls=%async_computation.1 | async-start | bytes 1048576 | tf_op jit(solution)/shard_map/all_to_all | solution.py:238
  62.9 1.9 %copy-done.2 = f32[8,384,256]{2,1,0:T(8,128)S(1)} copy-done((f32[8,384,256]{2,1,0:T(8,128)S(1)}, f32[8,384,256]{2,1,0:T(8,128)}, u32[]{:S(2)}) %copy-start.2) | copy-done | bytes 3145752
  64.7 1.4 %copy-done.4 = bf16[8,384,256]{2,1,0:T(8,128)(2,1)S(1)} copy-done((bf16[8,384,256]{2,1,0:T(8,128)(2,1)S(1)}, bf16[8,384,256]{2,1,0:T(8,128)(2,1)}, u32[]{:S(2)}) %copy-start.4) | copy-done | bytes 1572888
  66.1 1.2 copy-done.6
  67.4 0.9 copy-done.12
  68.3 5.3 %shard_map.115 = (bf16[256,256]{1,0:T(8,128)(2,1)S(1)}, bf16[256,256]{1,0:T(8,128)(2,1)S(1)}, bf16[256,256]{1,0:T(8,128)(2,1)S(1)}, bf16[256,256]{1,0:T(8,128)(2,1)S(1)}, bf16[8,48,256]{2,1,0:T(8,128)(2,1)S(1)}) custom-call(s32[30]{0:T(128)S(1)} %pad_add_fusion.1.info, f32[8]{0:T(128)S(1)} %add_log_fusion.rates, bf16[384,384]{1,0:T(8,128)(2,1)S(1)} %copy-done.10, ...), custom_call_target="tpu_custom_call" | custom-call | flops 100 | bytes 100 | tf_op jit(solution)/shard_map/pallas_call | solution.py:338
  73.6 3.1 %collective-permute-start.5 = (bf16[256,256]{1,0:T(8,128)(2,1)S(1)}, bf16[256,256]{1,0:T(8,128)(2,1)S(1)}, u32[]{:S(2)}, u32[]{:S(2)}) collective-permute-start(bf16[256,256]{1,0:T(8,128)(2,1)S(1)} %get-tuple-element.33), channel_id=1, source_target_pairs={{0,16},{1,17},{2,18},{3,19},{4,20},{5,21},{6,22},{7,23},{8,24},{9,... | collective-permute-start | bytes 393224 | tf_op jit(solution)/shard_map/ppermute | solution.py:355
  76.7 4.4 %collective-permute-start.6 = (bf16[256,256]{1,0:T(8,128)(2,1)S(1)}, bf16[256,256]{1,0:T(8,128)(2,1)S(1)}, u32[]{:S(2)}, u32[]{:S(2)}) collective-permute-start(bf16[256,256]{1,0:T(8,128)(2,1)S(1)} %get-tuple-element.34), channel_id=1, source_target_pairs={{0,32},{1,33},{2,34},{3,35},{4,36},{5,37},{6,38},{7,39},{8,40},{9,... | collective-permute-start | bytes 393224 | tf_op jit(solution)/shard_map/ppermute | solution.py:355
  81.1 3.1 %collective-permute-start.7 = (bf16[256,256]{1,0:T(8,128)(2,1)S(1)}, bf16[256,256]{1,0:T(8,128)(2,1)S(1)}, u32[]{:S(2)}, u32[]{:S(2)}) collective-permute-start(bf16[256,256]{1,0:T(8,128)(2,1)S(1)} %get-tuple-element.35), channel_id=1, source_target_pairs={{0,48},{1,49},{2,50},{3,51},{4,52},{5,53},{6,54},{7,55},{8,56},{9,... | collective-permute-start | bytes 393224 | tf_op jit(solution)/shard_map/ppermute | solution.py:355
  84.2 1.3 collective-permute-done.6.refs_2_
  85.5 1.8 %collective-permute-done.7.refs_3_ = bf16[256,256]{1,0:T(8,128)(2,1)S(1)} collective-permute-done((bf16[256,256]{1,0:T(8,128)(2,1)S(1)}, bf16[256,256]{1,0:T(8,128)(2,1)S(1)}, u32[]{:S(2)}, u32[]{:S(2)}) %collective-permute-start.7) | collective-permute-done | bytes 131104 | tf_op jit(solution)/shard_map/ppermute | solution.py:355
  87.3 0.8 shard_map.116
  88.1 6.1 %all-to-all-start.2 = ((bf16[8,80,256]{2,1,0:T(8,128)(2,1)}), bf16[8,80,256]{2,1,0:T(8,128)(2,1)S(1)}, u32[]{:S(2)}, u32[]{:S(2)}) async-start(bf16[8,80,256]{2,1,0:T(8,128)(2,1)} %shard_map.116), calls=%async_computation.2 | async-start | bytes 655360 | tf_op jit(solution)/shard_map/all_to_all | solution.py:238
  94.2 5.5 %collective-permute-start.8 = (bf16[4,128,256]{2,1,0:T(8,128)(2,1)S(1)}, bf16[4,128,256]{2,1,0:T(8,128)(2,1)S(1)}, u32[]{:S(2)}, u32[]{:S(2)}) collective-permute-start(bf16[4,128,256]{2,1,0:T(8,128)(2,1)S(1)} %get-tuple-element.40), channel_id=1, source_target_pairs={{0,63},{1,2},{2,1},{3,4},{4,3},{5,6},{6,5},{7,8},{8,7},{9,10},{10,... | collective-permute-start | bytes 786440 | tf_op jit(solution)/shard_map/ppermute | solution.py:378
  99.7 4.4 %all-to-all-done.2.arrived = bf16[8,80,256]{2,1,0:T(8,128)(2,1)S(1)} async-done(((bf16[8,80,256]{2,1,0:T(8,128)(2,1)}), bf16[8,80,256]{2,1,0:T(8,128)(2,1)S(1)}, u32[]{:S(2)}, u32[]{:S(2)}) %all-to-all-start.2) | async-done | bytes 327712 | tf_op jit(solution)/shard_map/all_to_all | solution.py:238
  104.1 14.6 %all_to_all.25 = bf16[8,32,256]{2,1,0:T(8,128)(2,1)S(1)} all-to-all(bf16[8,32,256]{2,1,0:T(8,128)(2,1)S(1)} %broadcast_in_dim.29), channel_id=1, replica_groups={{0,2,4,6,8,10,12,14},{1,3,5,7,9,11,13,15},{16,18,20,22,24,26,28,30},{17..., dimensions={0} | all-to-all | bytes 262144 | tf_op jit(solution)/shard_map/all_to_all | solution.py:238
  119.4 5.3 %all-to-all-start.4 = ((f32[4,32,256]{2,1,0:T(8,128)}), f32[4,32,256]{2,1,0:T(8,128)S(1)}, u32[]{:S(2)}, u32[]{:S(2)}) async-start(f32[4,32,256]{2,1,0:T(8,128)} %broadcast_in_dim.30), calls=%async_computation.4 | async-start | bytes 262144 | tf_op jit(solution)/shard_map/all_to_all | solution.py:238
  124.7 0.7 shard_map.119
  125.3 0.8 shard_map.118
  126.2 3.3 %all-to-all-done.4 = f32[4,32,256]{2,1,0:T(8,128)S(1)} async-done(((f32[4,32,256]{2,1,0:T(8,128)}), f32[4,32,256]{2,1,0:T(8,128)S(1)}, u32[]{:S(2)}, u32[]{:S(2)}) %all-to-all-start.4) | async-done | bytes 131104 | tf_op jit(solution)/shard_map/all_to_all | solution.py:238
  129.5 7.3 %all_gather.3 = f32[256,256]{1,0:T(8,128)S(1)} all-gather(f32[128,256]{1,0:T(8,128)S(1)} %bitcast.23), channel_id=1, replica_groups={{0,1},{2,3},{4,5},{6,7},{8,9},{10,11},{12,13},{14,15},{16,17},{18,19},{..., dimensions={0}, use_global_device_ids=true | all-gather | bytes 393216 | tf_op jit(solution)/shard_map/all_gather | solution.py:399
  136.8 0.7 copy.13
  (44 shorter events, 2.4 us)
Async XLA Ops:
  0.6 22.5 %copy-start = (bf16[4,12,128,128]{3,2,1,0:T(8,128)(2,1)S(1)}, bf16[4,12,128,128]{3,2,1,0:T(8,128)(2,1)}, u32[]{:S(2)}) copy-start(bf16[4,12,128,128]{3,2,1,0:T(8,128)(2,1)} %param.13) | copy-start | bytes 4718596
  0.7 1.2 copy-start.7
  1.8 0.9 copy-start.13
  2.7 12.9 %copy-start.19 = (s32[4,1]{0,1:T(1,128)S(1)}, s32[4,1]{0,1:T(1,128)}, u32[]{:S(2)}) copy-start(s32[4,1]{0,1:T(1,128)} %param.16) | copy-start | bytes 52
  2.7 13.5 %copy-start.18 = (s32[4,2]{0,1:T(2,128)S(1)}, s32[4,2]{0,1:T(2,128)}, u32[]{:S(2)}) copy-start(s32[4,2]{0,1:T(2,128)} %param.17) | copy-start | bytes 100
  3.8 39.8 %all-to-all-start = ((bf16[16,128,256]{2,1,0:T(8,128)(2,1)}), bf16[16,128,256]{2,1,0:T(8,128)(2,1)S(1)}, u32[]{:S(2)}, u32[]{:S(2)}) async-start(bf16[16,128,256]{2,1,0:T(8,128)(2,1)} %bitcast.11), calls=%async_computation | async-start | bytes 2097152 | tf_op jit(solution)/shard_map/all_to_all | solution.py:238
  17.8 10.7 %collective-permute-start = (s32[27]{0:T(128)S(1)}, s32[27]{0:T(128)S(1)}, u32[]{:S(2)}, u32[]{:S(2)}) collective-permute-start(s32[27]{0:T(128)S(1)} %pad_add_fusion), channel_id=1, source_target_pairs={{0,1},{1,0},{2,3},{3,2},{4,5},{5,4},{6,7},{7,6},{8,9},{9,8},{10,11... | collective-permute-start | bytes 332 | tf_op jit(solution)/shard_map/ppermute | solution.py:234
  20.8 7.8 %collective-permute-start.2 = (bf16[384,256]{1,0:T(8,128)(2,1)S(1)}, bf16[384,256]{1,0:T(8,128)(2,1)}, u32[]{:S(2)}, u32[]{:S(2)}) collective-permute-start(bf16[384,256]{1,0:T(8,128)(2,1)S(1)} %dynamic-slice_bitcast_fusion.1.own_g), channel_id=1, source_target_pairs={{0,1},{1,0},{2,3},{3,2},{4,5},{5,4},{6,7},{7,6},{8,9},{9,8},{10,11... | collective-permute-start | bytes 589832 | tf_op jit(solution)/shard_map/ppermute | solution.py:234
  23.1 6.5 %collective-permute-start.3 = (bf16[12,128,128]{2,1,0:T(8,128)(2,1)S(1)}, bf16[12,128,128]{2,1,0:T(8,128)(2,1)}, u32[]{:S(2)}, u32[]{:S(2)}) collective-permute-start(bf16[12,128,128]{2,1,0:T(8,128)(2,1)S(1)} %dynamic-slice_bitcast_fusion.own_t), channel_id=1, source_target_pairs={{0,1},{1,0},{2,3},{3,2},{4,5},{5,4},{6,7},{7,6},{8,9},{9,8},{10,11... | collective-permute-start | bytes 1179656 | tf_op jit(solution)/shard_map/ppermute | solution.py:234
  26.1 3.5 %collective-permute-start.1 = (bf16[384,256]{1,0:T(8,128)(2,1)S(1)}, bf16[384,256]{1,0:T(8,128)(2,1)}, u32[]{:S(2)}, u32[]{:S(2)}) collective-permute-start(bf16[384,256]{1,0:T(8,128)(2,1)S(1)} %dynamic-slice_bitcast_fusion.2.own_x), channel_id=1, source_target_pairs={{0,1},{1,0},{2,3},{3,2},{4,5},{5,4},{6,7},{7,6},{8,9},{9,8},{10,11... | collective-permute-start | bytes 589832 | tf_op jit(solution)/shard_map/ppermute | solution.py:234
  31.1 0.7 copy-start.9
  31.9 0.7 copy-start.11
  32.5 0.8 copy-start.14
  33.3 0.7 copy-start.16
  43.5 4.5 %collective-permute-start.4 = (bf16[16,128,256]{2,1,0:T(8,128)(2,1)S(1)}, bf16[16,128,256]{2,1,0:T(8,128)(2,1)S(1)}, u32[]{:S(2)}, u32[]{:S(2)}) collective-permute-start(bf16[16,128,256]{2,1,0:T(8,128)(2,1)S(1)} %all-to-all-done.mine), channel_id=1, source_target_pairs={{0,1},{1,0},{2,3},{3,2},{4,5},{5,4},{6,7},{7,6},{8,9},{9,8},{10,11... | collective-permute-start | bytes 3145736 | tf_op jit(solution)/shard_map/ppermute | solution.py:234
  48.1 7.7 %copy-start.5 = (bf16[16,128,256]{2,1,0:T(8,128)(2,1)}, bf16[16,128,256]{2,1,0:T(8,128)(2,1)S(1)}, u32[]{:S(2)}) copy-start(bf16[16,128,256]{2,1,0:T(8,128)(2,1)S(1)} %collective-permute-done.4.got) | copy-start | bytes 3145732
  48.1 1.4 copy-start.15
  49.4 0.9 copy-start.17
  50.4 12.5 %copy-start.10 = (bf16[384,384]{1,0:T(8,128)(2,1)S(1)}, bf16[384,384]{1,0:T(8,128)(2,1)}, u32[]{:S(2)}) copy-start(bf16[384,384]{1,0:T(8,128)(2,1)} %copy-done.9) | copy-start | bytes 884740
  55.7 1.6 %copy-start.1 = (f32[8,384,256]{2,1,0:T(8,128)}, f32[8,384,256]{2,1,0:T(8,128)S(1)}, u32[]{:S(2)}) copy-start(f32[8,384,256]{2,1,0:T(8,128)S(1)} %get-tuple-element.31.slope) | copy-start | bytes 9437188
  57.4 1.2 copy-start.3
  58.5 0.8 copy-start.8
  59.3 28.7 %all-to-all-start.1 = ((bf16[8,128,256]{2,1,0:T(8,128)(2,1)}), bf16[8,128,256]{2,1,0:T(8,128)(2,1)S(1)}, u32[]{:S(2)}, u32[]{:S(2)}) async-start(bf16[8,128,256]{2,1,0:T(8,128)(2,1)} %copy-done.8), calls=%async_computation.1 | async-start | bytes 1048576 | tf_op jit(solution)/shard_map/all_to_all | solution.py:238
  62.8 1.9 %copy-start.2 = (f32[8,384,256]{2,1,0:T(8,128)S(1)}, f32[8,384,256]{2,1,0:T(8,128)}, u32[]{:S(2)}) copy-start(f32[8,384,256]{2,1,0:T(8,128)} %copy-done.1) | copy-start | bytes 9437188
  64.7 1.4 %copy-start.4 = (bf16[8,384,256]{2,1,0:T(8,128)(2,1)S(1)}, bf16[8,384,256]{2,1,0:T(8,128)(2,1)}, u32[]{:S(2)}) copy-start(bf16[8,384,256]{2,1,0:T(8,128)(2,1)} %copy-done.3) | copy-start | bytes 4718596
  66.1 1.2 copy-start.6
  67.4 0.9 copy-start.12
  73.6 10.6 %collective-permute-start.5 = (bf16[256,256]{1,0:T(8,128)(2,1)S(1)}, bf16[256,256]{1,0:T(8,128)(2,1)S(1)}, u32[]{:S(2)}, u32[]{:S(2)}) collective-permute-start(bf16[256,256]{1,0:T(8,128)(2,1)S(1)} %get-tuple-element.33), channel_id=1, source_target_pairs={{0,16},{1,17},{2,18},{3,19},{4,20},{5,21},{6,22},{7,23},{8,24},{9,... | collective-permute-start | bytes 393224 | tf_op jit(solution)/shard_map/ppermute | solution.py:355
  76.7 8.8 %collective-permute-start.6 = (bf16[256,256]{1,0:T(8,128)(2,1)S(1)}, bf16[256,256]{1,0:T(8,128)(2,1)S(1)}, u32[]{:S(2)}, u32[]{:S(2)}) collective-permute-start(bf16[256,256]{1,0:T(8,128)(2,1)S(1)} %get-tuple-element.34), channel_id=1, source_target_pairs={{0,32},{1,33},{2,34},{3,35},{4,36},{5,37},{6,38},{7,39},{8,40},{9,... | collective-permute-start | bytes 393224 | tf_op jit(solution)/shard_map/ppermute | solution.py:355
  81.1 6.2 %collective-permute-start.7 = (bf16[256,256]{1,0:T(8,128)(2,1)S(1)}, bf16[256,256]{1,0:T(8,128)(2,1)S(1)}, u32[]{:S(2)}, u32[]{:S(2)}) collective-permute-start(bf16[256,256]{1,0:T(8,128)(2,1)S(1)} %get-tuple-element.35), channel_id=1, source_target_pairs={{0,48},{1,49},{2,50},{3,51},{4,52},{5,53},{6,54},{7,55},{8,56},{9,... | collective-permute-start | bytes 393224 | tf_op jit(solution)/shard_map/ppermute | solution.py:355
  88.1 16.0 %all-to-all-start.2 = ((bf16[8,80,256]{2,1,0:T(8,128)(2,1)}), bf16[8,80,256]{2,1,0:T(8,128)(2,1)S(1)}, u32[]{:S(2)}, u32[]{:S(2)}) async-start(bf16[8,80,256]{2,1,0:T(8,128)(2,1)} %shard_map.116), calls=%async_computation.2 | async-start | bytes 655360 | tf_op jit(solution)/shard_map/all_to_all | solution.py:238
  94.2 9.9 %collective-permute-start.8 = (bf16[4,128,256]{2,1,0:T(8,128)(2,1)S(1)}, bf16[4,128,256]{2,1,0:T(8,128)(2,1)S(1)}, u32[]{:S(2)}, u32[]{:S(2)}) collective-permute-start(bf16[4,128,256]{2,1,0:T(8,128)(2,1)S(1)} %get-tuple-element.40), channel_id=1, source_target_pairs={{0,63},{1,2},{2,1},{3,4},{4,3},{5,6},{6,5},{7,8},{8,7},{9,10},{10,... | collective-permute-start | bytes 786440 | tf_op jit(solution)/shard_map/ppermute | solution.py:378
  119.4 10.1 %all-to-all-start.4 = ((f32[4,32,256]{2,1,0:T(8,128)}), f32[4,32,256]{2,1,0:T(8,128)S(1)}, u32[]{:S(2)}, u32[]{:S(2)}) async-start(f32[4,32,256]{2,1,0:T(8,128)} %broadcast_in_dim.30), calls=%async_computation.4 | async-start | bytes 262144 | tf_op jit(solution)/shard_map/all_to_all | solution.py:238

commit v5 on v3

--- a/solution.py
+++ b/solution.py
@@ -12,6 +12,7 @@
 LAMBDA_RATE = 0.5
 CORES = 2
 CHIPS_X = 4
+LARGE = 56
 F32 = jnp.float32
 BF16 = jnp.bfloat16
 
@@ -24,33 +25,38 @@
     return pl.BlockSpec(memory_space=pltpu.SMEM)
 
 
-def call(body, out_shape, in_specs, scratch, flops, moved):
+def anywhere():
+    return pl.BlockSpec(memory_space=pl.ANY)
+
+
+def call(body, out_shape, in_specs, scratch, flops, moved, place=vmem, mib=24):
     return pl.pallas_call(
         body,
         out_shape=out_shape,
         in_specs=in_specs,
-        out_specs=jax.tree.map(lambda _: vmem(), out_shape),
+        out_specs=jax.tree.map(lambda _: place(), out_shape),
         scratch_shapes=scratch,
-        compiler_params=pltpu.CompilerParams(vmem_limit_bytes=24 * 1024 * 1024),
+        compiler_params=pltpu.CompilerParams(vmem_limit_bytes=mib * 1024 * 1024),
         cost_estimate=pl.CostEstimate(flops=flops, bytes_accessed=moved, transcendentals=0),
     )
 
 
-def slots_body(core_ref, halo, weight, out):
-    spans, _, _ = halo.shape
-    size = out.shape[1]
+def slots_body(core_ref, halo, weight, out, sems):
+    spans = halo.shape[0]
     core = core_ref[0]
-    for parity in range(CORES):
-        mine = core == parity
-        for span in range(spans):
-            for half in range(CORES):
-                slot = (parity * spans + span) * CORES + half
-                block = slice(half * size, (half + 1) * size)
-                out[slot] = jnp.where(mine, halo[span, block, :], weight[block, :])
+    copies = [pltpu.make_async_copy(halo, out.at[core], sems.at[0])]
+    for span in range(spans):
+        copies.append(
+            pltpu.make_async_copy(weight.at[0], out.at[1 - core, span], sems.at[1 + span])
+        )
+    for copy in copies:
+        copy.start()
+    for copy in copies:
+        copy.wait()
 
 
 def prepare_body(
-    tiles_max, nblocks, info, own_x, got_x, own_g, got_g, own_t, got_t, dense, flipped, x0, g0, acc
+    tiles_max, nblocks, info, own_x, got_x, own_g, got_g, own_t, got_t, job, acc
 ):
     size = acc.shape[-1]
     core = info[2 * tiles_max + 3]
@@ -69,13 +75,14 @@
     for row in range(nblocks):
         for col in range(nblocks + 2):
             block = acc[row, col]
-            dense[row * size : (row + 1) * size, col * size : (col + 1) * size] = block.astype(BF16)
+            job[row * size : (row + 1) * size, col * size : (col + 1) * size] = block.astype(BF16)
             if col < nblocks:
-                flipped[col * size : (col + 1) * size, row * size : (row + 1) * size] = (
-                    block.T.astype(BF16)
-                )
-    x0[...] = jnp.where(mine, own_x[...], got_x[...])
-    g0[...] = jnp.where(mine, own_g[...], got_g[...])
+                lane = (nblocks + 2 + row) * size
+                job[col * size : (col + 1) * size, lane : lane + size] = block.T.astype(BF16)
+    lane = (2 * nblocks + 2) * size
+    width = own_x.shape[1]
+    job[:, lane : lane + width] = jnp.where(mine, own_x[...], got_x[...])
+    job[:, lane + width : lane + 2 * width] = jnp.where(mine, own_g[...], got_g[...])
 
 
 def weight_of(core, parity, mine, got, layer):
@@ -86,75 +93,77 @@
     return jnp.concatenate([top, bottom], axis=0)
 
 
-def forward_body(
-    tiles_max, info, rates, dense, x0, mine, got, mix_out, slope_out, fresh, ext
+def chain_body(
+    tiles_max, info, rates, job, mine, got, fresh, terms, columns,
+    grad, ext, base, mixes, slopes, acc, last
 ):
-    rows = x0.shape[0]
-    size = fresh.shape[1]
+    rows, width = base.shape
+    wide = ext.shape[0]
+    dense = slice(0, wide)
+    flipped = slice(wide, wide + rows)
+    inputs = slice(wide + rows, wide + rows + width)
+    outer = slice(wide + rows + width, wide + rows + 2 * width)
+    depth, size, _ = fresh.shape
     half = mine.shape[1]
+    few = terms.shape[1] // depth
     core = info[2 * tiles_max + 3]
     parity = info[2 * tiles_max + 4]
     send = jnp.where(core == 0, info[2 * tiles_max + 1], info[2 * tiles_max + 2])
-    ext[0:rows, :] = x0[...]
-
-    def step(layer, carry):
+    ext[0:rows, :] = job[:, inputs]
+    base[...] = ALPHA * job[:, inputs].astype(F32)
+    grad[...] = job[:, outer]
+    acc[...] = jnp.zeros_like(acc)
+
+    def forward(layer, carry):
         rate = rates[layer]
         start = pl.multiple_of(send * size, size)
         fresh[layer] = ext[pl.ds(start, size), :]
         ext[rows : rows + half, :] = mine[CORES * layer + parity]
         ext[rows + half : rows + 2 * half, :] = got[CORES * layer + parity]
-        agg = jnp.dot(dense[...], ext[...], preferred_element_type=F32)
-        mix = ((1.0 - ALPHA) * agg + ALPHA * x0[...].astype(F32)).astype(BF16)
-        mix_out[layer] = mix
+        agg = jnp.dot(job[:, dense], ext[...], preferred_element_type=F32)
+        mix = ((1.0 - ALPHA) * agg + base[...]).astype(BF16)
+        mixes[layer] = mix
         weight = weight_of(core, parity, mine, got, layer)
         pre = (1.0 - rate) * mix.astype(F32) + rate * jnp.dot(
             mix, weight, preferred_element_type=F32
         )
-        gate = jax.nn.sigmoid(pre)
-        slope_out[layer] = gate * (1.0 + pre * (1.0 - gate))
-        ext[0:rows, :] = (pre * gate).astype(BF16)
+        gate = 0.5 * jnp.tanh(0.5 * pre) + 0.5
+        silu = pre * gate
+        slopes[layer] = gate + silu * (1.0 - gate)
+        ext[0:rows, :] = silu.astype(BF16)
         return carry
 
-    lax.fori_loop(0, fresh.shape[0], step, 0)
-
-
-def backward_body(
-    tiles_max, info, rates, flipped, g0, mine, got, mix, slope, terms, columns, grad, acc, last
-):
-    depth, _, width = columns.shape
-    parts = terms.shape[0]
-    few = terms.shape[1] // depth
-    half = parts * few
-    core = info[2 * tiles_max + 3]
-    parity = info[2 * tiles_max + 4]
-    grad[...] = g0[...]
-    acc[...] = jnp.zeros_like(acc)
-
-    def step(index, carry):
+    lax.fori_loop(0, depth, forward, 0)
+
+    def backward(index, carry):
         layer = depth - 1 - index
         rate = rates[layer]
-        delta = (grad[...].astype(F32) * slope[layer]).astype(BF16)
+        delta = (grad[...].astype(F32) * slopes[layer]).astype(BF16)
         start = pl.multiple_of(core * half, half)
-        part = mix[layer, :, pl.ds(start, half)]
+        part = mixes[layer, :, pl.ds(start, half)]
+        weight = weight_of(core, parity, mine, got, layer)
+        dmix = (1.0 - rate) * delta.astype(F32) + rate * lax.dot_general(
+            delta, weight, (((1,), (1,)), ((), ())), preferred_element_type=F32
+        )
+        acc[...] += dmix
+        back = jnp.dot(job[:, flipped], dmix.astype(BF16), preferred_element_type=F32)
+        gx = (1.0 - ALPHA) * back
+        grad[...] = gx.astype(BF16)
         dweight = lax.dot_general(
             part, delta, (((0,), (0,)), ((), ())), preferred_element_type=F32
         ).astype(BF16)
         row = pl.multiple_of(layer * few, few)
-        for piece in range(parts):
+        for piece in range(CHIPS_X):
             terms[piece, pl.ds(row, few), :] = dweight[piece * few : (piece + 1) * few]
-        weight = weight_of(core, parity, mine, got, layer)
-        dmix = (1.0 - rate) * delta.astype(F32) + rate * lax.dot_general(
-            delta, weight, (((1,), (1,)), ((), ())), preferred_element_type=F32
-        )
-        acc[...] += ALPHA * dmix
-        back = jnp.dot(flipped[...], dmix.astype(BF16), preferred_element_type=F32)
-        gx = (1.0 - ALPHA) * back
-        last[...] = gx
-        grad[...] = gx.astype(BF16)
+
+        @pl.when(layer == 0)
+        def _():
+            last[...] = gx
+
         return carry
 
-    lax.fori_loop(0, depth, step, 0)
-    dinput = (acc[...] + last[...]).T.astype(BF16)
+    lax.fori_loop(0, depth, backward, 0)
+    dinput = (ALPHA * acc[...] + last[...]).T.astype(BF16)
     share = width // depth
     hop = share // 2
     for part in range(depth):
@@ -201,6 +210,14 @@
         own, other = stays[span], comes[span]
         out[0, span, :size, :] = jnp.where(first, other, own)
         out[0, span, size:, :] = jnp.where(first, own, other)
+
+
+def assemble_body(spread, out):
+    peers, few, _ = spread.shape
+    for core in range(CORES):
+        for chip in range(peers // CORES):
+            row = (core * (peers // CORES) + chip) * few
+            out[0, row : row + few, :] = spread[CORES * chip + core].astype(F32)
 
 
 def swap(value):
@@ -238,12 +255,18 @@
 
     slots = call(
         slots_body,
-        jax.ShapeDtypeStruct((depth * CORES, size, width), BF16),
-        [smem(), vmem(), vmem()],
-        [],
+        jax.ShapeDtypeStruct((CORES, spans, CORES, size, width), BF16),
+        [smem(), anywhere(), anywhere()],
+        [pltpu.SemaphoreType.DMA((1 + spans,))],
         10**5,
         10**6,
-    )(core.astype(jnp.int32)[None], stale_halo[0], layer_weights[0])
+        anywhere,
+        LARGE,
+    )(
+        core.astype(jnp.int32)[None],
+        stale_halo.reshape(spans, CORES, size, width),
+        layer_weights.reshape(1, CORES, half, width),
+    ).reshape(depth * CORES, size, width)
     column = [
         [z * doms + CORES * i + j for z in range(depth) for j in range(CORES)] for i in range(chips)
     ]
@@ -261,53 +284,41 @@
     info = jnp.concatenate(
         [info, core.astype(jnp.int32)[None], parity.astype(jnp.int32)[None]]
     )
-    dense, flipped, x0, g0 = call(
+    wide = rows + 2 * size
+    job = call(
         functools.partial(prepare_body, tiles_max, nblocks),
-        (
-            jax.ShapeDtypeStruct((rows, rows + 2 * size), BF16),
-            jax.ShapeDtypeStruct((rows, rows), BF16),
-            jax.ShapeDtypeStruct((rows, width), BF16),
-            jax.ShapeDtypeStruct((rows, width), BF16),
-        ),
+        jax.ShapeDtypeStruct((rows, wide + rows + 2 * width), BF16),
         [smem()] + [vmem()] * 6,
         [pltpu.VMEM((nblocks, nblocks + 2, size, size), F32)],
         10**6,
         4 * 10**6,
     )(info, own_x, swap(own_x), own_g, swap(own_g), own_t, swap(own_t))
 
-    mine, dense = lax.optimization_barrier((mine, dense))
+    mine, job = lax.optimization_barrier((mine, job))
     got = swap(mine)
-
-    mix, slope, fresh_out = call(
-        functools.partial(forward_body, tiles_max),
-        (
-            jax.ShapeDtypeStruct((depth, rows, width), BF16),
-            jax.ShapeDtypeStruct((depth, rows, width), F32),
-            jax.ShapeDtypeStruct((depth, size, width), BF16),
-        ),
-        [smem()] * 2 + [vmem()] * 4,
-        [pltpu.VMEM((rows + 2 * size, width), BF16)],
-        1400 * 10**6,
-        10**7,
-    )(info, rates, dense, x0, mine, got)
 
     few = half // CHIPS_X
     spare = width // depth + width // depth // 2
-    terms, columns = call(
-        functools.partial(backward_body, tiles_max),
+    fresh_out, terms, columns = call(
+        functools.partial(chain_body, tiles_max),
         (
+            jax.ShapeDtypeStruct((depth, size, width), BF16),
             jax.ShapeDtypeStruct((CHIPS_X, depth * few, width), BF16),
             jax.ShapeDtypeStruct((depth, spare, width), BF16),
         ),
-        [smem()] * 2 + [vmem()] * 6,
+        [smem()] * 2 + [vmem()] * 3,
         [
             pltpu.VMEM((rows, width), BF16),
+            pltpu.VMEM((wide, width), BF16),
+            pltpu.VMEM((rows, width), F32),
+            pltpu.VMEM((depth, rows, width), BF16),
+            pltpu.VMEM((depth, rows, width), F32),
             pltpu.VMEM((rows, width), F32),
             pltpu.VMEM((rows, width), F32),
         ],
-        1400 * 10**6,
+        2800 * 10**6,
         10**7,
-    )(info, rates, flipped, g0, mine, got, mix, slope)
+    )(info, rates, job, mine, got)
 
     chips_y = chips // CHIPS_X
     along_x = [
@@ -320,7 +331,10 @@
         for x in range(CHIPS_X)
         for j in range(CORES)
     ]
-    pairs = [[CORES * i + j for j in range(CORES)] for i in range(chips)]
+    plane = [
+        [(x * chips_y + y) * CORES + j for x in range(CHIPS_X) for j in range(CORES)]
+        for y in range(chips_y)
+    ]
     pieces = exchange(terms, "dom", along_x)
     parcel = call(
         merge_body,
@@ -337,9 +351,17 @@
     copies = jnp.broadcast_to(piece[None], (chips_y,) + piece.shape)
     copies, arrived = lax.optimization_barrier((copies, arrived))
     piece = exchange(copies, "dom", along_y).astype(F32).sum(axis=0) * scale
-    copies = jnp.broadcast_to(piece[None], (CHIPS_X,) + piece.shape)
-    piece = exchange(copies, "dom", along_x).reshape(half, width)
-    weight_grad = lax.all_gather(piece, "dom", axis_index_groups=pairs, tiled=True)[None]
+    piece = piece.astype(BF16)
+    copies = jnp.broadcast_to(piece[None], (CHIPS_X * CORES,) + piece.shape)
+    spread = exchange(copies, "dom", plane)
+    weight_grad = call(
+        assemble_body,
+        jax.ShapeDtypeStruct((1, width, width), F32),
+        [vmem()],
+        [],
+        100,
+        100,
+    )(spread)
 
     initial_grad, stays, leaves = call(
         functools.partial(unpack_body, size),

time: 131 us -> 157 us (1.20)
  Pallas kernels: 14 us -> 46.5 us
  blocking collectives: 44.5 us -> 37.3 us
  starting transfers between devices: 40.3 us -> 44.7 us
  local copies, waits for them, and re-layouts: 12.3 us -> 9.7 us
    pallas_call x4, Pallas kernels: 12.4 us -> 44.8 us  [the longest x1 32.9 us: shards(): call(slots_body, jax.ShapeDtypeStruct((CORES, spans, CORES, size, width),...]
    all_gather x1 -> x0, blocking collectives: 7.69 us -> none  [shards(): lax.all_gather(piece, 'dom', axis_index_groups=pairs, tiled=True)[None]]
    all_to_all x3, starting transfers between devices: 22.1 us -> 26.4 us  [exchange(): lax.all_to_all(value, axis, 0, 0, tiled=True, axis_index_groups=groups)]
    unnamed x27 -> x18, local copies, waits for them, and re-layouts: 7.57 us -> 4.97 us
  transfers between devices with their start and end apart: 9 -> 9, of which waited for: 5 -> 4; matrix products, arithmetic and copies ran while one was open for 4% -> 3% of each run, Pallas kernels for 2% -> 2%
where the time goes in v5:
time: 157 us
  Pallas kernels  46.5 us (30%)
  starting transfers between devices  44.7 us (28%)
  blocking collectives  37.3 us (24%)
  waiting for transfers between devices  16.6 us (11%)
  local copies, waits for them, and re-layouts  9.7 us (6%)
    all_to_all x2, blocking collectives, exchange(): lax.all_to_all(value, axis, 0, 0, tiled=True, axis_index_groups=groups)  37.3 us
    pallas_call x1, Pallas kernels, shards(): call(slots_body, jax.ShapeDtypeStruct((CORES, spans, CORES, size, width),...  32.9 us
    all_to_all x3, starting transfers between devices, exchange(): lax.all_to_all(value, axis, 0, 0, tiled=True, axis_index_groups=groups)  26.4 us
    all_to_all x3, waiting for transfers between devices, exchange(): lax.all_to_all(value, axis, 0, 0, tiled=True, axis_index_groups=groups)  13.4 us
    ppermute x5, starting transfers between devices, swap(): return lax.ppermute(value, 'dom', [(i, i ^ 1) for i in range(size)])  10.6 us
    pallas_call x1, Pallas kernels, shards(): call(functools.partial(chain_body, tiles_max), (jax.ShapeDtypeStruct((dep...  10.4 us
    ppermute x1, starting transfers between devices, shards(): lax.ppermute(leaves, 'dom', [(i, (i - 1) % doms if i % 2 == 0 else (i + 1...  7.71 us
    unnamed x18, local copies, waits for them, and re-layouts  4.97 us
  transfers between devices with their start and end apart: 9, of which 4 were waited for; matrix products, arithmetic and copies ran while one was open for 3% of the time, Pallas kernels for 2%

profile of v5, /device:TPU:1, one launch (start us, length us, event | category | flops | bytes accessed | tf_op | source)
XLA Modules:
  0.0 156.5 jit_solution(7267343306347463469)
XLA Ops:
  0.6 0.0 copy-start
  0.7 0.0 copy-start.8
  0.7 0.0 copy-start.7
  0.7 32.9 %shard_map.112 = bf16[2,4,2,128,256]{4,3,2,1,0:T(8,128)(2,1)} custom-call(s32[1]{0:T(128)} %bitcast.3.core_ref, bf16[4,2,128,256]{3,2,1,0:T(8,128)(2,1)} %bitcast.18, bf16[1,2,128,256]{3,2,1,0:T(8,128)(2,1)} %bitcast.19), custom_call_target="tpu_custom_call" | custom-call | flops 100000 | bytes 1000000 | tf_op jit(solution)/shard_map/pallas_call | solution.py:256
  33.6 11.8 %all-to-all-start = ((bf16[16,128,256]{2,1,0:T(8,128)(2,1)}), bf16[16,128,256]{2,1,0:T(8,128)(2,1)}, u32[]{:S(2)}, u32[]{:S(2)}) async-start(bf16[16,128,256]{2,1,0:T(8,128)(2,1)} %bitcast.17), calls=%async_computation | async-start | bytes 2097152 | tf_op jit(solution)/shard_map/all_to_all | solution.py:229
  45.4 0.0 copy-done.8
  45.4 0.6 constant_dynamic-slice_fusion.1
  46.0 0.0 copy-done.7
  46.0 0.2 fusion
  46.2 0.7 fusion.1
  46.9 0.7 pad_add_fusion
  47.6 2.1 %collective-permute-start = (s32[27]{0:T(128)S(1)}, s32[27]{0:T(128)S(1)}, u32[]{:S(2)}, u32[]{:S(2)}) collective-permute-start(s32[27]{0:T(128)S(1)} %pad_add_fusion), channel_id=1, source_target_pairs={{0,1},{1,0},{2,3},{3,2},{4,5},{5,4},{6,7},{7,6},{8,9},{9,8},{10,11... | collective-permute-start | bytes 332 | tf_op jit(solution)/shard_map/ppermute | solution.py:225
  49.7 0.9 dynamic-slice_bitcast_fusion.1.own_g
  50.7 2.2 %collective-permute-start.2 = (bf16[384,256]{1,0:T(8,128)(2,1)S(1)}, bf16[384,256]{1,0:T(8,128)(2,1)S(1)}, u32[]{:S(2)}, u32[]{:S(2)}) collective-permute-start(bf16[384,256]{1,0:T(8,128)(2,1)S(1)} %dynamic-slice_bitcast_fusion.1.own_g), channel_id=1, source_target_pairs={{0,1},{1,0},{2,3},{3,2},{4,5},{5,4},{6,7},{7,6},{8,9},{9,8},{10,11... | collective-permute-start | bytes 589832 | tf_op jit(solution)/shard_map/ppermute | solution.py:225
  52.9 0.0 copy-done
  53.0 2.1 %collective-permute-start.3 = (bf16[12,128,128]{2,1,0:T(8,128)(2,1)S(1)}, bf16[12,128,128]{2,1,0:T(8,128)(2,1)S(1)}, u32[]{:S(2)}, u32[]{:S(2)}) collective-permute-start(bf16[12,128,128]{2,1,0:T(8,128)(2,1)S(1)} %dynamic-slice_bitcast_fusion.own_t), channel_id=1, source_target_pairs={{0,1},{1,0},{2,3},{3,2},{4,5},{5,4},{6,7},{7,6},{8,9},{9,8},{10,11... | collective-permute-start | bytes 1179656 | tf_op jit(solution)/shard_map/ppermute | solution.py:225
  55.1 0.9 dynamic-slice_bitcast_fusion.2.own_x
  56.0 2.2 %collective-permute-start.1 = (bf16[384,256]{1,0:T(8,128)(2,1)S(1)}, bf16[384,256]{1,0:T(8,128)(2,1)S(1)}, u32[]{:S(2)}, u32[]{:S(2)}) collective-permute-start(bf16[384,256]{1,0:T(8,128)(2,1)S(1)} %dynamic-slice_bitcast_fusion.2.own_x), channel_id=1, source_target_pairs={{0,1},{1,0},{2,3},{3,2},{4,5},{5,4},{6,7},{7,6},{8,9},{9,8},{10,11... | collective-permute-start | bytes 589832 | tf_op jit(solution)/shard_map/ppermute | solution.py:225
  58.3 0.0 collective-permute-done
  58.3 0.1 pad_add_fusion.1.info
  58.4 0.0 collective-permute-done.2.got_g
  58.4 0.7 copy-done.3
  59.1 0.3 collective-permute-done.1.got_x
  59.4 0.7 copy-done.5
  60.0 0.0 collective-permute-done.3.got_t
  60.0 0.7 copy-done.1
  60.8 1.0 copy-done.2
  61.8 0.9 copy-done.4
  62.7 0.9 copy-done.6
  63.6 0.9 shard_map.113.job
  64.5 9.0 %all-to-all-done.mine = bf16[16,128,256]{2,1,0:T(8,128)(2,1)} async-done(((bf16[16,128,256]{2,1,0:T(8,128)(2,1)}), bf16[16,128,256]{2,1,0:T(8,128)(2,1)}, u32[]{:S(2)}, u32[]{:S(2)}) %all-to-all-start) | async-done | bytes 1048608 | tf_op jit(solution)/shard_map/all_to_all | solution.py:229
  73.5 1.9 %collective-permute-start.4 = (bf16[16,128,256]{2,1,0:T(8,128)(2,1)}, bf16[16,128,256]{2,1,0:T(8,128)(2,1)S(1)}, u32[]{:S(2)}, u32[]{:S(2)}) collective-permute-start(bf16[16,128,256]{2,1,0:T(8,128)(2,1)} %all-to-all-done.mine), channel_id=1, source_target_pairs={{0,1},{1,0},{2,3},{3,2},{4,5},{5,4},{6,7},{7,6},{8,9},{9,8},{10,11... | collective-permute-start | bytes 3145736 | tf_op jit(solution)/shard_map/ppermute | solution.py:225
  75.4 2.8 %collective-permute-done.4.got = bf16[16,128,256]{2,1,0:T(8,128)(2,1)S(1)} collective-permute-done((bf16[16,128,256]{2,1,0:T(8,128)(2,1)}, bf16[16,128,256]{2,1,0:T(8,128)(2,1)S(1)}, u32[]{:S(2)}, u32[]{:S(2)}) %collective-permute-start.4) | collective-permute-done | bytes 1048608 | tf_op jit(solution)/shard_map/ppermute | solution.py:225
  78.2 10.4 %shard_map.114 = (bf16[8,128,256]{2,1,0:T(8,128)(2,1)S(1)}, bf16[4,256,256]{2,1,0:T(8,128)(2,1)S(1)}, bf16[8,48,256]{2,1,0:T(8,128)(2,1)S(1)}) custom-call(s32[29]{0:T(128)S(1)} %pad_add_fusion.1.info, f32[8]{0:T(128)S(1)} %add_log_fusion.rates, bf16[384,1536]{1,0:T(8,128)(2,1)S(1)} %shard_map.113.job, bf16[16,128,256]{2,1,0:T(8,128)(2,1)} %all-to-all-done.mine, ...), custom_call_target="tpu_custom_call" | custom-call | flops 2800000000 | bytes 10000000 | tf_op jit(solution)/shard_map/pallas_call | solution.py:302
  88.6 13.0 %all_to_all.25.pieces = bf16[4,256,256]{2,1,0:T(8,128)(2,1)S(1)} all-to-all(bf16[4,256,256]{2,1,0:T(8,128)(2,1)S(1)} %get-tuple-element.15), channel_id=1, replica_groups={{0,16,32,48},{1,17,33,49},{2,18,34,50},{3,19,35,51},{4,20,36,52},{5,21,..., dimensions={0} | all-to-all | bytes 1048576 | tf_op jit(solution)/shard_map/all_to_all | solution.py:229
  101.6 0.1 shard_map.115
  101.7 24.4 %all_to_all.26.arrived = bf16[8,208,256]{2,1,0:T(8,128)(2,1)S(1)} all-to-all(bf16[8,208,256]{2,1,0:T(8,128)(2,1)S(1)} %shard_map.115), channel_id=1, replica_groups=mesh['section'=8,'dom'=64] {'section'}, dimensions={0} | all-to-all | bytes 1703936 | tf_op jit(solution)/shard_map/all_to_all | solution.py:229
  126.1 0.7 broadcast_in_dim.10
  126.7 6.4 %all-to-all-start.3 = ((bf16[8,32,256]{2,1,0:T(8,128)(2,1)}), bf16[8,32,256]{2,1,0:T(8,128)(2,1)S(1)}, u32[]{:S(2)}, u32[]{:S(2)}) async-start(bf16[8,32,256]{2,1,0:T(8,128)(2,1)} %broadcast_in_dim.10), calls=%async_computation.3 | async-start | bytes 262144 | tf_op jit(solution)/shard_map/all_to_all | solution.py:229
  133.1 0.7 shard_map.117
  133.9 7.7 %collective-permute-start.5 = (bf16[4,128,256]{2,1,0:T(8,128)(2,1)S(1)}, bf16[4,128,256]{2,1,0:T(8,128)(2,1)S(1)}, u32[]{:S(2)}, u32[]{:S(2)}) collective-permute-start(bf16[4,128,256]{2,1,0:T(8,128)(2,1)S(1)} %get-tuple-element.21), channel_id=1, source_target_pairs={{0,63},{1,2},{2,1},{3,4},{4,3},{5,6},{6,5},{7,8},{8,7},{9,10},{10,... | collective-permute-start | bytes 786440 | tf_op jit(solution)/shard_map/ppermute | solution.py:378
  141.6 0.0 all-to-all-done.3
  141.6 0.7 broadcast_in_dim.11
  142.3 8.2 %all-to-all-start.4 = ((bf16[8,32,256]{2,1,0:T(8,128)(2,1)}), bf16[8,32,256]{2,1,0:T(8,128)(2,1)S(1)}, u32[]{:S(2)}, u32[]{:S(2)}) async-start(bf16[8,32,256]{2,1,0:T(8,128)(2,1)} %broadcast_in_dim.11), calls=%async_computation.4 | async-start | bytes 262144 | tf_op jit(solution)/shard_map/all_to_all | solution.py:229
  150.5 0.0 collective-permute-done.5.comes
  150.5 0.8 shard_map.118
  151.3 4.5 %all-to-all-done.4.spread = bf16[8,32,256]{2,1,0:T(8,128)(2,1)S(1)} async-done(((bf16[8,32,256]{2,1,0:T(8,128)(2,1)}), bf16[8,32,256]{2,1,0:T(8,128)(2,1)S(1)}, u32[]{:S(2)}, u32[]{:S(2)}) %all-to-all-start.4) | async-done | bytes 131104 | tf_op jit(solution)/shard_map/all_to_all | solution.py:229
  155.8 0.7 shard_map.116
  (12 shorter events, 0.1 us)
Async XLA Ops:
  0.6 52.3 %copy-start = (bf16[4,12,128,128]{3,2,1,0:T(8,128)(2,1)S(1)}, bf16[4,12,128,128]{3,2,1,0:T(8,128)(2,1)}, u32[]{:S(2)}) copy-start(bf16[4,12,128,128]{3,2,1,0:T(8,128)(2,1)} %param.13) | copy-start | bytes 4718596
  0.7 44.8 %copy-start.8 = (s32[4,1]{0,1:T(1,128)S(1)}, s32[4,1]{0,1:T(1,128)}, u32[]{:S(2)}) copy-start(s32[4,1]{0,1:T(1,128)} %param.16) | copy-start | bytes 52
  0.7 45.4 %copy-start.7 = (s32[4,2]{0,1:T(2,128)S(1)}, s32[4,2]{0,1:T(2,128)}, u32[]{:S(2)}) copy-start(s32[4,2]{0,1:T(2,128)} %param.17) | copy-start | bytes 100
  33.6 39.9 %all-to-all-start = ((bf16[16,128,256]{2,1,0:T(8,128)(2,1)}), bf16[16,128,256]{2,1,0:T(8,128)(2,1)}, u32[]{:S(2)}, u32[]{:S(2)}) async-start(bf16[16,128,256]{2,1,0:T(8,128)(2,1)} %bitcast.17), calls=%async_computation | async-start | bytes 2097152 | tf_op jit(solution)/shard_map/all_to_all | solution.py:229
  47.6 10.6 %collective-permute-start = (s32[27]{0:T(128)S(1)}, s32[27]{0:T(128)S(1)}, u32[]{:S(2)}, u32[]{:S(2)}) collective-permute-start(s32[27]{0:T(128)S(1)} %pad_add_fusion), channel_id=1, source_target_pairs={{0,1},{1,0},{2,3},{3,2},{4,5},{5,4},{6,7},{7,6},{8,9},{9,8},{10,11... | collective-permute-start | bytes 332 | tf_op jit(solution)/shard_map/ppermute | solution.py:225
  50.7 7.7 %collective-permute-start.2 = (bf16[384,256]{1,0:T(8,128)(2,1)S(1)}, bf16[384,256]{1,0:T(8,128)(2,1)S(1)}, u32[]{:S(2)}, u32[]{:S(2)}) collective-permute-start(bf16[384,256]{1,0:T(8,128)(2,1)S(1)} %dynamic-slice_bitcast_fusion.1.own_g), channel_id=1, source_target_pairs={{0,1},{1,0},{2,3},{3,2},{4,5},{5,4},{6,7},{7,6},{8,9},{9,8},{10,11... | collective-permute-start | bytes 589832 | tf_op jit(solution)/shard_map/ppermute | solution.py:225
  53.0 7.1 %collective-permute-start.3 = (bf16[12,128,128]{2,1,0:T(8,128)(2,1)S(1)}, bf16[12,128,128]{2,1,0:T(8,128)(2,1)S(1)}, u32[]{:S(2)}, u32[]{:S(2)}) collective-permute-start(bf16[12,128,128]{2,1,0:T(8,128)(2,1)S(1)} %dynamic-slice_bitcast_fusion.own_t), channel_id=1, source_target_pairs={{0,1},{1,0},{2,3},{3,2},{4,5},{5,4},{6,7},{7,6},{8,9},{9,8},{10,11... | collective-permute-start | bytes 1179656 | tf_op jit(solution)/shard_map/ppermute | solution.py:225
  56.0 3.3 %collective-permute-start.1 = (bf16[384,256]{1,0:T(8,128)(2,1)S(1)}, bf16[384,256]{1,0:T(8,128)(2,1)S(1)}, u32[]{:S(2)}, u32[]{:S(2)}) collective-permute-start(bf16[384,256]{1,0:T(8,128)(2,1)S(1)} %dynamic-slice_bitcast_fusion.2.own_x), channel_id=1, source_target_pairs={{0,1},{1,0},{2,3},{3,2},{4,5},{5,4},{6,7},{7,6},{8,9},{9,8},{10,11... | collective-permute-start | bytes 589832 | tf_op jit(solution)/shard_map/ppermute | solution.py:225
  58.4 0.7 copy-start.3
  59.4 0.7 copy-start.5
  60.0 0.7 copy-start.1
  60.8 1.0 copy-start.2
  61.8 0.9 copy-start.4
  62.7 0.9 copy-start.6
  73.5 4.8 %collective-permute-start.4 = (bf16[16,128,256]{2,1,0:T(8,128)(2,1)}, bf16[16,128,256]{2,1,0:T(8,128)(2,1)S(1)}, u32[]{:S(2)}, u32[]{:S(2)}) collective-permute-start(bf16[16,128,256]{2,1,0:T(8,128)(2,1)} %all-to-all-done.mine), channel_id=1, source_target_pairs={{0,1},{1,0},{2,3},{3,2},{4,5},{5,4},{6,7},{7,6},{8,9},{9,8},{10,11... | collective-permute-start | bytes 3145736 | tf_op jit(solution)/shard_map/ppermute | solution.py:225
  126.7 14.8 %all-to-all-start.3 = ((bf16[8,32,256]{2,1,0:T(8,128)(2,1)}), bf16[8,32,256]{2,1,0:T(8,128)(2,1)S(1)}, u32[]{:S(2)}, u32[]{:S(2)}) async-start(bf16[8,32,256]{2,1,0:T(8,128)(2,1)} %broadcast_in_dim.10), calls=%async_computation.3 | async-start | bytes 262144 | tf_op jit(solution)/shard_map/all_to_all | solution.py:229
  133.9 16.6 %collective-permute-start.5 = (bf16[4,128,256]{2,1,0:T(8,128)(2,1)S(1)}, bf16[4,128,256]{2,1,0:T(8,128)(2,1)S(1)}, u32[]{:S(2)}, u32[]{:S(2)}) collective-permute-start(bf16[4,128,256]{2,1,0:T(8,128)(2,1)S(1)} %get-tuple-element.21), channel_id=1, source_target_pairs={{0,63},{1,2},{2,1},{3,4},{4,3},{5,6},{6,5},{7,8},{8,7},{9,10},{10,... | collective-permute-start | bytes 786440 | tf_op jit(solution)/shard_map/ppermute | solution.py:378
  142.3 13.5 %all-to-all-start.4 = ((bf16[8,32,256]{2,1,0:T(8,128)(2,1)}), bf16[8,32,256]{2,1,0:T(8,128)(2,1)S(1)}, u32[]{:S(2)}, u32[]{:S(2)}) async-start(bf16[8,32,256]{2,1,0:T(8,128)(2,1)} %broadcast_in_dim.11), calls=%async_computation.4 | async-start | bytes 262144 | tf_op jit(solution)/shard_map/all_to_all | solution.py:229

commit v6 on v5

--- a/solution.py
+++ b/solution.py
@@ -41,16 +41,22 @@
     )
 
 
-def slots_body(core_ref, halo, weight, out, sems):
+def slots_body(core_ref, halo_far, weight_far, out, halo, weight, fetched, sent):
     spans = halo.shape[0]
     core = core_ref[0]
-    copies = [pltpu.make_async_copy(halo, out.at[core], sems.at[0])]
-    for span in range(spans):
-        copies.append(
-            pltpu.make_async_copy(weight.at[0], out.at[1 - core, span], sems.at[1 + span])
-        )
-    for copy in copies:
+    weight_in = pltpu.make_async_copy(weight_far, weight, fetched.at[0])
+    halo_in = pltpu.make_async_copy(halo_far, halo, fetched.at[1])
+    weight_in.start()
+    halo_in.start()
+    copies = [
+        pltpu.make_async_copy(weight, out.at[1 - core, span], sent.at[1 + span])
+        for span in range(spans)
+    ] + [pltpu.make_async_copy(halo, out.at[core], sent.at[0])]
+    weight_in.wait()
+    for copy in copies[:-1]:
         copy.start()
+    halo_in.wait()
+    copies[-1].start()
     for copy in copies:
         copy.wait()
 
@@ -257,7 +263,12 @@
         slots_body,
         jax.ShapeDtypeStruct((CORES, spans, CORES, size, width), BF16),
         [smem(), anywhere(), anywhere()],
-        [pltpu.SemaphoreType.DMA((1 + spans,))],
+        [
+            pltpu.VMEM((spans, CORES, size, width), BF16),
+            pltpu.VMEM((CORES, half, width), BF16),
+            pltpu.SemaphoreType.DMA((2,)),
+            pltpu.SemaphoreType.DMA((1 + spans,)),
+        ],
         10**5,
         10**6,
         anywhere,
@@ -265,7 +276,7 @@
     )(
         core.astype(jnp.int32)[None],
         stale_halo.reshape(spans, CORES, size, width),
-        layer_weights.reshape(1, CORES, half, width),
+        layer_weights.reshape(CORES, half, width),
     ).reshape(depth * CORES, size, width)
     column = [
         [z * doms + CORES * i + j for z in range(depth) for j in range(CORES)] for i in range(chips)

time: 157 us -> 127 us (0.81)
  Pallas kernels: 46.5 us -> 15.7 us
    pallas_call x1, Pallas kernels: 32.9 us -> 2.09 us  [shards(): call(slots_body, jax.ShapeDtypeStruct((CORES, spans, CORES, size, width),...]
  transfers between devices with their start and end apart: 9 -> 9, of which waited for: 4 -> 4; matrix products, arithmetic and copies ran while one was open for 3% -> 4% of each run, Pallas kernels for 2% -> 2%
where the time goes in v6:
time: 127 us; the launch traced here: 126 us
  starting transfers between devices  44.7 us (35%)
  blocking collectives  37.3 us (29%)
  waiting for transfers between devices  16.6 us (13%)
  Pallas kernels  15.7 us (12%)
  local copies, waits for them, and re-layouts  9.7 us (8%)
    all_to_all x2, blocking collectives, exchange(): lax.all_to_all(value, axis, 0, 0, tiled=True, axis_index_groups=groups)  37.3 us
    all_to_all x3, starting transfers between devices, exchange(): lax.all_to_all(value, axis, 0, 0, tiled=True, axis_index_groups=groups)  26.5 us
    all_to_all x3, waiting for transfers between devices, exchange(): lax.all_to_all(value, axis, 0, 0, tiled=True, axis_index_groups=groups)  13.4 us
    ppermute x5, starting transfers between devices, swap(): return lax.ppermute(value, 'dom', [(i, i ^ 1) for i in range(size)])  10.6 us
    pallas_call x1, Pallas kernels, shards(): call(functools.partial(chain_body, tiles_max), (jax.ShapeDtypeStruct((dep...  10.4 us
    ppermute x1, starting transfers between devices, shards(): lax.ppermute(leaves, 'dom', [(i, (i - 1) % doms if i % 2 == 0 else (i + 1...  7.71 us
    unnamed x18, local copies, waits for them, and re-layouts  4.97 us
    ppermute x5, waiting for transfers between devices, swap(): return lax.ppermute(value, 'dom', [(i, i ^ 1) for i in range(size)])  3.11 us
  transfers between devices with their start and end apart: 9, of which 4 were waited for; matrix products, arithmetic and copies ran while one was open for 4% of the time, Pallas kernels for 2%

profile of v6, /device:TPU:1, one launch (start us, length us, event | category | flops | bytes accessed | tf_op | source)
XLA Modules:
  0.0 125.7 jit_solution(12596804500964316824)
XLA Ops:
  0.6 0.0 copy-start
  0.7 0.0 copy-start.8
  0.7 0.0 copy-start.7
  0.7 2.1 %shard_map.112 = bf16[2,4,2,128,256]{4,3,2,1,0:T(8,128)(2,1)} custom-call(s32[1]{0:T(128)} %bitcast.3.core_ref, bf16[4,2,128,256]{3,2,1,0:T(8,128)(2,1)} %bitcast.18, bf16[2,128,256]{2,1,0:T(8,128)(2,1)} %bitcast.19), custom_call_target="tpu_custom_call" | custom-call | flops 100000 | bytes 1000000 | tf_op jit(solution)/shard_map/pallas_call | solution.py:262
  2.8 11.9 %all-to-all-start = ((bf16[16,128,256]{2,1,0:T(8,128)(2,1)}), bf16[16,128,256]{2,1,0:T(8,128)(2,1)}, u32[]{:S(2)}, u32[]{:S(2)}) async-start(bf16[16,128,256]{2,1,0:T(8,128)(2,1)} %bitcast.17), calls=%async_computation | async-start | bytes 2097152 | tf_op jit(solution)/shard_map/all_to_all | solution.py:235
  14.6 0.0 copy-done.8
  14.6 0.6 constant_dynamic-slice_fusion.1
  15.2 0.0 copy-done.7
  15.2 0.2 fusion
  15.4 0.7 fusion.1
  16.1 0.7 pad_add_fusion
  16.8 2.1 %collective-permute-start = (s32[27]{0:T(128)S(1)}, s32[27]{0:T(128)S(1)}, u32[]{:S(2)}, u32[]{:S(2)}) collective-permute-start(s32[27]{0:T(128)S(1)} %pad_add_fusion), channel_id=1, source_target_pairs={{0,1},{1,0},{2,3},{3,2},{4,5},{5,4},{6,7},{7,6},{8,9},{9,8},{10,11... | collective-permute-start | bytes 332 | tf_op jit(solution)/shard_map/ppermute | solution.py:231
  18.9 0.9 dynamic-slice_bitcast_fusion.1.own_g
  19.9 2.2 %collective-permute-start.2 = (bf16[384,256]{1,0:T(8,128)(2,1)S(1)}, bf16[384,256]{1,0:T(8,128)(2,1)S(1)}, u32[]{:S(2)}, u32[]{:S(2)}) collective-permute-start(bf16[384,256]{1,0:T(8,128)(2,1)S(1)} %dynamic-slice_bitcast_fusion.1.own_g), channel_id=1, source_target_pairs={{0,1},{1,0},{2,3},{3,2},{4,5},{5,4},{6,7},{7,6},{8,9},{9,8},{10,11... | collective-permute-start | bytes 589832 | tf_op jit(solution)/shard_map/ppermute | solution.py:231
  22.1 0.0 copy-done
  22.2 2.1 %collective-permute-start.3 = (bf16[12,128,128]{2,1,0:T(8,128)(2,1)S(1)}, bf16[12,128,128]{2,1,0:T(8,128)(2,1)S(1)}, u32[]{:S(2)}, u32[]{:S(2)}) collective-permute-start(bf16[12,128,128]{2,1,0:T(8,128)(2,1)S(1)} %dynamic-slice_bitcast_fusion.own_t), channel_id=1, source_target_pairs={{0,1},{1,0},{2,3},{3,2},{4,5},{5,4},{6,7},{7,6},{8,9},{9,8},{10,11... | collective-permute-start | bytes 1179656 | tf_op jit(solution)/shard_map/ppermute | solution.py:231
  24.3 0.9 dynamic-slice_bitcast_fusion.2.own_x
  25.2 2.2 %collective-permute-start.1 = (bf16[384,256]{1,0:T(8,128)(2,1)S(1)}, bf16[384,256]{1,0:T(8,128)(2,1)S(1)}, u32[]{:S(2)}, u32[]{:S(2)}) collective-permute-start(bf16[384,256]{1,0:T(8,128)(2,1)S(1)} %dynamic-slice_bitcast_fusion.2.own_x), channel_id=1, source_target_pairs={{0,1},{1,0},{2,3},{3,2},{4,5},{5,4},{6,7},{7,6},{8,9},{9,8},{10,11... | collective-permute-start | bytes 589832 | tf_op jit(solution)/shard_map/ppermute | solution.py:231
  27.5 0.0 collective-permute-done
  27.5 0.1 pad_add_fusion.1.info
  27.6 0.0 collective-permute-done.2.got_g
  27.6 0.7 copy-done.3
  28.3 0.3 collective-permute-done.1.got_x
  28.6 0.7 copy-done.5
  29.2 0.0 collective-permute-done.3.got_t
  29.2 0.7 copy-done.1
  30.0 1.0 copy-done.2
  31.0 0.9 copy-done.4
  31.9 0.9 copy-done.6
  32.8 0.9 shard_map.113.job
  33.7 9.0 %all-to-all-done.mine = bf16[16,128,256]{2,1,0:T(8,128)(2,1)} async-done(((bf16[16,128,256]{2,1,0:T(8,128)(2,1)}), bf16[16,128,256]{2,1,0:T(8,128)(2,1)}, u32[]{:S(2)}, u32[]{:S(2)}) %all-to-all-start) | async-done | bytes 1048608 | tf_op jit(solution)/shard_map/all_to_all | solution.py:235
  42.7 1.9 %collective-permute-start.4 = (bf16[16,128,256]{2,1,0:T(8,128)(2,1)}, bf16[16,128,256]{2,1,0:T(8,128)(2,1)S(1)}, u32[]{:S(2)}, u32[]{:S(2)}) collective-permute-start(bf16[16,128,256]{2,1,0:T(8,128)(2,1)} %all-to-all-done.mine), channel_id=1, source_target_pairs={{0,1},{1,0},{2,3},{3,2},{4,5},{5,4},{6,7},{7,6},{8,9},{9,8},{10,11... | collective-permute-start | bytes 3145736 | tf_op jit(solution)/shard_map/ppermute | solution.py:231
  44.6 2.8 %collective-permute-done.4.got = bf16[16,128,256]{2,1,0:T(8,128)(2,1)S(1)} collective-permute-done((bf16[16,128,256]{2,1,0:T(8,128)(2,1)}, bf16[16,128,256]{2,1,0:T(8,128)(2,1)S(1)}, u32[]{:S(2)}, u32[]{:S(2)}) %collective-permute-start.4) | collective-permute-done | bytes 1048608 | tf_op jit(solution)/shard_map/ppermute | solution.py:231
  47.4 10.4 %shard_map.114 = (bf16[8,128,256]{2,1,0:T(8,128)(2,1)S(1)}, bf16[4,256,256]{2,1,0:T(8,128)(2,1)S(1)}, bf16[8,48,256]{2,1,0:T(8,128)(2,1)S(1)}) custom-call(s32[29]{0:T(128)S(1)} %pad_add_fusion.1.info, f32[8]{0:T(128)S(1)} %add_log_fusion.rates, bf16[384,1536]{1,0:T(8,128)(2,1)S(1)} %shard_map.113.job, bf16[16,128,256]{2,1,0:T(8,128)(2,1)} %all-to-all-done.mine, ...), custom_call_target="tpu_custom_call" | custom-call | flops 2800000000 | bytes 10000000 | tf_op jit(solution)/shard_map/pallas_call | solution.py:313
  57.8 13.0 %all_to_all.25.pieces = bf16[4,256,256]{2,1,0:T(8,128)(2,1)S(1)} all-to-all(bf16[4,256,256]{2,1,0:T(8,128)(2,1)S(1)} %get-tuple-element.15), channel_id=1, replica_groups={{0,16,32,48},{1,17,33,49},{2,18,34,50},{3,19,35,51},{4,20,36,52},{5,21,..., dimensions={0} | all-to-all | bytes 1048576 | tf_op jit(solution)/shard_map/all_to_all | solution.py:235
  70.8 0.1 shard_map.115
  70.9 24.4 %all_to_all.26.arrived = bf16[8,208,256]{2,1,0:T(8,128)(2,1)S(1)} all-to-all(bf16[8,208,256]{2,1,0:T(8,128)(2,1)S(1)} %shard_map.115), channel_id=1, replica_groups=mesh['section'=8,'dom'=64] {'section'}, dimensions={0} | all-to-all | bytes 1703936 | tf_op jit(solution)/shard_map/all_to_all | solution.py:235
  95.3 0.7 broadcast_in_dim.10
  95.9 6.4 %all-to-all-start.3 = ((bf16[8,32,256]{2,1,0:T(8,128)(2,1)}), bf16[8,32,256]{2,1,0:T(8,128)(2,1)S(1)}, u32[]{:S(2)}, u32[]{:S(2)}) async-start(bf16[8,32,256]{2,1,0:T(8,128)(2,1)} %broadcast_in_dim.10), calls=%async_computation.3 | async-start | bytes 262144 | tf_op jit(solution)/shard_map/all_to_all | solution.py:235
  102.3 0.7 shard_map.117
  103.1 7.7 %collective-permute-start.5 = (bf16[4,128,256]{2,1,0:T(8,128)(2,1)S(1)}, bf16[4,128,256]{2,1,0:T(8,128)(2,1)S(1)}, u32[]{:S(2)}, u32[]{:S(2)}) collective-permute-start(bf16[4,128,256]{2,1,0:T(8,128)(2,1)S(1)} %get-tuple-element.21), channel_id=1, source_target_pairs={{0,63},{1,2},{2,1},{3,4},{4,3},{5,6},{6,5},{7,8},{8,7},{9,10},{10,... | collective-permute-start | bytes 786440 | tf_op jit(solution)/shard_map/ppermute | solution.py:389
  110.8 0.0 all-to-all-done.3
  110.8 0.7 broadcast_in_dim.11
  111.5 8.2 %all-to-all-start.4 = ((bf16[8,32,256]{2,1,0:T(8,128)(2,1)}), bf16[8,32,256]{2,1,0:T(8,128)(2,1)S(1)}, u32[]{:S(2)}, u32[]{:S(2)}) async-start(bf16[8,32,256]{2,1,0:T(8,128)(2,1)} %broadcast_in_dim.11), calls=%async_computation.4 | async-start | bytes 262144 | tf_op jit(solution)/shard_map/all_to_all | solution.py:235
  119.7 0.0 collective-permute-done.5.comes
  119.7 0.8 shard_map.118
  120.5 4.5 %all-to-all-done.4.spread = bf16[8,32,256]{2,1,0:T(8,128)(2,1)S(1)} async-done(((bf16[8,32,256]{2,1,0:T(8,128)(2,1)}), bf16[8,32,256]{2,1,0:T(8,128)(2,1)S(1)}, u32[]{:S(2)}, u32[]{:S(2)}) %all-to-all-start.4) | async-done | bytes 131104 | tf_op jit(solution)/shard_map/all_to_all | solution.py:235
  125.0 0.7 shard_map.116
  (12 shorter events, 0.1 us)
Async XLA Ops:
  0.6 21.5 %copy-start = (bf16[4,12,128,128]{3,2,1,0:T(8,128)(2,1)S(1)}, bf16[4,12,128,128]{3,2,1,0:T(8,128)(2,1)}, u32[]{:S(2)}) copy-start(bf16[4,12,128,128]{3,2,1,0:T(8,128)(2,1)} %param.13) | copy-start | bytes 4718596
  0.7 14.0 %copy-start.8 = (s32[4,1]{0,1:T(1,128)S(1)}, s32[4,1]{0,1:T(1,128)}, u32[]{:S(2)}) copy-start(s32[4,1]{0,1:T(1,128)} %param.16) | copy-start | bytes 52
  0.7 14.6 %copy-start.7 = (s32[4,2]{0,1:T(2,128)S(1)}, s32[4,2]{0,1:T(2,128)}, u32[]{:S(2)}) copy-start(s32[4,2]{0,1:T(2,128)} %param.17) | copy-start | bytes 100
  2.8 39.9 %all-to-all-start = ((bf16[16,128,256]{2,1,0:T(8,128)(2,1)}), bf16[16,128,256]{2,1,0:T(8,128)(2,1)}, u32[]{:S(2)}, u32[]{:S(2)}) async-start(bf16[16,128,256]{2,1,0:T(8,128)(2,1)} %bitcast.17), calls=%async_computation | async-start | bytes 2097152 | tf_op jit(solution)/shard_map/all_to_all | solution.py:235
  16.8 10.6 %collective-permute-start = (s32[27]{0:T(128)S(1)}, s32[27]{0:T(128)S(1)}, u32[]{:S(2)}, u32[]{:S(2)}) collective-permute-start(s32[27]{0:T(128)S(1)} %pad_add_fusion), channel_id=1, source_target_pairs={{0,1},{1,0},{2,3},{3,2},{4,5},{5,4},{6,7},{7,6},{8,9},{9,8},{10,11... | collective-permute-start | bytes 332 | tf_op jit(solution)/shard_map/ppermute | solution.py:231
  19.9 7.7 %collective-permute-start.2 = (bf16[384,256]{1,0:T(8,128)(2,1)S(1)}, bf16[384,256]{1,0:T(8,128)(2,1)S(1)}, u32[]{:S(2)}, u32[]{:S(2)}) collective-permute-start(bf16[384,256]{1,0:T(8,128)(2,1)S(1)} %dynamic-slice_bitcast_fusion.1.own_g), channel_id=1, source_target_pairs={{0,1},{1,0},{2,3},{3,2},{4,5},{5,4},{6,7},{7,6},{8,9},{9,8},{10,11... | collective-permute-start | bytes 589832 | tf_op jit(solution)/shard_map/ppermute | solution.py:231
  22.2 7.1 %collective-permute-start.3 = (bf16[12,128,128]{2,1,0:T(8,128)(2,1)S(1)}, bf16[12,128,128]{2,1,0:T(8,128)(2,1)S(1)}, u32[]{:S(2)}, u32[]{:S(2)}) collective-permute-start(bf16[12,128,128]{2,1,0:T(8,128)(2,1)S(1)} %dynamic-slice_bitcast_fusion.own_t), channel_id=1, source_target_pairs={{0,1},{1,0},{2,3},{3,2},{4,5},{5,4},{6,7},{7,6},{8,9},{9,8},{10,11... | collective-permute-start | bytes 1179656 | tf_op jit(solution)/shard_map/ppermute | solution.py:231
  25.2 3.3 %collective-permute-start.1 = (bf16[384,256]{1,0:T(8,128)(2,1)S(1)}, bf16[384,256]{1,0:T(8,128)(2,1)S(1)}, u32[]{:S(2)}, u32[]{:S(2)}) collective-permute-start(bf16[384,256]{1,0:T(8,128)(2,1)S(1)} %dynamic-slice_bitcast_fusion.2.own_x), channel_id=1, source_target_pairs={{0,1},{1,0},{2,3},{3,2},{4,5},{5,4},{6,7},{7,6},{8,9},{9,8},{10,11... | collective-permute-start | bytes 589832 | tf_op jit(solution)/shard_map/ppermute | solution.py:231
  27.6 0.7 copy-start.3
  28.6 0.7 copy-start.5
  29.2 0.7 copy-start.1
  30.0 1.0 copy-start.2
  31.0 0.9 copy-start.4
  31.9 0.9 copy-start.6
  42.7 4.8 %collective-permute-start.4 = (bf16[16,128,256]{2,1,0:T(8,128)(2,1)}, bf16[16,128,256]{2,1,0:T(8,128)(2,1)S(1)}, u32[]{:S(2)}, u32[]{:S(2)}) collective-permute-start(bf16[16,128,256]{2,1,0:T(8,128)(2,1)} %all-to-all-done.mine), channel_id=1, source_target_pairs={{0,1},{1,0},{2,3},{3,2},{4,5},{5,4},{6,7},{7,6},{8,9},{9,8},{10,11... | collective-permute-start | bytes 3145736 | tf_op jit(solution)/shard_map/ppermute | solution.py:231
  95.9 14.8 %all-to-all-start.3 = ((bf16[8,32,256]{2,1,0:T(8,128)(2,1)}), bf16[8,32,256]{2,1,0:T(8,128)(2,1)S(1)}, u32[]{:S(2)}, u32[]{:S(2)}) async-start(bf16[8,32,256]{2,1,0:T(8,128)(2,1)} %broadcast_in_dim.10), calls=%async_computation.3 | async-start | bytes 262144 | tf_op jit(solution)/shard_map/all_to_all | solution.py:235
  103.1 16.6 %collective-permute-start.5 = (bf16[4,128,256]{2,1,0:T(8,128)(2,1)S(1)}, bf16[4,128,256]{2,1,0:T(8,128)(2,1)S(1)}, u32[]{:S(2)}, u32[]{:S(2)}) collective-permute-start(bf16[4,128,256]{2,1,0:T(8,128)(2,1)S(1)} %get-tuple-element.21), channel_id=1, source_target_pairs={{0,63},{1,2},{2,1},{3,4},{4,3},{5,6},{6,5},{7,8},{8,7},{9,10},{10,... | collective-permute-start | bytes 786440 | tf_op jit(solution)/shard_map/ppermute | solution.py:389
  111.5 13.5 %all-to-all-start.4 = ((bf16[8,32,256]{2,1,0:T(8,128)(2,1)}), bf16[8,32,256]{2,1,0:T(8,128)(2,1)S(1)}, u32[]{:S(2)}, u32[]{:S(2)}) async-start(bf16[8,32,256]{2,1,0:T(8,128)(2,1)} %broadcast_in_dim.11), calls=%async_computation.4 | async-start | bytes 262144 | tf_op jit(solution)/shard_map/all_to_all | solution.py:235

commit v7 on v6

--- a/solution.py
+++ b/solution.py
@@ -139,7 +139,7 @@
         ext[0:rows, :] = silu.astype(BF16)
         return carry
 
-    lax.fori_loop(0, depth, forward, 0)
+    lax.fori_loop(0, depth, forward, 0, unroll=True)
 
     def backward(index, carry):
         layer = depth - 1 - index
@@ -168,7 +168,7 @@
 
         return carry
 
-    lax.fori_loop(0, depth, backward, 0)
+    lax.fori_loop(0, depth, backward, 0, unroll=True)
     dinput = (ALPHA * acc[...] + last[...]).T.astype(BF16)
     share = width // depth
     hop = share // 2
@@ -362,18 +362,6 @@
     copies = jnp.broadcast_to(piece[None], (chips_y,) + piece.shape)
     copies, arrived = lax.optimization_barrier((copies, arrived))
     piece = exchange(copies, "dom", along_y).astype(F32).sum(axis=0) * scale
-    piece = piece.astype(BF16)
-    copies = jnp.broadcast_to(piece[None], (CHIPS_X * CORES,) + piece.shape)
-    spread = exchange(copies, "dom", plane)
-    weight_grad = call(
-        assemble_body,
-        jax.ShapeDtypeStruct((1, width, width), F32),
-        [vmem()],
-        [],
-        100,
-        100,
-    )(spread)
-
     initial_grad, stays, leaves = call(
         functools.partial(unpack_body, size),
         (
@@ -386,6 +374,10 @@
         100,
         100,
     )(core.astype(jnp.int32)[None], arrived)
+    piece = piece.astype(BF16)
+    copies = jnp.broadcast_to(piece[None], (CHIPS_X * CORES,) + piece.shape)
+    copies, leaves = lax.optimization_barrier((copies, leaves))
+    spread = exchange(copies, "dom", plane)
     comes = lax.ppermute(
         leaves, "dom", [(i, (i - 1) % doms if i % 2 == 0 else (i + 1) % doms) for i in range(doms)]
     )
@@ -397,6 +389,15 @@
         100,
         100,
     )(core.astype(jnp.int32)[None], stays, comes)
+    spread, fresh = lax.optimization_barrier((spread, fresh))
+    weight_grad = call(
+        assemble_body,
+        jax.ShapeDtypeStruct((1, width, width), F32),
+        [vmem()],
+        [],
+        100,
+        100,
+    )(spread)
     return (weight_grad, fresh, initial_grad.transpose(0, 2, 1))
 
 

time: 127 us -> 128 us (level)
  waiting for transfers between devices: 16.6 us -> 24.7 us
  starting transfers between devices: 44.7 us -> 40 us
  Pallas kernels: 15.7 us -> 14.4 us
    all_to_all x3, waiting for transfers between devices: 13.4 us -> 20.9 us  [exchange(): lax.all_to_all(value, axis, 0, 0, tiled=True, axis_index_groups=groups)]
    all_to_all x3, starting transfers between devices: 26.5 us -> 22 us  [exchange(): lax.all_to_all(value, axis, 0, 0, tiled=True, axis_index_groups=groups)]
    pallas_call x1, Pallas kernels: 10.4 us -> 9.08 us  [shards(): call(functools.partial(chain_body, tiles_max), (jax.ShapeDtypeStruct((dep...]
  transfers between devices with their start and end apart: 9 -> 9, of which waited for: 4 -> 6; matrix products, arithmetic and copies ran while one was open for 4% -> 3% of each run, Pallas kernels for 2% -> 2%
where the time goes in v7:
time: 128 us; the launch traced here: 127 us
  starting transfers between devices  40 us (31%)
  blocking collectives  36.9 us (29%)
  waiting for transfers between devices  24.7 us (19%)
  Pallas kernels  14.4 us (11%)
  local copies, waits for them, and re-layouts  9.7 us (8%)
    all_to_all x2, blocking collectives, exchange(): lax.all_to_all(value, axis, 0, 0, tiled=True, axis_index_groups=groups)  36.9 us
    all_to_all x3, starting transfers between devices, exchange(): lax.all_to_all(value, axis, 0, 0, tiled=True, axis_index_groups=groups)  22 us
    all_to_all x3, waiting for transfers between devices, exchange(): lax.all_to_all(value, axis, 0, 0, tiled=True, axis_index_groups=groups)  20.9 us
    ppermute x5, starting transfers between devices, swap(): return lax.ppermute(value, 'dom', [(i, i ^ 1) for i in range(size)])  10.6 us
    pallas_call x1, Pallas kernels, shards(): call(functools.partial(chain_body, tiles_max), (jax.ShapeDtypeStruct((dep...  9.08 us
    ppermute x1, starting transfers between devices, shards(): lax.ppermute(leaves, 'dom', [(i, (i - 1) % doms if i % 2 == 0 else (i + 1...  7.38 us
    unnamed x18, local copies, waits for them, and re-layouts  4.97 us
    ppermute x5, waiting for transfers between devices, swap(): return lax.ppermute(value, 'dom', [(i, i ^ 1) for i in range(size)])  3.11 us
  transfers between devices with their start and end apart: 9, of which 6 were waited for; matrix products, arithmetic and copies ran while one was open for 3% of the time, Pallas kernels for 2%

profile of v7, /device:TPU:1, one launch (start us, length us, event | category | flops | bytes accessed | tf_op | source)
XLA Modules:
  0.0 127.4 jit_solution(11466902358904778029)
XLA Ops:
  0.6 0.0 copy-start
  0.7 0.0 copy-start.8
  0.7 0.0 copy-start.7
  0.7 2.1 %shard_map.112 = bf16[2,4,2,128,256]{4,3,2,1,0:T(8,128)(2,1)} custom-call(s32[1]{0:T(128)} %bitcast.3.core_ref, bf16[4,2,128,256]{3,2,1,0:T(8,128)(2,1)} %bitcast.18, bf16[2,128,256]{2,1,0:T(8,128)(2,1)} %bitcast.19), custom_call_target="tpu_custom_call" | custom-call | flops 100000 | bytes 1000000 | tf_op jit(solution)/shard_map/pallas_call | solution.py:262
  2.8 11.9 %all-to-all-start = ((bf16[16,128,256]{2,1,0:T(8,128)(2,1)}), bf16[16,128,256]{2,1,0:T(8,128)(2,1)}, u32[]{:S(2)}, u32[]{:S(2)}) async-start(bf16[16,128,256]{2,1,0:T(8,128)(2,1)} %bitcast.17), calls=%async_computation | async-start | bytes 2097152 | tf_op jit(solution)/shard_map/all_to_all | solution.py:235
  14.6 0.0 copy-done.8
  14.6 0.6 constant_dynamic-slice_fusion.1
  15.2 0.0 copy-done.7
  15.2 0.2 fusion
  15.4 0.7 fusion.1
  16.1 0.7 pad_add_fusion
  16.8 2.1 %collective-permute-start = (s32[27]{0:T(128)S(1)}, s32[27]{0:T(128)S(1)}, u32[]{:S(2)}, u32[]{:S(2)}) collective-permute-start(s32[27]{0:T(128)S(1)} %pad_add_fusion), channel_id=1, source_target_pairs={{0,1},{1,0},{2,3},{3,2},{4,5},{5,4},{6,7},{7,6},{8,9},{9,8},{10,11... | collective-permute-start | bytes 332 | tf_op jit(solution)/shard_map/ppermute | solution.py:231
  18.9 0.9 dynamic-slice_bitcast_fusion.1.own_g
  19.9 2.2 %collective-permute-start.2 = (bf16[384,256]{1,0:T(8,128)(2,1)S(1)}, bf16[384,256]{1,0:T(8,128)(2,1)S(1)}, u32[]{:S(2)}, u32[]{:S(2)}) collective-permute-start(bf16[384,256]{1,0:T(8,128)(2,1)S(1)} %dynamic-slice_bitcast_fusion.1.own_g), channel_id=1, source_target_pairs={{0,1},{1,0},{2,3},{3,2},{4,5},{5,4},{6,7},{7,6},{8,9},{9,8},{10,11... | collective-permute-start | bytes 589832 | tf_op jit(solution)/shard_map/ppermute | solution.py:231
  22.1 0.0 copy-done
  22.2 2.1 %collective-permute-start.3 = (bf16[12,128,128]{2,1,0:T(8,128)(2,1)S(1)}, bf16[12,128,128]{2,1,0:T(8,128)(2,1)S(1)}, u32[]{:S(2)}, u32[]{:S(2)}) collective-permute-start(bf16[12,128,128]{2,1,0:T(8,128)(2,1)S(1)} %dynamic-slice_bitcast_fusion.own_t), channel_id=1, source_target_pairs={{0,1},{1,0},{2,3},{3,2},{4,5},{5,4},{6,7},{7,6},{8,9},{9,8},{10,11... | collective-permute-start | bytes 1179656 | tf_op jit(solution)/shard_map/ppermute | solution.py:231
  24.3 0.9 dynamic-slice_bitcast_fusion.2.own_x
  25.2 2.2 %collective-permute-start.1 = (bf16[384,256]{1,0:T(8,128)(2,1)S(1)}, bf16[384,256]{1,0:T(8,128)(2,1)S(1)}, u32[]{:S(2)}, u32[]{:S(2)}) collective-permute-start(bf16[384,256]{1,0:T(8,128)(2,1)S(1)} %dynamic-slice_bitcast_fusion.2.own_x), channel_id=1, source_target_pairs={{0,1},{1,0},{2,3},{3,2},{4,5},{5,4},{6,7},{7,6},{8,9},{9,8},{10,11... | collective-permute-start | bytes 589832 | tf_op jit(solution)/shard_map/ppermute | solution.py:231
  27.5 0.0 collective-permute-done
  27.5 0.1 pad_add_fusion.1.info
  27.6 0.0 collective-permute-done.2.got_g
  27.6 0.7 copy-done.3
  28.3 0.3 collective-permute-done.1.got_x
  28.6 0.7 copy-done.5
  29.2 0.0 collective-permute-done.3.got_t
  29.2 0.7 copy-done.1
  30.0 1.0 copy-done.2
  31.0 0.9 copy-done.4
  31.9 0.9 copy-done.6
  32.8 0.9 shard_map.113.job
  33.7 9.0 %all-to-all-done.mine = bf16[16,128,256]{2,1,0:T(8,128)(2,1)} async-done(((bf16[16,128,256]{2,1,0:T(8,128)(2,1)}), bf16[16,128,256]{2,1,0:T(8,128)(2,1)}, u32[]{:S(2)}, u32[]{:S(2)}) %all-to-all-start) | async-done | bytes 1048608 | tf_op jit(solution)/shard_map/all_to_all | solution.py:235
  42.7 1.9 %collective-permute-start.4 = (bf16[16,128,256]{2,1,0:T(8,128)(2,1)}, bf16[16,128,256]{2,1,0:T(8,128)(2,1)S(1)}, u32[]{:S(2)}, u32[]{:S(2)}) collective-permute-start(bf16[16,128,256]{2,1,0:T(8,128)(2,1)} %all-to-all-done.mine), channel_id=1, source_target_pairs={{0,1},{1,0},{2,3},{3,2},{4,5},{5,4},{6,7},{7,6},{8,9},{9,8},{10,11... | collective-permute-start | bytes 3145736 | tf_op jit(solution)/shard_map/ppermute | solution.py:231
  44.6 2.8 %collective-permute-done.4.got = bf16[16,128,256]{2,1,0:T(8,128)(2,1)S(1)} collective-permute-done((bf16[16,128,256]{2,1,0:T(8,128)(2,1)}, bf16[16,128,256]{2,1,0:T(8,128)(2,1)S(1)}, u32[]{:S(2)}, u32[]{:S(2)}) %collective-permute-start.4) | collective-permute-done | bytes 1048608 | tf_op jit(solution)/shard_map/ppermute | solution.py:231
  47.4 9.1 %shard_map.114 = (bf16[8,128,256]{2,1,0:T(8,128)(2,1)S(1)}, bf16[4,256,256]{2,1,0:T(8,128)(2,1)S(1)}, bf16[8,48,256]{2,1,0:T(8,128)(2,1)S(1)}) custom-call(s32[29]{0:T(128)S(1)} %pad_add_fusion.1.info, f32[8]{0:T(128)S(1)} %add_log_fusion.rates, bf16[384,1536]{1,0:T(8,128)(2,1)S(1)} %shard_map.113.job, bf16[16,128,256]{2,1,0:T(8,128)(2,1)} %all-to-all-done.mine, ...), custom_call_target="tpu_custom_call" | custom-call | flops 2800000000 | bytes 10000000 | tf_op jit(solution)/shard_map/pallas_call | solution.py:313
  56.5 13.0 %all_to_all.25.pieces = bf16[4,256,256]{2,1,0:T(8,128)(2,1)S(1)} all-to-all(bf16[4,256,256]{2,1,0:T(8,128)(2,1)S(1)} %get-tuple-element.19), channel_id=1, replica_groups={{0,16,32,48},{1,17,33,49},{2,18,34,50},{3,19,35,51},{4,20,36,52},{5,21,..., dimensions={0} | all-to-all | bytes 1048576 | tf_op jit(solution)/shard_map/all_to_all | solution.py:235
  69.5 0.1 shard_map.115
  69.6 24.0 %all_to_all.26.arrived = bf16[8,208,256]{2,1,0:T(8,128)(2,1)S(1)} all-to-all(bf16[8,208,256]{2,1,0:T(8,128)(2,1)S(1)} %shard_map.115), channel_id=1, replica_groups=mesh['section'=8,'dom'=64] {'section'}, dimensions={0} | all-to-all | bytes 1703936 | tf_op jit(solution)/shard_map/all_to_all | solution.py:235
  93.6 0.7 broadcast_in_dim.10
  94.2 6.8 %all-to-all-start.3 = ((bf16[8,32,256]{2,1,0:T(8,128)(2,1)}), bf16[8,32,256]{2,1,0:T(8,128)(2,1)S(1)}, u32[]{:S(2)}, u32[]{:S(2)}) async-start(bf16[8,32,256]{2,1,0:T(8,128)(2,1)} %broadcast_in_dim.10), calls=%async_computation.3 | async-start | bytes 262144 | tf_op jit(solution)/shard_map/all_to_all | solution.py:235
  101.1 0.7 shard_map.116
  101.8 7.2 %all-to-all-done.3 = bf16[8,32,256]{2,1,0:T(8,128)(2,1)S(1)} async-done(((bf16[8,32,256]{2,1,0:T(8,128)(2,1)}), bf16[8,32,256]{2,1,0:T(8,128)(2,1)S(1)}, u32[]{:S(2)}, u32[]{:S(2)}) %all-to-all-start.3) | async-done | bytes 131104 | tf_op jit(solution)/shard_map/all_to_all | solution.py:235
  109.0 0.7 broadcast_in_dim.11
  109.7 7.4 %collective-permute-start.5 = (bf16[4,128,256]{2,1,0:T(8,128)(2,1)S(1)}, bf16[4,128,256]{2,1,0:T(8,128)(2,1)S(1)}, u32[]{:S(2)}, u32[]{:S(2)}) collective-permute-start(bf16[4,128,256]{2,1,0:T(8,128)(2,1)S(1)} %get-tuple-element.27), channel_id=1, source_target_pairs={{0,63},{1,2},{2,1},{3,4},{4,3},{5,6},{6,5},{7,8},{8,7},{9,10},{10,... | collective-permute-start | bytes 786440 | tf_op jit(solution)/shard_map/ppermute | solution.py:381
  117.1 3.3 %all-to-all-start.4 = ((bf16[8,32,256]{2,1,0:T(8,128)(2,1)}), bf16[8,32,256]{2,1,0:T(8,128)(2,1)S(1)}, u32[]{:S(2)}, u32[]{:S(2)}) async-start(bf16[8,32,256]{2,1,0:T(8,128)(2,1)} %broadcast_in_dim.11), calls=%async_computation.4 | async-start | bytes 262144 | tf_op jit(solution)/shard_map/all_to_all | solution.py:235
  120.4 0.7 collective-permute-done.5.comes
  121.1 0.8 shard_map.117
  122.0 4.8 %all-to-all-done.4.spread = bf16[8,32,256]{2,1,0:T(8,128)(2,1)S(1)} async-done(((bf16[8,32,256]{2,1,0:T(8,128)(2,1)}), bf16[8,32,256]{2,1,0:T(8,128)(2,1)S(1)}, u32[]{:S(2)}, u32[]{:S(2)}) %all-to-all-start.4) | async-done | bytes 131104 | tf_op jit(solution)/shard_map/all_to_all | solution.py:235
  126.7 0.7 shard_map.118
  (12 shorter events, 0.1 us)
Async XLA Ops:
  0.6 21.5 %copy-start = (bf16[4,12,128,128]{3,2,1,0:T(8,128)(2,1)S(1)}, bf16[4,12,128,128]{3,2,1,0:T(8,128)(2,1)}, u32[]{:S(2)}) copy-start(bf16[4,12,128,128]{3,2,1,0:T(8,128)(2,1)} %param.13) | copy-start | bytes 4718596
  0.7 14.0 %copy-start.8 = (s32[4,1]{0,1:T(1,128)S(1)}, s32[4,1]{0,1:T(1,128)}, u32[]{:S(2)}) copy-start(s32[4,1]{0,1:T(1,128)} %param.16) | copy-start | bytes 52
  0.7 14.6 %copy-start.7 = (s32[4,2]{0,1:T(2,128)S(1)}, s32[4,2]{0,1:T(2,128)}, u32[]{:S(2)}) copy-start(s32[4,2]{0,1:T(2,128)} %param.17) | copy-start | bytes 100
  2.8 39.9 %all-to-all-start = ((bf16[16,128,256]{2,1,0:T(8,128)(2,1)}), bf16[16,128,256]{2,1,0:T(8,128)(2,1)}, u32[]{:S(2)}, u32[]{:S(2)}) async-start(bf16[16,128,256]{2,1,0:T(8,128)(2,1)} %bitcast.17), calls=%async_computation | async-start | bytes 2097152 | tf_op jit(solution)/shard_map/all_to_all | solution.py:235
  16.8 10.6 %collective-permute-start = (s32[27]{0:T(128)S(1)}, s32[27]{0:T(128)S(1)}, u32[]{:S(2)}, u32[]{:S(2)}) collective-permute-start(s32[27]{0:T(128)S(1)} %pad_add_fusion), channel_id=1, source_target_pairs={{0,1},{1,0},{2,3},{3,2},{4,5},{5,4},{6,7},{7,6},{8,9},{9,8},{10,11... | collective-permute-start | bytes 332 | tf_op jit(solution)/shard_map/ppermute | solution.py:231
  19.9 7.7 %collective-permute-start.2 = (bf16[384,256]{1,0:T(8,128)(2,1)S(1)}, bf16[384,256]{1,0:T(8,128)(2,1)S(1)}, u32[]{:S(2)}, u32[]{:S(2)}) collective-permute-start(bf16[384,256]{1,0:T(8,128)(2,1)S(1)} %dynamic-slice_bitcast_fusion.1.own_g), channel_id=1, source_target_pairs={{0,1},{1,0},{2,3},{3,2},{4,5},{5,4},{6,7},{7,6},{8,9},{9,8},{10,11... | collective-permute-start | bytes 589832 | tf_op jit(solution)/shard_map/ppermute | solution.py:231
  22.2 7.1 %collective-permute-start.3 = (bf16[12,128,128]{2,1,0:T(8,128)(2,1)S(1)}, bf16[12,128,128]{2,1,0:T(8,128)(2,1)S(1)}, u32[]{:S(2)}, u32[]{:S(2)}) collective-permute-start(bf16[12,128,128]{2,1,0:T(8,128)(2,1)S(1)} %dynamic-slice_bitcast_fusion.own_t), channel_id=1, source_target_pairs={{0,1},{1,0},{2,3},{3,2},{4,5},{5,4},{6,7},{7,6},{8,9},{9,8},{10,11... | collective-permute-start | bytes 1179656 | tf_op jit(solution)/shard_map/ppermute | solution.py:231
  25.2 3.3 %collective-permute-start.1 = (bf16[384,256]{1,0:T(8,128)(2,1)S(1)}, bf16[384,256]{1,0:T(8,128)(2,1)S(1)}, u32[]{:S(2)}, u32[]{:S(2)}) collective-permute-start(bf16[384,256]{1,0:T(8,128)(2,1)S(1)} %dynamic-slice_bitcast_fusion.2.own_x), channel_id=1, source_target_pairs={{0,1},{1,0},{2,3},{3,2},{4,5},{5,4},{6,7},{7,6},{8,9},{9,8},{10,11... | collective-permute-start | bytes 589832 | tf_op jit(solution)/shard_map/ppermute | solution.py:231
  27.6 0.7 copy-start.3
  28.6 0.7 copy-start.5
  29.2 0.7 copy-start.1
  30.0 1.0 copy-start.2
  31.0 0.9 copy-start.4
  31.9 0.9 copy-start.6
  42.7 4.8 %collective-permute-start.4 = (bf16[16,128,256]{2,1,0:T(8,128)(2,1)}, bf16[16,128,256]{2,1,0:T(8,128)(2,1)S(1)}, u32[]{:S(2)}, u32[]{:S(2)}) collective-permute-start(bf16[16,128,256]{2,1,0:T(8,128)(2,1)} %all-to-all-done.mine), channel_id=1, source_target_pairs={{0,1},{1,0},{2,3},{3,2},{4,5},{5,4},{6,7},{7,6},{8,9},{9,8},{10,11... | collective-permute-start | bytes 3145736 | tf_op jit(solution)/shard_map/ppermute | solution.py:231
  94.2 14.8 %all-to-all-start.3 = ((bf16[8,32,256]{2,1,0:T(8,128)(2,1)}), bf16[8,32,256]{2,1,0:T(8,128)(2,1)S(1)}, u32[]{:S(2)}, u32[]{:S(2)}) async-start(bf16[8,32,256]{2,1,0:T(8,128)(2,1)} %broadcast_in_dim.10), calls=%async_computation.3 | async-start | bytes 262144 | tf_op jit(solution)/shard_map/all_to_all | solution.py:235
  109.7 11.4 %collective-permute-start.5 = (bf16[4,128,256]{2,1,0:T(8,128)(2,1)S(1)}, bf16[4,128,256]{2,1,0:T(8,128)(2,1)S(1)}, u32[]{:S(2)}, u32[]{:S(2)}) collective-permute-start(bf16[4,128,256]{2,1,0:T(8,128)(2,1)S(1)} %get-tuple-element.27), channel_id=1, source_target_pairs={{0,63},{1,2},{2,1},{3,4},{4,3},{5,6},{6,5},{7,8},{8,7},{9,10},{10,... | collective-permute-start | bytes 786440 | tf_op jit(solution)/shard_map/ppermute | solution.py:381
  117.1 9.6 %all-to-all-start.4 = ((bf16[8,32,256]{2,1,0:T(8,128)(2,1)}), bf16[8,32,256]{2,1,0:T(8,128)(2,1)S(1)}, u32[]{:S(2)}, u32[]{:S(2)}) async-start(bf16[8,32,256]{2,1,0:T(8,128)(2,1)} %broadcast_in_dim.11), calls=%async_computation.4 | async-start | bytes 262144 | tf_op jit(solution)/shard_map/all_to_all | solution.py:235

commit v8 on v6

--- a/solution.py
+++ b/solution.py
@@ -139,7 +139,7 @@
         ext[0:rows, :] = silu.astype(BF16)
         return carry
 
-    lax.fori_loop(0, depth, forward, 0)
+    lax.fori_loop(0, depth, forward, 0, unroll=True)
 
     def backward(index, carry):
         layer = depth - 1 - index
@@ -168,7 +168,7 @@
 
         return carry
 
-    lax.fori_loop(0, depth, backward, 0)
+    lax.fori_loop(0, depth, backward, 0, unroll=True)
     dinput = (ALPHA * acc[...] + last[...]).T.astype(BF16)
     share = width // depth
     hop = share // 2

time: 127 us -> 125 us (0.984)
  Pallas kernels: 15.7 us -> 14.4 us
    pallas_call x1, Pallas kernels: 10.4 us -> 9.08 us  [shards(): call(functools.partial(chain_body, tiles_max), (jax.ShapeDtypeStruct((dep...]
where the time goes in v8:
time: 125 us; the launch traced here: 124 us
  starting transfers between devices  45.1 us (36%)
  blocking collectives  36.9 us (30%)
  waiting for transfers between devices  16.5 us (13%)
  Pallas kernels  14.4 us (12%)
  local copies, waits for them, and re-layouts  9.7 us (8%)
    all_to_all x2, blocking collectives, exchange(): lax.all_to_all(value, axis, 0, 0, tiled=True, axis_index_groups=groups)  36.9 us
    all_to_all x3, starting transfers between devices, exchange(): lax.all_to_all(value, axis, 0, 0, tiled=True, axis_index_groups=groups)  26.9 us
    all_to_all x3, waiting for transfers between devices, exchange(): lax.all_to_all(value, axis, 0, 0, tiled=True, axis_index_groups=groups)  13.4 us
    ppermute x5, starting transfers between devices, swap(): return lax.ppermute(value, 'dom', [(i, i ^ 1) for i in range(size)])  10.6 us
    pallas_call x1, Pallas kernels, shards(): call(functools.partial(chain_body, tiles_max), (jax.ShapeDtypeStruct((dep...  9.08 us
    ppermute x1, starting transfers between devices, shards(): lax.ppermute(leaves, 'dom', [(i, (i - 1) % doms if i % 2 == 0 else (i + 1...  7.69 us
    unnamed x18, local copies, waits for them, and re-layouts  4.97 us
    ppermute x5, waiting for transfers between devices, swap(): return lax.ppermute(value, 'dom', [(i, i ^ 1) for i in range(size)])  3.11 us
  transfers between devices with their start and end apart: 9, of which 4 were waited for; matrix products, arithmetic and copies ran while one was open for 4% of the time, Pallas kernels for 2%

profile of v8, /device:TPU:1, one launch (start us, length us, event | category | flops | bytes accessed | tf_op | source)
XLA Modules:
  0.0 124.4 jit_solution(1653844414707456027)
XLA Ops:
  0.6 0.0 copy-start
  0.7 0.0 copy-start.8
  0.7 0.0 copy-start.7
  0.7 2.1 %shard_map.112 = bf16[2,4,2,128,256]{4,3,2,1,0:T(8,128)(2,1)} custom-call(s32[1]{0:T(128)} %bitcast.3.core_ref, bf16[4,2,128,256]{3,2,1,0:T(8,128)(2,1)} %bitcast.18, bf16[2,128,256]{2,1,0:T(8,128)(2,1)} %bitcast.19), custom_call_target="tpu_custom_call" | custom-call | flops 100000 | bytes 1000000 | tf_op jit(solution)/shard_map/pallas_call | solution.py:262
  2.8 11.9 %all-to-all-start = ((bf16[16,128,256]{2,1,0:T(8,128)(2,1)}), bf16[16,128,256]{2,1,0:T(8,128)(2,1)}, u32[]{:S(2)}, u32[]{:S(2)}) async-start(bf16[16,128,256]{2,1,0:T(8,128)(2,1)} %bitcast.17), calls=%async_computation | async-start | bytes 2097152 | tf_op jit(solution)/shard_map/all_to_all | solution.py:235
  14.6 0.0 copy-done.8
  14.6 0.6 constant_dynamic-slice_fusion.1
  15.2 0.0 copy-done.7
  15.2 0.2 fusion
  15.4 0.7 fusion.1
  16.1 0.7 pad_add_fusion
  16.8 2.1 %collective-permute-start = (s32[27]{0:T(128)S(1)}, s32[27]{0:T(128)S(1)}, u32[]{:S(2)}, u32[]{:S(2)}) collective-permute-start(s32[27]{0:T(128)S(1)} %pad_add_fusion), channel_id=1, source_target_pairs={{0,1},{1,0},{2,3},{3,2},{4,5},{5,4},{6,7},{7,6},{8,9},{9,8},{10,11... | collective-permute-start | bytes 332 | tf_op jit(solution)/shard_map/ppermute | solution.py:231
  18.9 0.9 dynamic-slice_bitcast_fusion.1.own_g
  19.9 2.2 %collective-permute-start.2 = (bf16[384,256]{1,0:T(8,128)(2,1)S(1)}, bf16[384,256]{1,0:T(8,128)(2,1)S(1)}, u32[]{:S(2)}, u32[]{:S(2)}) collective-permute-start(bf16[384,256]{1,0:T(8,128)(2,1)S(1)} %dynamic-slice_bitcast_fusion.1.own_g), channel_id=1, source_target_pairs={{0,1},{1,0},{2,3},{3,2},{4,5},{5,4},{6,7},{7,6},{8,9},{9,8},{10,11... | collective-permute-start | bytes 589832 | tf_op jit(solution)/shard_map/ppermute | solution.py:231
  22.1 0.0 copy-done
  22.2 2.1 %collective-permute-start.3 = (bf16[12,128,128]{2,1,0:T(8,128)(2,1)S(1)}, bf16[12,128,128]{2,1,0:T(8,128)(2,1)S(1)}, u32[]{:S(2)}, u32[]{:S(2)}) collective-permute-start(bf16[12,128,128]{2,1,0:T(8,128)(2,1)S(1)} %dynamic-slice_bitcast_fusion.own_t), channel_id=1, source_target_pairs={{0,1},{1,0},{2,3},{3,2},{4,5},{5,4},{6,7},{7,6},{8,9},{9,8},{10,11... | collective-permute-start | bytes 1179656 | tf_op jit(solution)/shard_map/ppermute | solution.py:231
  24.3 0.9 dynamic-slice_bitcast_fusion.2.own_x
  25.2 2.2 %collective-permute-start.1 = (bf16[384,256]{1,0:T(8,128)(2,1)S(1)}, bf16[384,256]{1,0:T(8,128)(2,1)S(1)}, u32[]{:S(2)}, u32[]{:S(2)}) collective-permute-start(bf16[384,256]{1,0:T(8,128)(2,1)S(1)} %dynamic-slice_bitcast_fusion.2.own_x), channel_id=1, source_target_pairs={{0,1},{1,0},{2,3},{3,2},{4,5},{5,4},{6,7},{7,6},{8,9},{9,8},{10,11... | collective-permute-start | bytes 589832 | tf_op jit(solution)/shard_map/ppermute | solution.py:231
  27.5 0.0 collective-permute-done
  27.5 0.1 pad_add_fusion.1.info
  27.6 0.0 collective-permute-done.2.got_g
  27.6 0.7 copy-done.3
  28.3 0.3 collective-permute-done.1.got_x
  28.6 0.7 copy-done.5
  29.2 0.0 collective-permute-done.3.got_t
  29.2 0.7 copy-done.1
  30.0 1.0 copy-done.2
  31.0 0.9 copy-done.4
  31.9 0.9 copy-done.6
  32.8 0.9 shard_map.113.job
  33.8 8.9 %all-to-all-done.mine = bf16[16,128,256]{2,1,0:T(8,128)(2,1)} async-done(((bf16[16,128,256]{2,1,0:T(8,128)(2,1)}), bf16[16,128,256]{2,1,0:T(8,128)(2,1)}, u32[]{:S(2)}, u32[]{:S(2)}) %all-to-all-start) | async-done | bytes 1048608 | tf_op jit(solution)/shard_map/all_to_all | solution.py:235
  42.7 1.9 %collective-permute-start.4 = (bf16[16,128,256]{2,1,0:T(8,128)(2,1)}, bf16[16,128,256]{2,1,0:T(8,128)(2,1)S(1)}, u32[]{:S(2)}, u32[]{:S(2)}) collective-permute-start(bf16[16,128,256]{2,1,0:T(8,128)(2,1)} %all-to-all-done.mine), channel_id=1, source_target_pairs={{0,1},{1,0},{2,3},{3,2},{4,5},{5,4},{6,7},{7,6},{8,9},{9,8},{10,11... | collective-permute-start | bytes 3145736 | tf_op jit(solution)/shard_map/ppermute | solution.py:231
  44.6 2.8 %collective-permute-done.4.got = bf16[16,128,256]{2,1,0:T(8,128)(2,1)S(1)} collective-permute-done((bf16[16,128,256]{2,1,0:T(8,128)(2,1)}, bf16[16,128,256]{2,1,0:T(8,128)(2,1)S(1)}, u32[]{:S(2)}, u32[]{:S(2)}) %collective-permute-start.4) | collective-permute-done | bytes 1048608 | tf_op jit(solution)/shard_map/ppermute | solution.py:231
  47.4 9.1 %shard_map.114 = (bf16[8,128,256]{2,1,0:T(8,128)(2,1)S(1)}, bf16[4,256,256]{2,1,0:T(8,128)(2,1)S(1)}, bf16[8,48,256]{2,1,0:T(8,128)(2,1)S(1)}) custom-call(s32[29]{0:T(128)S(1)} %pad_add_fusion.1.info, f32[8]{0:T(128)S(1)} %add_log_fusion.rates, bf16[384,1536]{1,0:T(8,128)(2,1)S(1)} %shard_map.113.job, bf16[16,128,256]{2,1,0:T(8,128)(2,1)} %all-to-all-done.mine, ...), custom_call_target="tpu_custom_call" | custom-call | flops 2800000000 | bytes 10000000 | tf_op jit(solution)/shard_map/pallas_call | solution.py:313
  56.5 13.0 %all_to_all.25.pieces = bf16[4,256,256]{2,1,0:T(8,128)(2,1)S(1)} all-to-all(bf16[4,256,256]{2,1,0:T(8,128)(2,1)S(1)} %get-tuple-element.15), channel_id=1, replica_groups={{0,16,32,48},{1,17,33,49},{2,18,34,50},{3,19,35,51},{4,20,36,52},{5,21,..., dimensions={0} | all-to-all | bytes 1048576 | tf_op jit(solution)/shard_map/all_to_all | solution.py:235
  69.5 0.1 shard_map.115
  69.6 24.0 %all_to_all.26.arrived = bf16[8,208,256]{2,1,0:T(8,128)(2,1)S(1)} all-to-all(bf16[8,208,256]{2,1,0:T(8,128)(2,1)S(1)} %shard_map.115), channel_id=1, replica_groups=mesh['section'=8,'dom'=64] {'section'}, dimensions={0} | all-to-all | bytes 1703936 | tf_op jit(solution)/shard_map/all_to_all | solution.py:235
  93.6 0.7 broadcast_in_dim.10
  94.2 6.8 %all-to-all-start.3 = ((bf16[8,32,256]{2,1,0:T(8,128)(2,1)}), bf16[8,32,256]{2,1,0:T(8,128)(2,1)S(1)}, u32[]{:S(2)}, u32[]{:S(2)}) async-start(bf16[8,32,256]{2,1,0:T(8,128)(2,1)} %broadcast_in_dim.10), calls=%async_computation.3 | async-start | bytes 262144 | tf_op jit(solution)/shard_map/all_to_all | solution.py:235
  101.1 0.7 shard_map.117
  101.8 7.7 %collective-permute-start.5 = (bf16[4,128,256]{2,1,0:T(8,128)(2,1)S(1)}, bf16[4,128,256]{2,1,0:T(8,128)(2,1)S(1)}, u32[]{:S(2)}, u32[]{:S(2)}) collective-permute-start(bf16[4,128,256]{2,1,0:T(8,128)(2,1)S(1)} %get-tuple-element.21), channel_id=1, source_target_pairs={{0,63},{1,2},{2,1},{3,4},{4,3},{5,6},{6,5},{7,8},{8,7},{9,10},{10,... | collective-permute-start | bytes 786440 | tf_op jit(solution)/shard_map/ppermute | solution.py:389
  109.5 0.0 all-to-all-done.3
  109.5 0.7 broadcast_in_dim.11
  110.2 8.2 %all-to-all-start.4 = ((bf16[8,32,256]{2,1,0:T(8,128)(2,1)}), bf16[8,32,256]{2,1,0:T(8,128)(2,1)S(1)}, u32[]{:S(2)}, u32[]{:S(2)}) async-start(bf16[8,32,256]{2,1,0:T(8,128)(2,1)} %broadcast_in_dim.11), calls=%async_computation.4 | async-start | bytes 262144 | tf_op jit(solution)/shard_map/all_to_all | solution.py:235
  118.4 0.0 collective-permute-done.5.comes
  118.4 0.8 shard_map.118
  119.2 4.5 %all-to-all-done.4.spread = bf16[8,32,256]{2,1,0:T(8,128)(2,1)S(1)} async-done(((bf16[8,32,256]{2,1,0:T(8,128)(2,1)}), bf16[8,32,256]{2,1,0:T(8,128)(2,1)S(1)}, u32[]{:S(2)}, u32[]{:S(2)}) %all-to-all-start.4) | async-done | bytes 131104 | tf_op jit(solution)/shard_map/all_to_all | solution.py:235
  123.7 0.7 shard_map.116
  (12 shorter events, 0.1 us)
Async XLA Ops:
  0.6 21.5 %copy-start = (bf16[4,12,128,128]{3,2,1,0:T(8,128)(2,1)S(1)}, bf16[4,12,128,128]{3,2,1,0:T(8,128)(2,1)}, u32[]{:S(2)}) copy-start(bf16[4,12,128,128]{3,2,1,0:T(8,128)(2,1)} %param.13) | copy-start | bytes 4718596
  0.7 14.0 %copy-start.8 = (s32[4,1]{0,1:T(1,128)S(1)}, s32[4,1]{0,1:T(1,128)}, u32[]{:S(2)}) copy-start(s32[4,1]{0,1:T(1,128)} %param.16) | copy-start | bytes 52
  0.7 14.6 %copy-start.7 = (s32[4,2]{0,1:T(2,128)S(1)}, s32[4,2]{0,1:T(2,128)}, u32[]{:S(2)}) copy-start(s32[4,2]{0,1:T(2,128)} %param.17) | copy-start | bytes 100
  2.8 39.9 %all-to-all-start = ((bf16[16,128,256]{2,1,0:T(8,128)(2,1)}), bf16[16,128,256]{2,1,0:T(8,128)(2,1)}, u32[]{:S(2)}, u32[]{:S(2)}) async-start(bf16[16,128,256]{2,1,0:T(8,128)(2,1)} %bitcast.17), calls=%async_computation | async-start | bytes 2097152 | tf_op jit(solution)/shard_map/all_to_all | solution.py:235
  16.8 10.6 %collective-permute-start = (s32[27]{0:T(128)S(1)}, s32[27]{0:T(128)S(1)}, u32[]{:S(2)}, u32[]{:S(2)}) collective-permute-start(s32[27]{0:T(128)S(1)} %pad_add_fusion), channel_id=1, source_target_pairs={{0,1},{1,0},{2,3},{3,2},{4,5},{5,4},{6,7},{7,6},{8,9},{9,8},{10,11... | collective-permute-start | bytes 332 | tf_op jit(solution)/shard_map/ppermute | solution.py:231
  19.9 7.7 %collective-permute-start.2 = (bf16[384,256]{1,0:T(8,128)(2,1)S(1)}, bf16[384,256]{1,0:T(8,128)(2,1)S(1)}, u32[]{:S(2)}, u32[]{:S(2)}) collective-permute-start(bf16[384,256]{1,0:T(8,128)(2,1)S(1)} %dynamic-slice_bitcast_fusion.1.own_g), channel_id=1, source_target_pairs={{0,1},{1,0},{2,3},{3,2},{4,5},{5,4},{6,7},{7,6},{8,9},{9,8},{10,11... | collective-permute-start | bytes 589832 | tf_op jit(solution)/shard_map/ppermute | solution.py:231
  22.2 7.1 %collective-permute-start.3 = (bf16[12,128,128]{2,1,0:T(8,128)(2,1)S(1)}, bf16[12,128,128]{2,1,0:T(8,128)(2,1)S(1)}, u32[]{:S(2)}, u32[]{:S(2)}) collective-permute-start(bf16[12,128,128]{2,1,0:T(8,128)(2,1)S(1)} %dynamic-slice_bitcast_fusion.own_t), channel_id=1, source_target_pairs={{0,1},{1,0},{2,3},{3,2},{4,5},{5,4},{6,7},{7,6},{8,9},{9,8},{10,11... | collective-permute-start | bytes 1179656 | tf_op jit(solution)/shard_map/ppermute | solution.py:231
  25.2 3.3 %collective-permute-start.1 = (bf16[384,256]{1,0:T(8,128)(2,1)S(1)}, bf16[384,256]{1,0:T(8,128)(2,1)S(1)}, u32[]{:S(2)}, u32[]{:S(2)}) collective-permute-start(bf16[384,256]{1,0:T(8,128)(2,1)S(1)} %dynamic-slice_bitcast_fusion.2.own_x), channel_id=1, source_target_pairs={{0,1},{1,0},{2,3},{3,2},{4,5},{5,4},{6,7},{7,6},{8,9},{9,8},{10,11... | collective-permute-start | bytes 589832 | tf_op jit(solution)/shard_map/ppermute | solution.py:231
  27.6 0.7 copy-start.3
  28.6 0.7 copy-start.5
  29.2 0.7 copy-start.1
  30.0 1.0 copy-start.2
  31.0 0.9 copy-start.4
  31.9 0.9 copy-start.6
  42.7 4.8 %collective-permute-start.4 = (bf16[16,128,256]{2,1,0:T(8,128)(2,1)}, bf16[16,128,256]{2,1,0:T(8,128)(2,1)S(1)}, u32[]{:S(2)}, u32[]{:S(2)}) collective-permute-start(bf16[16,128,256]{2,1,0:T(8,128)(2,1)} %all-to-all-done.mine), channel_id=1, source_target_pairs={{0,1},{1,0},{2,3},{3,2},{4,5},{5,4},{6,7},{7,6},{8,9},{9,8},{10,11... | collective-permute-start | bytes 3145736 | tf_op jit(solution)/shard_map/ppermute | solution.py:231
  94.2 15.2 %all-to-all-start.3 = ((bf16[8,32,256]{2,1,0:T(8,128)(2,1)}), bf16[8,32,256]{2,1,0:T(8,128)(2,1)S(1)}, u32[]{:S(2)}, u32[]{:S(2)}) async-start(bf16[8,32,256]{2,1,0:T(8,128)(2,1)} %broadcast_in_dim.10), calls=%async_computation.3 | async-start | bytes 262144 | tf_op jit(solution)/shard_map/all_to_all | solution.py:235
  101.8 16.6 %collective-permute-start.5 = (bf16[4,128,256]{2,1,0:T(8,128)(2,1)S(1)}, bf16[4,128,256]{2,1,0:T(8,128)(2,1)S(1)}, u32[]{:S(2)}, u32[]{:S(2)}) collective-permute-start(bf16[4,128,256]{2,1,0:T(8,128)(2,1)S(1)} %get-tuple-element.21), channel_id=1, source_target_pairs={{0,63},{1,2},{2,1},{3,4},{4,3},{5,6},{6,5},{7,8},{8,7},{9,10},{10,... | collective-permute-start | bytes 786440 | tf_op jit(solution)/shard_map/ppermute | solution.py:389
  110.2 13.5 %all-to-all-start.4 = ((bf16[8,32,256]{2,1,0:T(8,128)(2,1)}), bf16[8,32,256]{2,1,0:T(8,128)(2,1)S(1)}, u32[]{:S(2)}, u32[]{:S(2)}) async-start(bf16[8,32,256]{2,1,0:T(8,128)(2,1)} %broadcast_in_dim.11), calls=%async_computation.4 | async-start | bytes 262144 | tf_op jit(solution)/shard_map/all_to_all | solution.py:235

commit v9 on v8

--- a/solution.py
+++ b/solution.py
@@ -12,6 +12,8 @@
 LAMBDA_RATE = 0.5
 CORES = 2
 CHIPS_X = 4
+NEAR_Y = 2
+PARTS = CHIPS_X * NEAR_Y
 LARGE = 56
 F32 = jnp.float32
 BF16 = jnp.bfloat16
@@ -159,7 +161,7 @@
             part, delta, (((0,), (0,)), ((), ())), preferred_element_type=F32
         ).astype(BF16)
         row = pl.multiple_of(layer * few, few)
-        for piece in range(CHIPS_X):
+        for piece in range(PARTS):
             terms[piece, pl.ds(row, few), :] = dweight[piece * few : (piece + 1) * few]
 
         @pl.when(layer == 0)
@@ -308,13 +310,13 @@
     mine, job = lax.optimization_barrier((mine, job))
     got = swap(mine)
 
-    few = half // CHIPS_X
+    few = half // PARTS
     spare = width // depth + width // depth // 2
     fresh_out, terms, columns = call(
         functools.partial(chain_body, tiles_max),
         (
             jax.ShapeDtypeStruct((depth, size, width), BF16),
-            jax.ShapeDtypeStruct((CHIPS_X, depth * few, width), BF16),
+            jax.ShapeDtypeStruct((PARTS, depth * few, width), BF16),
             jax.ShapeDtypeStruct((depth, spare, width), BF16),
         ),
         [smem()] * 2 + [vmem()] * 3,
@@ -332,21 +334,16 @@
     )(info, rates, job, mine, got)
 
     chips_y = chips // CHIPS_X
-    along_x = [
-        [(x * chips_y + y) * CORES + j for x in range(CHIPS_X)]
-        for y in range(chips_y)
-        for j in range(CORES)
-    ]
-    along_y = [
-        [(x * chips_y + y) * CORES + j for y in range(chips_y)]
-        for x in range(CHIPS_X)
-        for j in range(CORES)
-    ]
-    plane = [
-        [(x * chips_y + y) * CORES + j for x in range(CHIPS_X) for j in range(CORES)]
-        for y in range(chips_y)
-    ]
-    pieces = exchange(terms, "dom", along_x)
+    far_y = chips_y // NEAR_Y
+
+    def dom_of(x, far, near, j):
+        return (x * chips_y + far * NEAR_Y + near) * CORES + j
+
+    xs, nears, fars, cores = range(CHIPS_X), range(NEAR_Y), range(far_y), range(CORES)
+    block = [[dom_of(x, f, n, j) for x in xs for n in nears] for f in fars for j in cores]
+    along_y = [[dom_of(x, f, n, j) for f in fars] for x in xs for n in nears for j in cores]
+    plane = [[dom_of(x, f, n, j) for x in xs for n in nears for j in cores] for f in fars]
+    pieces = exchange(terms, "dom", block)
     parcel = call(
         merge_body,
         jax.ShapeDtypeStruct((depth, size + spare + few, width), BF16),
@@ -359,11 +356,11 @@
     arrived = exchange(parcel, "section")
     scale = 1.0 / math.sqrt(spans * rows * doms)
     piece = arrived[:, size + spare :, :].astype(F32).sum(axis=0).astype(BF16)
-    copies = jnp.broadcast_to(piece[None], (chips_y,) + piece.shape)
+    copies = jnp.broadcast_to(piece[None], (far_y,) + piece.shape)
     copies, arrived = lax.optimization_barrier((copies, arrived))
     piece = exchange(copies, "dom", along_y).astype(F32).sum(axis=0) * scale
     piece = piece.astype(BF16)
-    copies = jnp.broadcast_to(piece[None], (CHIPS_X * CORES,) + piece.shape)
+    copies = jnp.broadcast_to(piece[None], (PARTS * CORES,) + piece.shape)
     spread = exchange(copies, "dom", plane)
     weight_grad = call(
         assemble_body,

time: 125 us -> 124 us (level)
  starting transfers between devices: 45.1 us -> 42.8 us
    ppermute x1, starting transfers between devices: 7.69 us -> 6.29 us  [shards(): lax.ppermute(leaves, 'dom', [(i, (i - 1) % doms if i % 2 == 0 else (i + 1...]
where the time goes in v9:
time: 124 us; the launch traced here: 123 us
  starting transfers between devices  42.8 us (35%)
  blocking collectives  37.4 us (30%)
  waiting for transfers between devices  17.5 us (14%)
  Pallas kernels  14.4 us (12%)
  local copies, waits for them, and re-layouts  9.65 us (8%)
    all_to_all x2, blocking collectives, exchange(): lax.all_to_all(value, axis, 0, 0, tiled=True, axis_index_groups=groups)  37.4 us
    all_to_all x3, starting transfers between devices, exchange(): lax.all_to_all(value, axis, 0, 0, tiled=True, axis_index_groups=groups)  26 us
    all_to_all x3, waiting for transfers between devices, exchange(): lax.all_to_all(value, axis, 0, 0, tiled=True, axis_index_groups=groups)  14.4 us
    ppermute x5, starting transfers between devices, swap(): return lax.ppermute(value, 'dom', [(i, i ^ 1) for i in range(size)])  10.6 us
    pallas_call x1, Pallas kernels, shards(): call(functools.partial(chain_body, tiles_max), (jax.ShapeDtypeStruct((dep...  9.08 us
    ppermute x1, starting transfers between devices, shards(): lax.ppermute(leaves, 'dom', [(i, (i - 1) % doms if i % 2 == 0 else (i + 1...  6.29 us
    unnamed x18, local copies, waits for them, and re-layouts  4.97 us
    ppermute x5, waiting for transfers between devices, swap(): return lax.ppermute(value, 'dom', [(i, i ^ 1) for i in range(size)])  3.11 us
  transfers between devices with their start and end apart: 9, of which 4 were waited for; matrix products, arithmetic and copies ran while one was open for 4% of the time, Pallas kernels for 2%

profile of v9, /device:TPU:1, one launch (start us, length us, event | category | flops | bytes accessed | tf_op | source)
XLA Modules:
  0.0 123.4 jit_solution(2718725832484675271)
XLA Ops:
  0.6 0.0 copy-start
  0.7 0.0 copy-start.8
  0.7 0.0 copy-start.7
  0.7 2.1 %shard_map.112 = bf16[2,4,2,128,256]{4,3,2,1,0:T(8,128)(2,1)} custom-call(s32[1]{0:T(128)} %bitcast.3.core_ref, bf16[4,2,128,256]{3,2,1,0:T(8,128)(2,1)} %bitcast.18, bf16[2,128,256]{2,1,0:T(8,128)(2,1)} %bitcast.19), custom_call_target="tpu_custom_call" | custom-call | flops 100000 | bytes 1000000 | tf_op jit(solution)/shard_map/pallas_call | solution.py:264
  2.8 11.9 %all-to-all-start = ((bf16[16,128,256]{2,1,0:T(8,128)(2,1)}), bf16[16,128,256]{2,1,0:T(8,128)(2,1)}, u32[]{:S(2)}, u32[]{:S(2)}) async-start(bf16[16,128,256]{2,1,0:T(8,128)(2,1)} %bitcast.17), calls=%async_computation | async-start | bytes 2097152 | tf_op jit(solution)/shard_map/all_to_all | solution.py:237
  14.6 0.0 copy-done.8
  14.6 0.6 constant_dynamic-slice_fusion.1
  15.2 0.0 copy-done.7
  15.2 0.2 fusion
  15.4 0.7 fusion.1
  16.1 0.7 pad_add_fusion
  16.8 2.1 %collective-permute-start = (s32[27]{0:T(128)S(1)}, s32[27]{0:T(128)S(1)}, u32[]{:S(2)}, u32[]{:S(2)}) collective-permute-start(s32[27]{0:T(128)S(1)} %pad_add_fusion), channel_id=1, source_target_pairs={{0,1},{1,0},{2,3},{3,2},{4,5},{5,4},{6,7},{7,6},{8,9},{9,8},{10,11... | collective-permute-start | bytes 332 | tf_op jit(solution)/shard_map/ppermute | solution.py:233
  18.9 0.9 dynamic-slice_bitcast_fusion.1.own_g
  19.9 2.2 %collective-permute-start.2 = (bf16[384,256]{1,0:T(8,128)(2,1)S(1)}, bf16[384,256]{1,0:T(8,128)(2,1)S(1)}, u32[]{:S(2)}, u32[]{:S(2)}) collective-permute-start(bf16[384,256]{1,0:T(8,128)(2,1)S(1)} %dynamic-slice_bitcast_fusion.1.own_g), channel_id=1, source_target_pairs={{0,1},{1,0},{2,3},{3,2},{4,5},{5,4},{6,7},{7,6},{8,9},{9,8},{10,11... | collective-permute-start | bytes 589832 | tf_op jit(solution)/shard_map/ppermute | solution.py:233
  22.1 0.0 copy-done
  22.2 2.1 %collective-permute-start.3 = (bf16[12,128,128]{2,1,0:T(8,128)(2,1)S(1)}, bf16[12,128,128]{2,1,0:T(8,128)(2,1)S(1)}, u32[]{:S(2)}, u32[]{:S(2)}) collective-permute-start(bf16[12,128,128]{2,1,0:T(8,128)(2,1)S(1)} %dynamic-slice_bitcast_fusion.own_t), channel_id=1, source_target_pairs={{0,1},{1,0},{2,3},{3,2},{4,5},{5,4},{6,7},{7,6},{8,9},{9,8},{10,11... | collective-permute-start | bytes 1179656 | tf_op jit(solution)/shard_map/ppermute | solution.py:233
  24.3 0.9 dynamic-slice_bitcast_fusion.2.own_x
  25.2 2.2 %collective-permute-start.1 = (bf16[384,256]{1,0:T(8,128)(2,1)S(1)}, bf16[384,256]{1,0:T(8,128)(2,1)S(1)}, u32[]{:S(2)}, u32[]{:S(2)}) collective-permute-start(bf16[384,256]{1,0:T(8,128)(2,1)S(1)} %dynamic-slice_bitcast_fusion.2.own_x), channel_id=1, source_target_pairs={{0,1},{1,0},{2,3},{3,2},{4,5},{5,4},{6,7},{7,6},{8,9},{9,8},{10,11... | collective-permute-start | bytes 589832 | tf_op jit(solution)/shard_map/ppermute | solution.py:233
  27.5 0.0 collective-permute-done
  27.5 0.1 pad_add_fusion.1.info
  27.6 0.0 collective-permute-done.2.got_g
  27.6 0.7 copy-done.3
  28.3 0.3 collective-permute-done.1.got_x
  28.6 0.7 copy-done.5
  29.2 0.0 collective-permute-done.3.got_t
  29.2 0.7 copy-done.1
  30.0 1.0 copy-done.2
  31.0 0.9 copy-done.4
  31.9 0.9 copy-done.6
  32.8 0.9 shard_map.113.job
  33.7 9.0 %all-to-all-done.mine = bf16[16,128,256]{2,1,0:T(8,128)(2,1)} async-done(((bf16[16,128,256]{2,1,0:T(8,128)(2,1)}), bf16[16,128,256]{2,1,0:T(8,128)(2,1)}, u32[]{:S(2)}, u32[]{:S(2)}) %all-to-all-start) | async-done | bytes 1048608 | tf_op jit(solution)/shard_map/all_to_all | solution.py:237
  42.7 1.9 %collective-permute-start.4 = (bf16[16,128,256]{2,1,0:T(8,128)(2,1)}, bf16[16,128,256]{2,1,0:T(8,128)(2,1)S(1)}, u32[]{:S(2)}, u32[]{:S(2)}) collective-permute-start(bf16[16,128,256]{2,1,0:T(8,128)(2,1)} %all-to-all-done.mine), channel_id=1, source_target_pairs={{0,1},{1,0},{2,3},{3,2},{4,5},{5,4},{6,7},{7,6},{8,9},{9,8},{10,11... | collective-permute-start | bytes 3145736 | tf_op jit(solution)/shard_map/ppermute | solution.py:233
  44.6 2.8 %collective-permute-done.4.got = bf16[16,128,256]{2,1,0:T(8,128)(2,1)S(1)} collective-permute-done((bf16[16,128,256]{2,1,0:T(8,128)(2,1)}, bf16[16,128,256]{2,1,0:T(8,128)(2,1)S(1)}, u32[]{:S(2)}, u32[]{:S(2)}) %collective-permute-start.4) | collective-permute-done | bytes 1048608 | tf_op jit(solution)/shard_map/ppermute | solution.py:233
  47.4 9.1 %shard_map.114 = (bf16[8,128,256]{2,1,0:T(8,128)(2,1)S(1)}, bf16[8,128,256]{2,1,0:T(8,128)(2,1)S(1)}, bf16[8,48,256]{2,1,0:T(8,128)(2,1)S(1)}) custom-call(s32[29]{0:T(128)S(1)} %pad_add_fusion.1.info, f32[8]{0:T(128)S(1)} %add_log_fusion.rates, bf16[384,1536]{1,0:T(8,128)(2,1)S(1)} %shard_map.113.job, bf16[16,128,256]{2,1,0:T(8,128)(2,1)} %all-to-all-done.mine, ...), custom_call_target="tpu_custom_call" | custom-call | flops 2800000000 | bytes 10000000 | tf_op jit(solution)/shard_map/pallas_call | solution.py:315
  56.5 14.6 %all_to_all.25.pieces = bf16[8,128,256]{2,1,0:T(8,128)(2,1)S(1)} all-to-all(bf16[8,128,256]{2,1,0:T(8,128)(2,1)S(1)} %get-tuple-element.15), channel_id=1, replica_groups={{0,2,16,18,32,34,48,50},{1,3,17,19,33,35,49,51},{4,6,20,22,36,38,52,54}..., dimensions={0} | all-to-all | bytes 1048576 | tf_op jit(solution)/shard_map/all_to_all | solution.py:237
  71.1 0.1 shard_map.115
  71.2 22.8 %all_to_all.26.arrived = bf16[8,192,256]{2,1,0:T(8,128)(2,1)S(1)} all-to-all(bf16[8,192,256]{2,1,0:T(8,128)(2,1)S(1)} %shard_map.115), channel_id=1, replica_groups=mesh['section'=8,'dom'=64] {'section'}, dimensions={0} | all-to-all | bytes 1572864 | tf_op jit(solution)/shard_map/all_to_all | solution.py:237
  94.0 0.6 broadcast_in_dim.10
  94.6 5.9 %all-to-all-start.3 = ((bf16[4,16,256]{2,1,0:T(8,128)(2,1)}), bf16[4,16,256]{2,1,0:T(8,128)(2,1)S(1)}, u32[]{:S(2)}, u32[]{:S(2)}) async-start(bf16[4,16,256]{2,1,0:T(8,128)(2,1)} %broadcast_in_dim.10), calls=%async_computation.3 | async-start | bytes 65536 | tf_op jit(solution)/shard_map/all_to_all | solution.py:237
  100.5 0.7 shard_map.117
  101.3 6.3 %collective-permute-start.5 = (bf16[4,128,256]{2,1,0:T(8,128)(2,1)S(1)}, bf16[4,128,256]{2,1,0:T(8,128)(2,1)S(1)}, u32[]{:S(2)}, u32[]{:S(2)}) collective-permute-start(bf16[4,128,256]{2,1,0:T(8,128)(2,1)S(1)} %get-tuple-element.21), channel_id=1, source_target_pairs={{0,63},{1,2},{2,1},{3,4},{4,3},{5,6},{6,5},{7,8},{8,7},{9,10},{10,... | collective-permute-start | bytes 786440 | tf_op jit(solution)/shard_map/ppermute | solution.py:386
  107.6 0.0 all-to-all-done.3
  107.6 0.7 broadcast_in_dim.11
  108.3 8.2 %all-to-all-start.4 = ((bf16[16,16,256]{2,1,0:T(8,128)(2,1)}), bf16[16,16,256]{2,1,0:T(8,128)(2,1)S(1)}, u32[]{:S(2)}, u32[]{:S(2)}) async-start(bf16[16,16,256]{2,1,0:T(8,128)(2,1)} %broadcast_in_dim.11), calls=%async_computation.4 | async-start | bytes 262144 | tf_op jit(solution)/shard_map/all_to_all | solution.py:237
  116.5 0.0 collective-permute-done.5.comes
  116.5 0.8 shard_map.118
  117.3 5.4 %all-to-all-done.4.spread = bf16[16,16,256]{2,1,0:T(8,128)(2,1)S(1)} async-done(((bf16[16,16,256]{2,1,0:T(8,128)(2,1)}), bf16[16,16,256]{2,1,0:T(8,128)(2,1)S(1)}, u32[]{:S(2)}, u32[]{:S(2)}) %all-to-all-start.4) | async-done | bytes 131104 | tf_op jit(solution)/shard_map/all_to_all | solution.py:237
  122.7 0.7 shard_map.116
  (12 shorter events, 0.1 us)
Async XLA Ops:
  0.6 21.5 %copy-start = (bf16[4,12,128,128]{3,2,1,0:T(8,128)(2,1)S(1)}, bf16[4,12,128,128]{3,2,1,0:T(8,128)(2,1)}, u32[]{:S(2)}) copy-start(bf16[4,12,128,128]{3,2,1,0:T(8,128)(2,1)} %param.13) | copy-start | bytes 4718596
  0.7 14.0 %copy-start.8 = (s32[4,1]{0,1:T(1,128)S(1)}, s32[4,1]{0,1:T(1,128)}, u32[]{:S(2)}) copy-start(s32[4,1]{0,1:T(1,128)} %param.16) | copy-start | bytes 52
  0.7 14.6 %copy-start.7 = (s32[4,2]{0,1:T(2,128)S(1)}, s32[4,2]{0,1:T(2,128)}, u32[]{:S(2)}) copy-start(s32[4,2]{0,1:T(2,128)} %param.17) | copy-start | bytes 100
  2.8 39.9 %all-to-all-start = ((bf16[16,128,256]{2,1,0:T(8,128)(2,1)}), bf16[16,128,256]{2,1,0:T(8,128)(2,1)}, u32[]{:S(2)}, u32[]{:S(2)}) async-start(bf16[16,128,256]{2,1,0:T(8,128)(2,1)} %bitcast.17), calls=%async_computation | async-start | bytes 2097152 | tf_op jit(solution)/shard_map/all_to_all | solution.py:237
  16.8 10.6 %collective-permute-start = (s32[27]{0:T(128)S(1)}, s32[27]{0:T(128)S(1)}, u32[]{:S(2)}, u32[]{:S(2)}) collective-permute-start(s32[27]{0:T(128)S(1)} %pad_add_fusion), channel_id=1, source_target_pairs={{0,1},{1,0},{2,3},{3,2},{4,5},{5,4},{6,7},{7,6},{8,9},{9,8},{10,11... | collective-permute-start | bytes 332 | tf_op jit(solution)/shard_map/ppermute | solution.py:233
  19.9 7.7 %collective-permute-start.2 = (bf16[384,256]{1,0:T(8,128)(2,1)S(1)}, bf16[384,256]{1,0:T(8,128)(2,1)S(1)}, u32[]{:S(2)}, u32[]{:S(2)}) collective-permute-start(bf16[384,256]{1,0:T(8,128)(2,1)S(1)} %dynamic-slice_bitcast_fusion.1.own_g), channel_id=1, source_target_pairs={{0,1},{1,0},{2,3},{3,2},{4,5},{5,4},{6,7},{7,6},{8,9},{9,8},{10,11... | collective-permute-start | bytes 589832 | tf_op jit(solution)/shard_map/ppermute | solution.py:233
  22.2 7.1 %collective-permute-start.3 = (bf16[12,128,128]{2,1,0:T(8,128)(2,1)S(1)}, bf16[12,128,128]{2,1,0:T(8,128)(2,1)S(1)}, u32[]{:S(2)}, u32[]{:S(2)}) collective-permute-start(bf16[12,128,128]{2,1,0:T(8,128)(2,1)S(1)} %dynamic-slice_bitcast_fusion.own_t), channel_id=1, source_target_pairs={{0,1},{1,0},{2,3},{3,2},{4,5},{5,4},{6,7},{7,6},{8,9},{9,8},{10,11... | collective-permute-start | bytes 1179656 | tf_op jit(solution)/shard_map/ppermute | solution.py:233
  25.2 3.3 %collective-permute-start.1 = (bf16[384,256]{1,0:T(8,128)(2,1)S(1)}, bf16[384,256]{1,0:T(8,128)(2,1)S(1)}, u32[]{:S(2)}, u32[]{:S(2)}) collective-permute-start(bf16[384,256]{1,0:T(8,128)(2,1)S(1)} %dynamic-slice_bitcast_fusion.2.own_x), channel_id=1, source_target_pairs={{0,1},{1,0},{2,3},{3,2},{4,5},{5,4},{6,7},{7,6},{8,9},{9,8},{10,11... | collective-permute-start | bytes 589832 | tf_op jit(solution)/shard_map/ppermute | solution.py:233
  27.6 0.7 copy-start.3
  28.6 0.7 copy-start.5
  29.2 0.7 copy-start.1
  30.0 1.0 copy-start.2
  31.0 0.9 copy-start.4
  31.9 0.9 copy-start.6
  42.7 4.8 %collective-permute-start.4 = (bf16[16,128,256]{2,1,0:T(8,128)(2,1)}, bf16[16,128,256]{2,1,0:T(8,128)(2,1)S(1)}, u32[]{:S(2)}, u32[]{:S(2)}) collective-permute-start(bf16[16,128,256]{2,1,0:T(8,128)(2,1)} %all-to-all-done.mine), channel_id=1, source_target_pairs={{0,1},{1,0},{2,3},{3,2},{4,5},{5,4},{6,7},{7,6},{8,9},{9,8},{10,11... | collective-permute-start | bytes 3145736 | tf_op jit(solution)/shard_map/ppermute | solution.py:233
  94.6 13.0 %all-to-all-start.3 = ((bf16[4,16,256]{2,1,0:T(8,128)(2,1)}), bf16[4,16,256]{2,1,0:T(8,128)(2,1)S(1)}, u32[]{:S(2)}, u32[]{:S(2)}) async-start(bf16[4,16,256]{2,1,0:T(8,128)(2,1)} %broadcast_in_dim.10), calls=%async_computation.3 | async-start | bytes 65536 | tf_op jit(solution)/shard_map/all_to_all | solution.py:237
  101.3 15.2 %collective-permute-start.5 = (bf16[4,128,256]{2,1,0:T(8,128)(2,1)S(1)}, bf16[4,128,256]{2,1,0:T(8,128)(2,1)S(1)}, u32[]{:S(2)}, u32[]{:S(2)}) collective-permute-start(bf16[4,128,256]{2,1,0:T(8,128)(2,1)S(1)} %get-tuple-element.21), channel_id=1, source_target_pairs={{0,63},{1,2},{2,1},{3,4},{4,3},{5,6},{6,5},{7,8},{8,7},{9,10},{10,... | collective-permute-start | bytes 786440 | tf_op jit(solution)/shard_map/ppermute | solution.py:386
  108.3 14.4 %all-to-all-start.4 = ((bf16[16,16,256]{2,1,0:T(8,128)(2,1)}), bf16[16,16,256]{2,1,0:T(8,128)(2,1)S(1)}, u32[]{:S(2)}, u32[]{:S(2)}) async-start(bf16[16,16,256]{2,1,0:T(8,128)(2,1)} %broadcast_in_dim.11), calls=%async_computation.4 | async-start | bytes 262144 | tf_op jit(solution)/shard_map/all_to_all | solution.py:237

commit v10 on v9

--- a/solution.py
+++ b/solution.py
@@ -103,7 +103,7 @@
 
 def chain_body(
     tiles_max, info, rates, job, mine, got, fresh, terms, columns,
-    grad, ext, base, mixes, slopes, acc, last
+    grad, ext, base, mixes, slopes, acc, last, turned
 ):
     rows, width = base.shape
     wide = ext.shape[0]
@@ -171,14 +171,15 @@
         return carry
 
     lax.fori_loop(0, depth, backward, 0, unroll=True)
-    dinput = (ALPHA * acc[...] + last[...]).T.astype(BF16)
+    turned[...] = (ALPHA * acc[...] + last[...]).T.astype(BF16)
     share = width // depth
     hop = share // 2
     for part in range(depth):
-        piece = dinput[part * share : (part + 1) * share]
-        columns[part, :share, :] = piece[:, :width]
-        columns[part, share:, : width // 2] = piece[:hop, width:]
-        columns[part, share:, width // 2 :] = piece[hop:, width:]
+        first = pl.multiple_of(part * share + core * hop, hop)
+        piece = turned[pl.ds(first, hop), :]
+        columns[part, :hop, :] = piece[:, :width]
+        columns[part, hop:, : width // 2] = piece[:, width:]
+        columns[part, hop:, width // 2 :] = jnp.zeros((hop, width // 2), BF16)
 
 
 def merge_body(pieces, fresh, columns, parcel):
@@ -195,20 +196,29 @@
         parcel[layer, middle:, :] = total.astype(BF16)
 
 
-def unpack_body(size, core_ref, arrived, out, stays, leaves):
+def part_body(core_ref, arrived, stays, leaves, held, handed):
+    spans, size, _ = stays.shape
+    spare = held.shape[1]
+    core = core_ref[0]
+    for span in range(spans):
+        near = core * spans + span
+        away = (1 - core) * spans + span
+        leaves[span] = arrived[near, :size, :]
+        stays[span] = arrived[away, :size, :]
+        held[span] = arrived[near, size : size + spare, :]
+        handed[span] = arrived[away, size : size + spare, :]
+
+
+def unpack_body(core_ref, held, passed, out):
     spans, share, _ = out.shape
-    width = arrived.shape[-1]
+    width = held.shape[-1]
     hop = share // 2
-    base = core_ref[0] * spans
-    away = (1 - core_ref[0]) * spans
-    for span in range(spans):
-        leaves[span] = arrived[base + span, :size, :]
-        stays[span] = arrived[away + span, :size, :]
-        top = arrived[base + span, size : size + share, :].astype(F32)
-        low = arrived[base + span, size + share : size + share + hop, :].astype(F32)
-        tail = jnp.concatenate([low[:, : width // 2], low[:, width // 2 :]], axis=0)
-        out[span, :, :width] = top
-        out[span, :, width:] = tail
+    core = core_ref[0]
+    for half, source in ((core, held), (1 - core, passed)):
+        rows = pl.ds(pl.multiple_of(half * hop, hop), hop)
+        for span in range(spans):
+            out[span, rows, :width] = source[span, :hop, :].astype(F32)
+            out[span, rows, width:] = source[span, hop:, : width // 2].astype(F32)
 
 
 def fresh_body(core_ref, stays, comes, out):
@@ -259,6 +269,7 @@
     chips = doms // CORES
     span = section % spans
     parity = section // spans
+    core_ref = core.astype(jnp.int32)[None]
     rates = jnp.log(LAMBDA_RATE / (jnp.arange(depth, dtype=F32) + 1.0) + 1.0)
 
     slots = call(
@@ -311,7 +322,7 @@
     got = swap(mine)
 
     few = half // PARTS
-    spare = width // depth + width // depth // 2
+    spare = width // depth
     fresh_out, terms, columns = call(
         functools.partial(chain_body, tiles_max),
         (
@@ -328,6 +339,7 @@
             pltpu.VMEM((depth, rows, width), F32),
             pltpu.VMEM((rows, width), F32),
             pltpu.VMEM((rows, width), F32),
+            pltpu.VMEM((width, rows), BF16),
         ],
         2800 * 10**6,
         10**7,
@@ -359,8 +371,33 @@
     copies = jnp.broadcast_to(piece[None], (far_y,) + piece.shape)
     copies, arrived = lax.optimization_barrier((copies, arrived))
     piece = exchange(copies, "dom", along_y).astype(F32).sum(axis=0) * scale
+    stays, leaves, held, handed = call(
+        part_body,
+        (
+            jax.ShapeDtypeStruct((spans, size, width), BF16),
+            jax.ShapeDtypeStruct((spans, size, width), BF16),
+            jax.ShapeDtypeStruct((spans, spare, width), BF16),
+            jax.ShapeDtypeStruct((spans, spare, width), BF16),
+        ),
+        [smem(), vmem()],
+        [],
+        100,
+        100,
+    )(core_ref, arrived)
+    comes = lax.ppermute(
+        leaves, "dom", [(i, (i - 1) % doms if i % 2 == 0 else (i + 1) % doms) for i in range(doms)]
+    )
+    fresh = call(
+        fresh_body,
+        jax.ShapeDtypeStruct((1, spans, 2 * size, width), BF16),
+        [smem(), vmem(), vmem()],
+        [],
+        100,
+        100,
+    )(core_ref, stays, comes)
     piece = piece.astype(BF16)
     copies = jnp.broadcast_to(piece[None], (PARTS * CORES,) + piece.shape)
+    copies, handed = lax.optimization_barrier((copies, handed))
     spread = exchange(copies, "dom", plane)
     weight_grad = call(
         assemble_body,
@@ -371,29 +408,15 @@
         100,
     )(spread)
 
-    initial_grad, stays, leaves = call(
-        functools.partial(unpack_body, size),
-        (
-            jax.ShapeDtypeStruct((spans, width // depth, rows), F32),
-            jax.ShapeDtypeStruct((spans, size, width), BF16),
-            jax.ShapeDtypeStruct((spans, size, width), BF16),
-        ),
-        [smem(), vmem()],
-        [],
-        100,
-        100,
-    )(core.astype(jnp.int32)[None], arrived)
-    comes = lax.ppermute(
-        leaves, "dom", [(i, (i - 1) % doms if i % 2 == 0 else (i + 1) % doms) for i in range(doms)]
-    )
-    fresh = call(
-        fresh_body,
-        jax.ShapeDtypeStruct((1, spans, 2 * size, width), BF16),
+    passed = swap(handed)
+    initial_grad = call(
+        unpack_body,
+        jax.ShapeDtypeStruct((spans, width // depth, rows), F32),
         [smem(), vmem(), vmem()],
         [],
         100,
         100,
-    )(core.astype(jnp.int32)[None], stays, comes)
+    )(core_ref, held, passed)
     return (weight_grad, fresh, initial_grad.transpose(0, 2, 1))
 
 

time: 124 us -> 123 us (level)
  waiting for transfers between devices: 17.5 us -> 15.5 us
  starting transfers between devices: 42.8 us -> 44.4 us
    all_to_all x3, waiting for transfers between devices: 14.4 us -> 11.4 us  [exchange(): lax.all_to_all(value, axis, 0, 0, tiled=True, axis_index_groups=groups)]
    ppermute x5 -> x6, starting transfers between devices: 10.6 us -> 12.7 us  [swap(): return lax.ppermute(value, 'dom', [(i, i ^ 1) for i in range(size)])]
    ppermute x5 -> x6, waiting for transfers between devices: 3.11 us -> 4.11 us  [swap(): return lax.ppermute(value, 'dom', [(i, i ^ 1) for i in range(size)])]
  transfers between devices with their start and end apart: 9 -> 10, of which waited for: 4 -> 6; matrix products, arithmetic and copies ran while one was open for 4% -> 4% of each run, Pallas kernels for 2% -> 2%
where the time goes in v10:
time: 123 us; the launch traced here: 122 us
  starting transfers between devices  44.4 us (36%)
  blocking collectives  36.4 us (30%)
  waiting for transfers between devices  15.5 us (13%)
  Pallas kernels  14.4 us (12%)
  local copies, waits for them, and re-layouts  9.65 us (8%)
    all_to_all x2, blocking collectives, exchange(): lax.all_to_all(value, axis, 0, 0, tiled=True, axis_index_groups=groups)  36.4 us
    all_to_all x3, starting transfers between devices, exchange(): lax.all_to_all(value, axis, 0, 0, tiled=True, axis_index_groups=groups)  25.9 us
    ppermute x6, starting transfers between devices, swap(): return lax.ppermute(value, 'dom', [(i, i ^ 1) for i in range(size)])  12.7 us
    all_to_all x3, waiting for transfers between devices, exchange(): lax.all_to_all(value, axis, 0, 0, tiled=True, axis_index_groups=groups)  11.4 us
    pallas_call x1, Pallas kernels, shards(): call(functools.partial(chain_body, tiles_max), (jax.ShapeDtypeStruct((dep...  9.1 us
    ppermute x1, starting transfers between devices, shards(): lax.ppermute(leaves, 'dom', [(i, (i - 1) % doms if i % 2 == 0 else (i + 1...  5.82 us
    unnamed x18, local copies, waits for them, and re-layouts  4.97 us
    ppermute x6, waiting for transfers between devices, swap(): return lax.ppermute(value, 'dom', [(i, i ^ 1) for i in range(size)])  4.11 us
  transfers between devices with their start and end apart: 10, of which 6 were waited for; matrix products, arithmetic and copies ran while one was open for 4% of the time, Pallas kernels for 2%

profile of v10, /device:TPU:1, one launch (start us, length us, event | category | flops | bytes accessed | tf_op | source)
XLA Modules:
  0.0 122.0 jit_solution(15066507900957347031)
XLA Ops:
  0.6 0.0 copy-start
  0.7 0.0 copy-start.8
  0.7 0.0 copy-start.7
  0.7 2.1 %shard_map.112 = bf16[2,4,2,128,256]{4,3,2,1,0:T(8,128)(2,1)} custom-call(s32[1]{0:T(128)} %bitcast.3.core_ref, bf16[4,2,128,256]{3,2,1,0:T(8,128)(2,1)} %bitcast.18, bf16[2,128,256]{2,1,0:T(8,128)(2,1)} %bitcast.20), custom_call_target="tpu_custom_call" | custom-call | flops 100000 | bytes 1000000 | tf_op jit(solution)/shard_map/pallas_call | solution.py:275
  2.8 11.9 %all-to-all-start = ((bf16[16,128,256]{2,1,0:T(8,128)(2,1)}), bf16[16,128,256]{2,1,0:T(8,128)(2,1)}, u32[]{:S(2)}, u32[]{:S(2)}) async-start(bf16[16,128,256]{2,1,0:T(8,128)(2,1)} %bitcast.17), calls=%async_computation | async-start | bytes 2097152 | tf_op jit(solution)/shard_map/all_to_all | solution.py:247
  14.7 0.0 copy-done.8
  14.7 0.6 constant_dynamic-slice_fusion.1
  15.2 0.2 fusion
  15.4 0.7 fusion.1
  16.1 0.7 pad_add_fusion
  16.9 2.1 %collective-permute-start = (s32[27]{0:T(128)S(1)}, s32[27]{0:T(128)S(1)}, u32[]{:S(2)}, u32[]{:S(2)}) collective-permute-start(s32[27]{0:T(128)S(1)} %pad_add_fusion), channel_id=1, source_target_pairs={{0,1},{1,0},{2,3},{3,2},{4,5},{5,4},{6,7},{7,6},{8,9},{9,8},{10,11... | collective-permute-start | bytes 332 | tf_op jit(solution)/shard_map/ppermute | solution.py:243
  18.9 0.9 dynamic-slice_bitcast_fusion.1.own_g
  19.9 2.2 %collective-permute-start.2 = (bf16[384,256]{1,0:T(8,128)(2,1)S(1)}, bf16[384,256]{1,0:T(8,128)(2,1)S(1)}, u32[]{:S(2)}, u32[]{:S(2)}) collective-permute-start(bf16[384,256]{1,0:T(8,128)(2,1)S(1)} %dynamic-slice_bitcast_fusion.1.own_g), channel_id=1, source_target_pairs={{0,1},{1,0},{2,3},{3,2},{4,5},{5,4},{6,7},{7,6},{8,9},{9,8},{10,11... | collective-permute-start | bytes 589832 | tf_op jit(solution)/shard_map/ppermute | solution.py:243
  22.2 2.1 %collective-permute-start.3 = (bf16[12,128,128]{2,1,0:T(8,128)(2,1)S(1)}, bf16[12,128,128]{2,1,0:T(8,128)(2,1)S(1)}, u32[]{:S(2)}, u32[]{:S(2)}) collective-permute-start(bf16[12,128,128]{2,1,0:T(8,128)(2,1)S(1)} %dynamic-slice_bitcast_fusion.own_t), channel_id=1, source_target_pairs={{0,1},{1,0},{2,3},{3,2},{4,5},{5,4},{6,7},{7,6},{8,9},{9,8},{10,11... | collective-permute-start | bytes 1179656 | tf_op jit(solution)/shard_map/ppermute | solution.py:243
  24.3 0.9 dynamic-slice_bitcast_fusion.2.own_x
  25.2 2.2 %collective-permute-start.1 = (bf16[384,256]{1,0:T(8,128)(2,1)S(1)}, bf16[384,256]{1,0:T(8,128)(2,1)S(1)}, u32[]{:S(2)}, u32[]{:S(2)}) collective-permute-start(bf16[384,256]{1,0:T(8,128)(2,1)S(1)} %dynamic-slice_bitcast_fusion.2.own_x), channel_id=1, source_target_pairs={{0,1},{1,0},{2,3},{3,2},{4,5},{5,4},{6,7},{7,6},{8,9},{9,8},{10,11... | collective-permute-start | bytes 589832 | tf_op jit(solution)/shard_map/ppermute | solution.py:243
  27.5 0.0 collective-permute-done
  27.5 0.1 pad_add_fusion.1.info
  27.6 0.0 collective-permute-done.2.got_g
  27.6 0.7 copy-done.3
  28.3 0.3 collective-permute-done.1.got_x
  28.6 0.7 copy-done.5
  29.2 0.0 collective-permute-done.3.got_t
  29.2 0.7 copy-done.1
  30.0 1.0 copy-done.2
  31.0 0.9 copy-done.4
  31.9 0.9 copy-done.6
  32.8 0.9 shard_map.113.job
  33.7 9.0 %all-to-all-done.mine = bf16[16,128,256]{2,1,0:T(8,128)(2,1)} async-done(((bf16[16,128,256]{2,1,0:T(8,128)(2,1)}), bf16[16,128,256]{2,1,0:T(8,128)(2,1)}, u32[]{:S(2)}, u32[]{:S(2)}) %all-to-all-start) | async-done | bytes 1048608 | tf_op jit(solution)/shard_map/all_to_all | solution.py:247
  42.7 1.9 %collective-permute-start.4 = (bf16[16,128,256]{2,1,0:T(8,128)(2,1)}, bf16[16,128,256]{2,1,0:T(8,128)(2,1)S(1)}, u32[]{:S(2)}, u32[]{:S(2)}) collective-permute-start(bf16[16,128,256]{2,1,0:T(8,128)(2,1)} %all-to-all-done.mine), channel_id=1, source_target_pairs={{0,1},{1,0},{2,3},{3,2},{4,5},{5,4},{6,7},{7,6},{8,9},{9,8},{10,11... | collective-permute-start | bytes 3145736 | tf_op jit(solution)/shard_map/ppermute | solution.py:243
  44.6 2.8 %collective-permute-done.4.got = bf16[16,128,256]{2,1,0:T(8,128)(2,1)S(1)} collective-permute-done((bf16[16,128,256]{2,1,0:T(8,128)(2,1)}, bf16[16,128,256]{2,1,0:T(8,128)(2,1)S(1)}, u32[]{:S(2)}, u32[]{:S(2)}) %collective-permute-start.4) | collective-permute-done | bytes 1048608 | tf_op jit(solution)/shard_map/ppermute | solution.py:243
  47.4 9.1 %shard_map.114 = (bf16[8,128,256]{2,1,0:T(8,128)(2,1)S(1)}, bf16[8,128,256]{2,1,0:T(8,128)(2,1)S(1)}, bf16[8,32,256]{2,1,0:T(8,128)(2,1)S(1)}) custom-call(s32[29]{0:T(128)S(1)} %pad_add_fusion.1.info, f32[8]{0:T(128)S(1)} %add_log_fusion.rates, bf16[384,1536]{1,0:T(8,128)(2,1)S(1)} %shard_map.113.job, bf16[16,128,256]{2,1,0:T(8,128)(2,1)} %all-to-all-done.mine, ...), custom_call_target="tpu_custom_call" | custom-call | flops 2800000000 | bytes 10000000 | tf_op jit(solution)/shard_map/pallas_call | solution.py:326
  56.5 14.6 %all_to_all.25.pieces = bf16[8,128,256]{2,1,0:T(8,128)(2,1)S(1)} all-to-all(bf16[8,128,256]{2,1,0:T(8,128)(2,1)S(1)} %get-tuple-element.18), channel_id=1, replica_groups={{0,2,16,18,32,34,48,50},{1,3,17,19,33,35,49,51},{4,6,20,22,36,38,52,54}..., dimensions={0} | all-to-all | bytes 1048576 | tf_op jit(solution)/shard_map/all_to_all | solution.py:247
  71.1 0.1 shard_map.115
  71.2 21.8 %all_to_all.26.arrived = bf16[8,176,256]{2,1,0:T(8,128)(2,1)S(1)} all-to-all(bf16[8,176,256]{2,1,0:T(8,128)(2,1)S(1)} %shard_map.115), channel_id=1, replica_groups=mesh['section'=8,'dom'=64] {'section'}, dimensions={0} | all-to-all | bytes 1441792 | tf_op jit(solution)/shard_map/all_to_all | solution.py:247
  93.1 0.6 broadcast_in_dim.10
  93.7 6.0 %all-to-all-start.3 = ((bf16[4,16,256]{2,1,0:T(8,128)(2,1)}), bf16[4,16,256]{2,1,0:T(8,128)(2,1)S(1)}, u32[]{:S(2)}, u32[]{:S(2)}) async-start(bf16[4,16,256]{2,1,0:T(8,128)(2,1)} %broadcast_in_dim.10), calls=%async_computation.3 | async-start | bytes 65536 | tf_op jit(solution)/shard_map/all_to_all | solution.py:247
  99.7 5.8 %collective-permute-start.5 = (bf16[4,128,256]{2,1,0:T(8,128)(2,1)S(1)}, bf16[4,128,256]{2,1,0:T(8,128)(2,1)S(1)}, u32[]{:S(2)}, u32[]{:S(2)}) collective-permute-start(bf16[4,128,256]{2,1,0:T(8,128)(2,1)S(1)} %get-tuple-element.26), channel_id=1, source_target_pairs={{0,63},{1,2},{2,1},{3,4},{4,3},{5,6},{6,5},{7,8},{8,7},{9,10},{10,... | collective-permute-start | bytes 786440 | tf_op jit(solution)/shard_map/ppermute | solution.py:387
  105.5 0.8 all-to-all-done.3
  106.4 0.7 broadcast_in_dim.11
  107.1 8.0 %all-to-all-start.4 = ((bf16[16,16,256]{2,1,0:T(8,128)(2,1)}), bf16[16,16,256]{2,1,0:T(8,128)(2,1)S(1)}, u32[]{:S(2)}, u32[]{:S(2)}) async-start(bf16[16,16,256]{2,1,0:T(8,128)(2,1)} %broadcast_in_dim.11), calls=%async_computation.4 | async-start | bytes 262144 | tf_op jit(solution)/shard_map/all_to_all | solution.py:247
  115.1 2.1 %collective-permute-start.6 = (bf16[4,32,256]{2,1,0:T(8,128)(2,1)S(1)}, bf16[4,32,256]{2,1,0:T(8,128)(2,1)S(1)}, u32[]{:S(2)}, u32[]{:S(2)}) collective-permute-start(bf16[4,32,256]{2,1,0:T(8,128)(2,1)S(1)} %get-tuple-element.28), channel_id=1, source_target_pairs={{0,1},{1,0},{2,3},{3,2},{4,5},{5,4},{6,7},{7,6},{8,9},{9,8},{10,11... | collective-permute-start | bytes 196616 | tf_op jit(solution)/shard_map/ppermute | solution.py:243
  117.2 1.0 collective-permute-done.6.passed
  118.2 0.7 shard_map.119
  118.9 0.0 collective-permute-done.5.comes
  118.9 0.8 shard_map.118
  119.8 1.6 %all-to-all-done.4.spread = bf16[16,16,256]{2,1,0:T(8,128)(2,1)S(1)} async-done(((bf16[16,16,256]{2,1,0:T(8,128)(2,1)}), bf16[16,16,256]{2,1,0:T(8,128)(2,1)S(1)}, u32[]{:S(2)}, u32[]{:S(2)}) %all-to-all-start.4) | async-done | bytes 131104 | tf_op jit(solution)/shard_map/all_to_all | solution.py:247
  121.3 0.7 shard_map.117
  (15 shorter events, 0.1 us)
Async XLA Ops:
  0.6 21.5 %copy-start = (bf16[4,12,128,128]{3,2,1,0:T(8,128)(2,1)S(1)}, bf16[4,12,128,128]{3,2,1,0:T(8,128)(2,1)}, u32[]{:S(2)}) copy-start(bf16[4,12,128,128]{3,2,1,0:T(8,128)(2,1)} %param.13) | copy-start | bytes 4718596
  0.7 14.0 %copy-start.8 = (s32[4,1]{0,1:T(1,128)S(1)}, s32[4,1]{0,1:T(1,128)}, u32[]{:S(2)}) copy-start(s32[4,1]{0,1:T(1,128)} %param.16) | copy-start | bytes 52
  0.7 14.6 %copy-start.7 = (s32[4,2]{0,1:T(2,128)S(1)}, s32[4,2]{0,1:T(2,128)}, u32[]{:S(2)}) copy-start(s32[4,2]{0,1:T(2,128)} %param.17) | copy-start | bytes 100
  2.8 39.9 %all-to-all-start = ((bf16[16,128,256]{2,1,0:T(8,128)(2,1)}), bf16[16,128,256]{2,1,0:T(8,128)(2,1)}, u32[]{:S(2)}, u32[]{:S(2)}) async-start(bf16[16,128,256]{2,1,0:T(8,128)(2,1)} %bitcast.17), calls=%async_computation | async-start | bytes 2097152 | tf_op jit(solution)/shard_map/all_to_all | solution.py:247
  16.9 10.6 %collective-permute-start = (s32[27]{0:T(128)S(1)}, s32[27]{0:T(128)S(1)}, u32[]{:S(2)}, u32[]{:S(2)}) collective-permute-start(s32[27]{0:T(128)S(1)} %pad_add_fusion), channel_id=1, source_target_pairs={{0,1},{1,0},{2,3},{3,2},{4,5},{5,4},{6,7},{7,6},{8,9},{9,8},{10,11... | collective-permute-start | bytes 332 | tf_op jit(solution)/shard_map/ppermute | solution.py:243
  19.9 7.7 %collective-permute-start.2 = (bf16[384,256]{1,0:T(8,128)(2,1)S(1)}, bf16[384,256]{1,0:T(8,128)(2,1)S(1)}, u32[]{:S(2)}, u32[]{:S(2)}) collective-permute-start(bf16[384,256]{1,0:T(8,128)(2,1)S(1)} %dynamic-slice_bitcast_fusion.1.own_g), channel_id=1, source_target_pairs={{0,1},{1,0},{2,3},{3,2},{4,5},{5,4},{6,7},{7,6},{8,9},{9,8},{10,11... | collective-permute-start | bytes 589832 | tf_op jit(solution)/shard_map/ppermute | solution.py:243
  22.2 7.1 %collective-permute-start.3 = (bf16[12,128,128]{2,1,0:T(8,128)(2,1)S(1)}, bf16[12,128,128]{2,1,0:T(8,128)(2,1)S(1)}, u32[]{:S(2)}, u32[]{:S(2)}) collective-permute-start(bf16[12,128,128]{2,1,0:T(8,128)(2,1)S(1)} %dynamic-slice_bitcast_fusion.own_t), channel_id=1, source_target_pairs={{0,1},{1,0},{2,3},{3,2},{4,5},{5,4},{6,7},{7,6},{8,9},{9,8},{10,11... | collective-permute-start | bytes 1179656 | tf_op jit(solution)/shard_map/ppermute | solution.py:243
  25.2 3.3 %collective-permute-start.1 = (bf16[384,256]{1,0:T(8,128)(2,1)S(1)}, bf16[384,256]{1,0:T(8,128)(2,1)S(1)}, u32[]{:S(2)}, u32[]{:S(2)}) collective-permute-start(bf16[384,256]{1,0:T(8,128)(2,1)S(1)} %dynamic-slice_bitcast_fusion.2.own_x), channel_id=1, source_target_pairs={{0,1},{1,0},{2,3},{3,2},{4,5},{5,4},{6,7},{7,6},{8,9},{9,8},{10,11... | collective-permute-start | bytes 589832 | tf_op jit(solution)/shard_map/ppermute | solution.py:243
  27.6 0.7 copy-start.3
  28.6 0.7 copy-start.5
  29.2 0.7 copy-start.1
  30.0 1.0 copy-start.2
  31.0 0.9 copy-start.4
  31.9 0.9 copy-start.6
  42.7 4.8 %collective-permute-start.4 = (bf16[16,128,256]{2,1,0:T(8,128)(2,1)}, bf16[16,128,256]{2,1,0:T(8,128)(2,1)S(1)}, u32[]{:S(2)}, u32[]{:S(2)}) collective-permute-start(bf16[16,128,256]{2,1,0:T(8,128)(2,1)} %all-to-all-done.mine), channel_id=1, source_target_pairs={{0,1},{1,0},{2,3},{3,2},{4,5},{5,4},{6,7},{7,6},{8,9},{9,8},{10,11... | collective-permute-start | bytes 3145736 | tf_op jit(solution)/shard_map/ppermute | solution.py:243
  93.7 12.7 %all-to-all-start.3 = ((bf16[4,16,256]{2,1,0:T(8,128)(2,1)}), bf16[4,16,256]{2,1,0:T(8,128)(2,1)S(1)}, u32[]{:S(2)}, u32[]{:S(2)}) async-start(bf16[4,16,256]{2,1,0:T(8,128)(2,1)} %broadcast_in_dim.10), calls=%async_computation.3 | async-start | bytes 65536 | tf_op jit(solution)/shard_map/all_to_all | solution.py:247
  99.7 19.2 %collective-permute-start.5 = (bf16[4,128,256]{2,1,0:T(8,128)(2,1)S(1)}, bf16[4,128,256]{2,1,0:T(8,128)(2,1)S(1)}, u32[]{:S(2)}, u32[]{:S(2)}) collective-permute-start(bf16[4,128,256]{2,1,0:T(8,128)(2,1)S(1)} %get-tuple-element.26), channel_id=1, source_target_pairs={{0,63},{1,2},{2,1},{3,4},{4,3},{5,6},{6,5},{7,8},{8,7},{9,10},{10,... | collective-permute-start | bytes 786440 | tf_op jit(solution)/shard_map/ppermute | solution.py:387
  107.1 14.3 %all-to-all-start.4 = ((bf16[16,16,256]{2,1,0:T(8,128)(2,1)}), bf16[16,16,256]{2,1,0:T(8,128)(2,1)S(1)}, u32[]{:S(2)}, u32[]{:S(2)}) async-start(bf16[16,16,256]{2,1,0:T(8,128)(2,1)} %broadcast_in_dim.11), calls=%async_computation.4 | async-start | bytes 262144 | tf_op jit(solution)/shard_map/all_to_all | solution.py:247
  115.1 3.1 %collective-permute-start.6 = (bf16[4,32,256]{2,1,0:T(8,128)(2,1)S(1)}, bf16[4,32,256]{2,1,0:T(8,128)(2,1)S(1)}, u32[]{:S(2)}, u32[]{:S(2)}) collective-permute-start(bf16[4,32,256]{2,1,0:T(8,128)(2,1)S(1)} %get-tuple-element.28), channel_id=1, source_target_pairs={{0,1},{1,0},{2,3},{3,2},{4,5},{5,4},{6,7},{7,6},{8,9},{9,8},{10,11... | collective-permute-start | bytes 196616 | tf_op jit(solution)/shard_map/ppermute | solution.py:243

commit v11 on v10

--- a/solution.py
+++ b/solution.py
@@ -47,18 +47,26 @@
     spans = halo.shape[0]
     core = core_ref[0]
     weight_in = pltpu.make_async_copy(weight_far, weight, fetched.at[0])
-    halo_in = pltpu.make_async_copy(halo_far, halo, fetched.at[1])
+    halo_in = [
+        pltpu.make_async_copy(halo_far.at[span], halo.at[span], fetched.at[1 + span])
+        for span in range(spans)
+    ]
     weight_in.start()
-    halo_in.start()
+    for copy in halo_in:
+        copy.start()
     copies = [
-        pltpu.make_async_copy(weight, out.at[1 - core, span], sent.at[1 + span])
+        pltpu.make_async_copy(weight, out.at[1 - core, span], sent.at[span])
         for span in range(spans)
-    ] + [pltpu.make_async_copy(halo, out.at[core], sent.at[0])]
+    ] + [
+        pltpu.make_async_copy(halo.at[span], out.at[core, span], sent.at[spans + span])
+        for span in range(spans)
+    ]
     weight_in.wait()
-    for copy in copies[:-1]:
+    for copy in copies[:spans]:
         copy.start()
-    halo_in.wait()
-    copies[-1].start()
+    for span in range(spans):
+        halo_in[span].wait()
+        copies[spans + span].start()
     for copy in copies:
         copy.wait()
 
@@ -209,7 +217,8 @@
         handed[span] = arrived[away, size : size + spare, :]
 
 
-def unpack_body(core_ref, held, passed, out):
+def finish_body(core_ref, held, passed, stays, comes, out, fresh):
+    fresh_body(core_ref, stays, comes, fresh)
     spans, share, _ = out.shape
     width = held.shape[-1]
     hop = share // 2
@@ -279,8 +288,8 @@
         [
             pltpu.VMEM((spans, CORES, size, width), BF16),
             pltpu.VMEM((CORES, half, width), BF16),
-            pltpu.SemaphoreType.DMA((2,)),
             pltpu.SemaphoreType.DMA((1 + spans,)),
+            pltpu.SemaphoreType.DMA((2 * spans,)),
         ],
         10**5,
         10**6,
@@ -387,14 +396,6 @@
     comes = lax.ppermute(
         leaves, "dom", [(i, (i - 1) % doms if i % 2 == 0 else (i + 1) % doms) for i in range(doms)]
     )
-    fresh = call(
-        fresh_body,
-        jax.ShapeDtypeStruct((1, spans, 2 * size, width), BF16),
-        [smem(), vmem(), vmem()],
-        [],
-        100,
-        100,
-    )(core_ref, stays, comes)
     piece = piece.astype(BF16)
     copies = jnp.broadcast_to(piece[None], (PARTS * CORES,) + piece.shape)
     copies, handed = lax.optimization_barrier((copies, handed))
@@ -409,14 +410,17 @@
     )(spread)
 
     passed = swap(handed)
-    initial_grad = call(
-        unpack_body,
-        jax.ShapeDtypeStruct((spans, width // depth, rows), F32),
-        [smem(), vmem(), vmem()],
+    initial_grad, fresh = call(
+        finish_body,
+        (
+            jax.ShapeDtypeStruct((spans, width // depth, rows), F32),
+            jax.ShapeDtypeStruct((1, spans, 2 * size, width), BF16),
+        ),
+        [smem()] + [vmem()] * 4,
         [],
         100,
         100,
-    )(core_ref, held, passed)
+    )(core_ref, held, passed, stays, comes)
     return (weight_grad, fresh, initial_grad.transpose(0, 2, 1))
 
 

time: 123 us -> 123 us (level)
  transfers between devices with their start and end apart: 10 -> 10, of which waited for: 6 -> 6; matrix products, arithmetic and copies ran while one was open for 4% -> 4% of each run, Pallas kernels for 2% -> 1%
where the time goes in v11:
time: 123 us; the launch traced here: 122 us
  starting transfers between devices  44.5 us (36%)
  blocking collectives  36.4 us (30%)
  waiting for transfers between devices  16 us (13%)
  Pallas kernels  13.9 us (11%)
  local copies, waits for them, and re-layouts  9.65 us (8%)
    all_to_all x2, blocking collectives, exchange(): lax.all_to_all(value, axis, 0, 0, tiled=True, axis_index_groups=groups)  36.4 us
    all_to_all x3, starting transfers between devices, exchange(): lax.all_to_all(value, axis, 0, 0, tiled=True, axis_index_groups=groups)  25.9 us
    ppermute x6, starting transfers between devices, swap(): return lax.ppermute(value, 'dom', [(i, i ^ 1) for i in range(size)])  12.7 us
    all_to_all x3, waiting for transfers between devices, exchange(): lax.all_to_all(value, axis, 0, 0, tiled=True, axis_index_groups=groups)  11.9 us
    pallas_call x1, Pallas kernels, shards(): call(functools.partial(chain_body, tiles_max), (jax.ShapeDtypeStruct((dep...  9.09 us
    ppermute x1, starting transfers between devices, shards(): lax.ppermute(leaves, 'dom', [(i, (i - 1) % doms if i % 2 == 0 else (i + 1...  5.9 us
    unnamed x18, local copies, waits for them, and re-layouts  4.97 us
    ppermute x6, waiting for transfers between devices, swap(): return lax.ppermute(value, 'dom', [(i, i ^ 1) for i in range(size)])  4.11 us
  transfers between devices with their start and end apart: 10, of which 6 were waited for; matrix products, arithmetic and copies ran while one was open for 4% of the time, Pallas kernels for 1%

profile of v11, /device:TPU:1, one launch (start us, length us, event | category | flops | bytes accessed | tf_op | source)
XLA Modules:
  0.0 122.1 jit_solution(4084631570583178895)
XLA Ops:
  0.6 0.0 copy-start
  0.7 0.0 copy-start.8
  0.7 0.0 copy-start.7
  0.7 2.1 %shard_map.112 = bf16[2,4,2,128,256]{4,3,2,1,0:T(8,128)(2,1)} custom-call(s32[1]{0:T(128)} %bitcast.3.core_ref, bf16[4,2,128,256]{3,2,1,0:T(8,128)(2,1)} %bitcast.18, bf16[2,128,256]{2,1,0:T(8,128)(2,1)} %bitcast.19), custom_call_target="tpu_custom_call" | custom-call | flops 100000 | bytes 1000000 | tf_op jit(solution)/shard_map/pallas_call | solution.py:284
  2.8 11.9 %all-to-all-start = ((bf16[16,128,256]{2,1,0:T(8,128)(2,1)}), bf16[16,128,256]{2,1,0:T(8,128)(2,1)}, u32[]{:S(2)}, u32[]{:S(2)}) async-start(bf16[16,128,256]{2,1,0:T(8,128)(2,1)} %bitcast.17), calls=%async_computation | async-start | bytes 2097152 | tf_op jit(solution)/shard_map/all_to_all | solution.py:256
  14.7 0.6 constant_dynamic-slice_fusion.1
  15.3 0.0 copy-done.7
  15.3 0.2 fusion
  15.5 0.7 fusion.1
  16.2 0.7 pad_add_fusion
  16.9 2.1 %collective-permute-start = (s32[27]{0:T(128)S(1)}, s32[27]{0:T(128)S(1)}, u32[]{:S(2)}, u32[]{:S(2)}) collective-permute-start(s32[27]{0:T(128)S(1)} %pad_add_fusion), channel_id=1, source_target_pairs={{0,1},{1,0},{2,3},{3,2},{4,5},{5,4},{6,7},{7,6},{8,9},{9,8},{10,11... | collective-permute-start | bytes 332 | tf_op jit(solution)/shard_map/ppermute | solution.py:252
  19.0 0.9 dynamic-slice_bitcast_fusion.1.own_g
  19.9 2.2 %collective-permute-start.2 = (bf16[384,256]{1,0:T(8,128)(2,1)S(1)}, bf16[384,256]{1,0:T(8,128)(2,1)S(1)}, u32[]{:S(2)}, u32[]{:S(2)}) collective-permute-start(bf16[384,256]{1,0:T(8,128)(2,1)S(1)} %dynamic-slice_bitcast_fusion.1.own_g), channel_id=1, source_target_pairs={{0,1},{1,0},{2,3},{3,2},{4,5},{5,4},{6,7},{7,6},{8,9},{9,8},{10,11... | collective-permute-start | bytes 589832 | tf_op jit(solution)/shard_map/ppermute | solution.py:252
  22.2 0.0 copy-done
  22.2 2.1 %collective-permute-start.3 = (bf16[12,128,128]{2,1,0:T(8,128)(2,1)S(1)}, bf16[12,128,128]{2,1,0:T(8,128)(2,1)S(1)}, u32[]{:S(2)}, u32[]{:S(2)}) collective-permute-start(bf16[12,128,128]{2,1,0:T(8,128)(2,1)S(1)} %dynamic-slice_bitcast_fusion.own_t), channel_id=1, source_target_pairs={{0,1},{1,0},{2,3},{3,2},{4,5},{5,4},{6,7},{7,6},{8,9},{9,8},{10,11... | collective-permute-start | bytes 1179656 | tf_op jit(solution)/shard_map/ppermute | solution.py:252
  24.3 0.9 dynamic-slice_bitcast_fusion.2.own_x
  25.3 2.2 %collective-permute-start.1 = (bf16[384,256]{1,0:T(8,128)(2,1)S(1)}, bf16[384,256]{1,0:T(8,128)(2,1)S(1)}, u32[]{:S(2)}, u32[]{:S(2)}) collective-permute-start(bf16[384,256]{1,0:T(8,128)(2,1)S(1)} %dynamic-slice_bitcast_fusion.2.own_x), channel_id=1, source_target_pairs={{0,1},{1,0},{2,3},{3,2},{4,5},{5,4},{6,7},{7,6},{8,9},{9,8},{10,11... | collective-permute-start | bytes 589832 | tf_op jit(solution)/shard_map/ppermute | solution.py:252
  27.6 0.0 collective-permute-done
  27.6 0.1 pad_add_fusion.1.info
  27.7 0.0 collective-permute-done.2.got_g
  27.7 0.7 copy-done.3
  28.3 0.3 collective-permute-done.1.got_x
  28.6 0.7 copy-done.5
  29.3 0.0 collective-permute-done.3.got_t
  29.3 0.7 copy-done.1
  30.0 1.0 copy-done.2
  31.0 0.9 copy-done.4
  32.0 0.9 copy-done.6
  32.9 0.9 shard_map.113.job
  33.8 9.0 %all-to-all-done.mine = bf16[16,128,256]{2,1,0:T(8,128)(2,1)} async-done(((bf16[16,128,256]{2,1,0:T(8,128)(2,1)}), bf16[16,128,256]{2,1,0:T(8,128)(2,1)}, u32[]{:S(2)}, u32[]{:S(2)}) %all-to-all-start) | async-done | bytes 1048608 | tf_op jit(solution)/shard_map/all_to_all | solution.py:256
  42.7 1.9 %collective-permute-start.4 = (bf16[16,128,256]{2,1,0:T(8,128)(2,1)}, bf16[16,128,256]{2,1,0:T(8,128)(2,1)S(1)}, u32[]{:S(2)}, u32[]{:S(2)}) collective-permute-start(bf16[16,128,256]{2,1,0:T(8,128)(2,1)} %all-to-all-done.mine), channel_id=1, source_target_pairs={{0,1},{1,0},{2,3},{3,2},{4,5},{5,4},{6,7},{7,6},{8,9},{9,8},{10,11... | collective-permute-start | bytes 3145736 | tf_op jit(solution)/shard_map/ppermute | solution.py:252
  44.7 2.8 %collective-permute-done.4.got = bf16[16,128,256]{2,1,0:T(8,128)(2,1)S(1)} collective-permute-done((bf16[16,128,256]{2,1,0:T(8,128)(2,1)}, bf16[16,128,256]{2,1,0:T(8,128)(2,1)S(1)}, u32[]{:S(2)}, u32[]{:S(2)}) %collective-permute-start.4) | collective-permute-done | bytes 1048608 | tf_op jit(solution)/shard_map/ppermute | solution.py:252
  47.5 9.1 %shard_map.114 = (bf16[8,128,256]{2,1,0:T(8,128)(2,1)S(1)}, bf16[8,128,256]{2,1,0:T(8,128)(2,1)S(1)}, bf16[8,32,256]{2,1,0:T(8,128)(2,1)S(1)}) custom-call(s32[29]{0:T(128)S(1)} %pad_add_fusion.1.info, f32[8]{0:T(128)S(1)} %add_log_fusion.rates, bf16[384,1536]{1,0:T(8,128)(2,1)S(1)} %shard_map.113.job, bf16[16,128,256]{2,1,0:T(8,128)(2,1)} %all-to-all-done.mine, ...), custom_call_target="tpu_custom_call" | custom-call | flops 2800000000 | bytes 10000000 | tf_op jit(solution)/shard_map/pallas_call | solution.py:335
  56.6 14.6 %all_to_all.25.pieces = bf16[8,128,256]{2,1,0:T(8,128)(2,1)S(1)} all-to-all(bf16[8,128,256]{2,1,0:T(8,128)(2,1)S(1)} %get-tuple-element.20), channel_id=1, replica_groups={{0,2,16,18,32,34,48,50},{1,3,17,19,33,35,49,51},{4,6,20,22,36,38,52,54}..., dimensions={0} | all-to-all | bytes 1048576 | tf_op jit(solution)/shard_map/all_to_all | solution.py:256
  71.2 0.1 shard_map.115
  71.3 21.8 %all_to_all.26.arrived = bf16[8,176,256]{2,1,0:T(8,128)(2,1)S(1)} all-to-all(bf16[8,176,256]{2,1,0:T(8,128)(2,1)S(1)} %shard_map.115), channel_id=1, replica_groups=mesh['section'=8,'dom'=64] {'section'}, dimensions={0} | all-to-all | bytes 1441792 | tf_op jit(solution)/shard_map/all_to_all | solution.py:256
  93.1 0.6 broadcast_in_dim.10
  93.7 5.9 %all-to-all-start.3 = ((bf16[4,16,256]{2,1,0:T(8,128)(2,1)}), bf16[4,16,256]{2,1,0:T(8,128)(2,1)S(1)}, u32[]{:S(2)}, u32[]{:S(2)}) async-start(bf16[4,16,256]{2,1,0:T(8,128)(2,1)} %broadcast_in_dim.10), calls=%async_computation.3 | async-start | bytes 65536 | tf_op jit(solution)/shard_map/all_to_all | solution.py:256
  99.7 5.9 %collective-permute-start.6 = (bf16[4,128,256]{2,1,0:T(8,128)(2,1)S(1)}, bf16[4,128,256]{2,1,0:T(8,128)(2,1)S(1)}, u32[]{:S(2)}, u32[]{:S(2)}) collective-permute-start(bf16[4,128,256]{2,1,0:T(8,128)(2,1)S(1)} %get-tuple-element.30), channel_id=1, source_target_pairs={{0,63},{1,2},{2,1},{3,4},{4,3},{5,6},{6,5},{7,8},{8,7},{9,10},{10,... | collective-permute-start | bytes 786440 | tf_op jit(solution)/shard_map/ppermute | solution.py:396
  105.6 0.8 all-to-all-done.3
  106.4 0.7 broadcast_in_dim.11
  107.0 8.1 %all-to-all-start.4 = ((bf16[16,16,256]{2,1,0:T(8,128)(2,1)}), bf16[16,16,256]{2,1,0:T(8,128)(2,1)S(1)}, u32[]{:S(2)}, u32[]{:S(2)}) async-start(bf16[16,16,256]{2,1,0:T(8,128)(2,1)} %broadcast_in_dim.11), calls=%async_computation.4 | async-start | bytes 262144 | tf_op jit(solution)/shard_map/all_to_all | solution.py:256
  115.1 2.1 %collective-permute-start.5 = (bf16[4,32,256]{2,1,0:T(8,128)(2,1)S(1)}, bf16[4,32,256]{2,1,0:T(8,128)(2,1)S(1)}, u32[]{:S(2)}, u32[]{:S(2)}) collective-permute-start(bf16[4,32,256]{2,1,0:T(8,128)(2,1)S(1)} %get-tuple-element.28), channel_id=1, source_target_pairs={{0,1},{1,0},{2,3},{3,2},{4,5},{5,4},{6,7},{7,6},{8,9},{9,8},{10,11... | collective-permute-start | bytes 196616 | tf_op jit(solution)/shard_map/ppermute | solution.py:252
  117.3 1.0 collective-permute-done.5.passed
  118.3 0.0 collective-permute-done.6.comes
  118.3 0.9 shard_map.118
  119.2 2.2 %all-to-all-done.4.spread = bf16[16,16,256]{2,1,0:T(8,128)(2,1)S(1)} async-done(((bf16[16,16,256]{2,1,0:T(8,128)(2,1)}), bf16[16,16,256]{2,1,0:T(8,128)(2,1)S(1)}, u32[]{:S(2)}, u32[]{:S(2)}) %all-to-all-start.4) | async-done | bytes 131104 | tf_op jit(solution)/shard_map/all_to_all | solution.py:256
  121.4 0.7 shard_map.117
  (14 shorter events, 0.1 us)
Async XLA Ops:
  0.6 21.6 %copy-start = (bf16[4,12,128,128]{3,2,1,0:T(8,128)(2,1)S(1)}, bf16[4,12,128,128]{3,2,1,0:T(8,128)(2,1)}, u32[]{:S(2)}) copy-start(bf16[4,12,128,128]{3,2,1,0:T(8,128)(2,1)} %param.13) | copy-start | bytes 4718596
  0.7 14.0 %copy-start.8 = (s32[4,1]{0,1:T(1,128)S(1)}, s32[4,1]{0,1:T(1,128)}, u32[]{:S(2)}) copy-start(s32[4,1]{0,1:T(1,128)} %param.16) | copy-start | bytes 52
  0.7 14.6 %copy-start.7 = (s32[4,2]{0,1:T(2,128)S(1)}, s32[4,2]{0,1:T(2,128)}, u32[]{:S(2)}) copy-start(s32[4,2]{0,1:T(2,128)} %param.17) | copy-start | bytes 100
  2.8 39.9 %all-to-all-start = ((bf16[16,128,256]{2,1,0:T(8,128)(2,1)}), bf16[16,128,256]{2,1,0:T(8,128)(2,1)}, u32[]{:S(2)}, u32[]{:S(2)}) async-start(bf16[16,128,256]{2,1,0:T(8,128)(2,1)} %bitcast.17), calls=%async_computation | async-start | bytes 2097152 | tf_op jit(solution)/shard_map/all_to_all | solution.py:256
  16.9 10.6 %collective-permute-start = (s32[27]{0:T(128)S(1)}, s32[27]{0:T(128)S(1)}, u32[]{:S(2)}, u32[]{:S(2)}) collective-permute-start(s32[27]{0:T(128)S(1)} %pad_add_fusion), channel_id=1, source_target_pairs={{0,1},{1,0},{2,3},{3,2},{4,5},{5,4},{6,7},{7,6},{8,9},{9,8},{10,11... | collective-permute-start | bytes 332 | tf_op jit(solution)/shard_map/ppermute | solution.py:252
  19.9 7.7 %collective-permute-start.2 = (bf16[384,256]{1,0:T(8,128)(2,1)S(1)}, bf16[384,256]{1,0:T(8,128)(2,1)S(1)}, u32[]{:S(2)}, u32[]{:S(2)}) collective-permute-start(bf16[384,256]{1,0:T(8,128)(2,1)S(1)} %dynamic-slice_bitcast_fusion.1.own_g), channel_id=1, source_target_pairs={{0,1},{1,0},{2,3},{3,2},{4,5},{5,4},{6,7},{7,6},{8,9},{9,8},{10,11... | collective-permute-start | bytes 589832 | tf_op jit(solution)/shard_map/ppermute | solution.py:252
  22.2 7.1 %collective-permute-start.3 = (bf16[12,128,128]{2,1,0:T(8,128)(2,1)S(1)}, bf16[12,128,128]{2,1,0:T(8,128)(2,1)S(1)}, u32[]{:S(2)}, u32[]{:S(2)}) collective-permute-start(bf16[12,128,128]{2,1,0:T(8,128)(2,1)S(1)} %dynamic-slice_bitcast_fusion.own_t), channel_id=1, source_target_pairs={{0,1},{1,0},{2,3},{3,2},{4,5},{5,4},{6,7},{7,6},{8,9},{9,8},{10,11... | collective-permute-start | bytes 1179656 | tf_op jit(solution)/shard_map/ppermute | solution.py:252
  25.3 3.3 %collective-permute-start.1 = (bf16[384,256]{1,0:T(8,128)(2,1)S(1)}, bf16[384,256]{1,0:T(8,128)(2,1)S(1)}, u32[]{:S(2)}, u32[]{:S(2)}) collective-permute-start(bf16[384,256]{1,0:T(8,128)(2,1)S(1)} %dynamic-slice_bitcast_fusion.2.own_x), channel_id=1, source_target_pairs={{0,1},{1,0},{2,3},{3,2},{4,5},{5,4},{6,7},{7,6},{8,9},{9,8},{10,11... | collective-permute-start | bytes 589832 | tf_op jit(solution)/shard_map/ppermute | solution.py:252
  27.7 0.7 copy-start.3
  28.6 0.7 copy-start.5
  29.3 0.7 copy-start.1
  30.0 1.0 copy-start.2
  31.0 0.9 copy-start.4
  32.0 0.9 copy-start.6
  42.7 4.8 %collective-permute-start.4 = (bf16[16,128,256]{2,1,0:T(8,128)(2,1)}, bf16[16,128,256]{2,1,0:T(8,128)(2,1)S(1)}, u32[]{:S(2)}, u32[]{:S(2)}) collective-permute-start(bf16[16,128,256]{2,1,0:T(8,128)(2,1)} %all-to-all-done.mine), channel_id=1, source_target_pairs={{0,1},{1,0},{2,3},{3,2},{4,5},{5,4},{6,7},{7,6},{8,9},{9,8},{10,11... | collective-permute-start | bytes 3145736 | tf_op jit(solution)/shard_map/ppermute | solution.py:252
  93.7 12.6 %all-to-all-start.3 = ((bf16[4,16,256]{2,1,0:T(8,128)(2,1)}), bf16[4,16,256]{2,1,0:T(8,128)(2,1)S(1)}, u32[]{:S(2)}, u32[]{:S(2)}) async-start(bf16[4,16,256]{2,1,0:T(8,128)(2,1)} %broadcast_in_dim.10), calls=%async_computation.3 | async-start | bytes 65536 | tf_op jit(solution)/shard_map/all_to_all | solution.py:256
  99.7 18.6 %collective-permute-start.6 = (bf16[4,128,256]{2,1,0:T(8,128)(2,1)S(1)}, bf16[4,128,256]{2,1,0:T(8,128)(2,1)S(1)}, u32[]{:S(2)}, u32[]{:S(2)}) collective-permute-start(bf16[4,128,256]{2,1,0:T(8,128)(2,1)S(1)} %get-tuple-element.30), channel_id=1, source_target_pairs={{0,63},{1,2},{2,1},{3,4},{4,3},{5,6},{6,5},{7,8},{8,7},{9,10},{10,... | collective-permute-start | bytes 786440 | tf_op jit(solution)/shard_map/ppermute | solution.py:396
  107.0 14.3 %all-to-all-start.4 = ((bf16[16,16,256]{2,1,0:T(8,128)(2,1)}), bf16[16,16,256]{2,1,0:T(8,128)(2,1)S(1)}, u32[]{:S(2)}, u32[]{:S(2)}) async-start(bf16[16,16,256]{2,1,0:T(8,128)(2,1)} %broadcast_in_dim.11), calls=%async_computation.4 | async-start | bytes 262144 | tf_op jit(solution)/shard_map/all_to_all | solution.py:256
  115.1 3.1 %collective-permute-start.5 = (bf16[4,32,256]{2,1,0:T(8,128)(2,1)S(1)}, bf16[4,32,256]{2,1,0:T(8,128)(2,1)S(1)}, u32[]{:S(2)}, u32[]{:S(2)}) collective-permute-start(bf16[4,32,256]{2,1,0:T(8,128)(2,1)S(1)} %get-tuple-element.28), channel_id=1, source_target_pairs={{0,1},{1,0},{2,3},{3,2},{4,5},{5,4},{6,7},{7,6},{8,9},{9,8},{10,11... | collective-permute-start | bytes 196616 | tf_op jit(solution)/shard_map/ppermute | solution.py:252

commit v12 on v11

--- a/solution.py
+++ b/solution.py
@@ -110,9 +110,11 @@
 
 
 def chain_body(
-    tiles_max, info, rates, job, mine, got, fresh, terms, columns,
-    grad, ext, base, mixes, slopes, acc, last, turned
+    tiles_max, info, rates, job, mine_far, got, fresh, terms, columns,
+    grad, ext, base, mixes, slopes, acc, last, turned, mine, fetched
 ):
+    fetch = pltpu.make_async_copy(mine_far, mine, fetched.at[0])
+    fetch.start()
     rows, width = base.shape
     wide = ext.shape[0]
     dense = slice(0, wide)
@@ -129,6 +131,7 @@
     base[...] = ALPHA * job[:, inputs].astype(F32)
     grad[...] = job[:, outer]
     acc[...] = jnp.zeros_like(acc)
+    fetch.wait()
 
     def forward(layer, carry):
         rate = rates[layer]
@@ -339,7 +342,7 @@
             jax.ShapeDtypeStruct((PARTS, depth * few, width), BF16),
             jax.ShapeDtypeStruct((depth, spare, width), BF16),
         ),
-        [smem()] * 2 + [vmem()] * 3,
+        [smem()] * 2 + [vmem(), anywhere(), vmem()],
         [
             pltpu.VMEM((rows, width), BF16),
             pltpu.VMEM((wide, width), BF16),
@@ -349,6 +352,8 @@
             pltpu.VMEM((rows, width), F32),
             pltpu.VMEM((rows, width), F32),
             pltpu.VMEM((width, rows), BF16),
+            pltpu.VMEM(mine.shape, BF16),
+            pltpu.SemaphoreType.DMA((1,)),
         ],
         2800 * 10**6,
         10**7,

time: 123 us -> 123 us (level)
  no operation moved by 1% of the time
where the time goes in v12:
time: 123 us
  starting transfers between devices  44.4 us (36%)
  blocking collectives  36.4 us (30%)
  waiting for transfers between devices  16.1 us (13%)
  Pallas kernels  14.4 us (12%)
  local copies, waits for them, and re-layouts  9.65 us (8%)
    all_to_all x2, blocking collectives, exchange(): lax.all_to_all(value, axis, 0, 0, tiled=True, axis_index_groups=groups)  36.4 us
    all_to_all x3, starting transfers between devices, exchange(): lax.all_to_all(value, axis, 0, 0, tiled=True, axis_index_groups=groups)  25.9 us
    ppermute x6, starting transfers between devices, swap(): return lax.ppermute(value, 'dom', [(i, i ^ 1) for i in range(size)])  12.7 us
    all_to_all x3, waiting for transfers between devices, exchange(): lax.all_to_all(value, axis, 0, 0, tiled=True, axis_index_groups=groups)  12 us
    pallas_call x1, Pallas kernels, shards(): call(functools.partial(chain_body, tiles_max), (jax.ShapeDtypeStruct((dep...  9.65 us
    ppermute x1, starting transfers between devices, shards(): lax.ppermute(leaves, 'dom', [(i, (i - 1) % doms if i % 2 == 0 else (i + 1...  5.85 us
    unnamed x18, local copies, waits for them, and re-layouts  4.97 us
    ppermute x6, waiting for transfers between devices, swap(): return lax.ppermute(value, 'dom', [(i, i ^ 1) for i in range(size)])  4.11 us
  transfers between devices with their start and end apart: 10, of which 6 were waited for; matrix products, arithmetic and copies ran while one was open for 4% of the time, Pallas kernels for 1%

profile of v12, /device:TPU:1, one launch (start us, length us, event | category | flops | bytes accessed | tf_op | source)
XLA Modules:
  0.0 122.6 jit_solution(630347827832256703)
XLA Ops:
  0.6 0.0 copy-start
  0.7 0.0 copy-start.8
  0.7 0.0 copy-start.7
  0.7 2.1 %shard_map.112 = bf16[2,4,2,128,256]{4,3,2,1,0:T(8,128)(2,1)} custom-call(s32[1]{0:T(128)} %bitcast.3.core_ref, bf16[4,2,128,256]{3,2,1,0:T(8,128)(2,1)} %bitcast.18, bf16[2,128,256]{2,1,0:T(8,128)(2,1)} %bitcast.19), custom_call_target="tpu_custom_call" | custom-call | flops 100000 | bytes 1000000 | tf_op jit(solution)/shard_map/pallas_call | solution.py:287
  2.8 11.9 %all-to-all-start = ((bf16[16,128,256]{2,1,0:T(8,128)(2,1)}), bf16[16,128,256]{2,1,0:T(8,128)(2,1)}, u32[]{:S(2)}, u32[]{:S(2)}) async-start(bf16[16,128,256]{2,1,0:T(8,128)(2,1)} %bitcast.17), calls=%async_computation | async-start | bytes 2097152 | tf_op jit(solution)/shard_map/all_to_all | solution.py:259
  14.7 0.6 constant_dynamic-slice_fusion.1
  15.3 0.0 copy-done.7
  15.3 0.2 fusion
  15.5 0.7 fusion.1
  16.2 0.7 pad_add_fusion
  16.9 2.1 %collective-permute-start = (s32[27]{0:T(128)S(1)}, s32[27]{0:T(128)S(1)}, u32[]{:S(2)}, u32[]{:S(2)}) collective-permute-start(s32[27]{0:T(128)S(1)} %pad_add_fusion), channel_id=1, source_target_pairs={{0,1},{1,0},{2,3},{3,2},{4,5},{5,4},{6,7},{7,6},{8,9},{9,8},{10,11... | collective-permute-start | bytes 332 | tf_op jit(solution)/shard_map/ppermute | solution.py:255
  19.0 0.9 dynamic-slice_bitcast_fusion.1.own_g
  19.9 2.2 %collective-permute-start.2 = (bf16[384,256]{1,0:T(8,128)(2,1)S(1)}, bf16[384,256]{1,0:T(8,128)(2,1)S(1)}, u32[]{:S(2)}, u32[]{:S(2)}) collective-permute-start(bf16[384,256]{1,0:T(8,128)(2,1)S(1)} %dynamic-slice_bitcast_fusion.1.own_g), channel_id=1, source_target_pairs={{0,1},{1,0},{2,3},{3,2},{4,5},{5,4},{6,7},{7,6},{8,9},{9,8},{10,11... | collective-permute-start | bytes 589832 | tf_op jit(solution)/shard_map/ppermute | solution.py:255
  22.2 0.0 copy-done
  22.2 2.1 %collective-permute-start.3 = (bf16[12,128,128]{2,1,0:T(8,128)(2,1)S(1)}, bf16[12,128,128]{2,1,0:T(8,128)(2,1)S(1)}, u32[]{:S(2)}, u32[]{:S(2)}) collective-permute-start(bf16[12,128,128]{2,1,0:T(8,128)(2,1)S(1)} %dynamic-slice_bitcast_fusion.own_t), channel_id=1, source_target_pairs={{0,1},{1,0},{2,3},{3,2},{4,5},{5,4},{6,7},{7,6},{8,9},{9,8},{10,11... | collective-permute-start | bytes 1179656 | tf_op jit(solution)/shard_map/ppermute | solution.py:255
  24.3 0.9 dynamic-slice_bitcast_fusion.2.own_x
  25.3 2.2 %collective-permute-start.1 = (bf16[384,256]{1,0:T(8,128)(2,1)S(1)}, bf16[384,256]{1,0:T(8,128)(2,1)S(1)}, u32[]{:S(2)}, u32[]{:S(2)}) collective-permute-start(bf16[384,256]{1,0:T(8,128)(2,1)S(1)} %dynamic-slice_bitcast_fusion.2.own_x), channel_id=1, source_target_pairs={{0,1},{1,0},{2,3},{3,2},{4,5},{5,4},{6,7},{7,6},{8,9},{9,8},{10,11... | collective-permute-start | bytes 589832 | tf_op jit(solution)/shard_map/ppermute | solution.py:255
  27.6 0.0 collective-permute-done
  27.6 0.1 pad_add_fusion.1.info
  27.7 0.0 collective-permute-done.2.got_g
  27.7 0.7 copy-done.3
  28.3 0.3 collective-permute-done.1.got_x
  28.6 0.7 copy-done.5
  29.3 0.0 collective-permute-done.3.got_t
  29.3 0.7 copy-done.1
  30.0 1.0 copy-done.2
  31.0 0.9 copy-done.4
  32.0 0.9 copy-done.6
  32.9 0.9 shard_map.113.job
  33.8 9.0 %all-to-all-done.mine_far = bf16[16,128,256]{2,1,0:T(8,128)(2,1)} async-done(((bf16[16,128,256]{2,1,0:T(8,128)(2,1)}), bf16[16,128,256]{2,1,0:T(8,128)(2,1)}, u32[]{:S(2)}, u32[]{:S(2)}) %all-to-all-start) | async-done | bytes 1048608 | tf_op jit(solution)/shard_map/all_to_all | solution.py:259
  42.7 1.9 %collective-permute-start.4 = (bf16[16,128,256]{2,1,0:T(8,128)(2,1)}, bf16[16,128,256]{2,1,0:T(8,128)(2,1)S(1)}, u32[]{:S(2)}, u32[]{:S(2)}) collective-permute-start(bf16[16,128,256]{2,1,0:T(8,128)(2,1)} %all-to-all-done.mine_far), channel_id=1, source_target_pairs={{0,1},{1,0},{2,3},{3,2},{4,5},{5,4},{6,7},{7,6},{8,9},{9,8},{10,11... | collective-permute-start | bytes 3145736 | tf_op jit(solution)/shard_map/ppermute | solution.py:255
  44.7 2.8 %collective-permute-done.4.got = bf16[16,128,256]{2,1,0:T(8,128)(2,1)S(1)} collective-permute-done((bf16[16,128,256]{2,1,0:T(8,128)(2,1)}, bf16[16,128,256]{2,1,0:T(8,128)(2,1)S(1)}, u32[]{:S(2)}, u32[]{:S(2)}) %collective-permute-start.4) | collective-permute-done | bytes 1048608 | tf_op jit(solution)/shard_map/ppermute | solution.py:255
  47.5 9.6 %shard_map.114 = (bf16[8,128,256]{2,1,0:T(8,128)(2,1)S(1)}, bf16[8,128,256]{2,1,0:T(8,128)(2,1)S(1)}, bf16[8,32,256]{2,1,0:T(8,128)(2,1)S(1)}) custom-call(s32[29]{0:T(128)S(1)} %pad_add_fusion.1.info, f32[8]{0:T(128)S(1)} %add_log_fusion.rates, bf16[384,1536]{1,0:T(8,128)(2,1)S(1)} %shard_map.113.job, bf16[16,128,256]{2,1,0:T(8,128)(2,1)} %all-to-all-done.mine_far, ...), custom_call_target="tpu_custom_call" | custom-call | flops 2800000000 | bytes 10000000 | tf_op jit(solution)/shard_map/pallas_call | solution.py:338
  57.1 14.6 %all_to_all.25.pieces = bf16[8,128,256]{2,1,0:T(8,128)(2,1)S(1)} all-to-all(bf16[8,128,256]{2,1,0:T(8,128)(2,1)S(1)} %get-tuple-element.20), channel_id=1, replica_groups={{0,2,16,18,32,34,48,50},{1,3,17,19,33,35,49,51},{4,6,20,22,36,38,52,54}..., dimensions={0} | all-to-all | bytes 1048576 | tf_op jit(solution)/shard_map/all_to_all | solution.py:259
  71.7 0.1 shard_map.115
  71.8 21.8 %all_to_all.26.arrived = bf16[8,176,256]{2,1,0:T(8,128)(2,1)S(1)} all-to-all(bf16[8,176,256]{2,1,0:T(8,128)(2,1)S(1)} %shard_map.115), channel_id=1, replica_groups=mesh['section'=8,'dom'=64] {'section'}, dimensions={0} | all-to-all | bytes 1441792 | tf_op jit(solution)/shard_map/all_to_all | solution.py:259
  93.7 0.6 broadcast_in_dim.10
  94.3 5.9 %all-to-all-start.3 = ((bf16[4,16,256]{2,1,0:T(8,128)(2,1)}), bf16[4,16,256]{2,1,0:T(8,128)(2,1)S(1)}, u32[]{:S(2)}, u32[]{:S(2)}) async-start(bf16[4,16,256]{2,1,0:T(8,128)(2,1)} %broadcast_in_dim.10), calls=%async_computation.3 | async-start | bytes 65536 | tf_op jit(solution)/shard_map/all_to_all | solution.py:259
  100.3 5.9 %collective-permute-start.6 = (bf16[4,128,256]{2,1,0:T(8,128)(2,1)S(1)}, bf16[4,128,256]{2,1,0:T(8,128)(2,1)S(1)}, u32[]{:S(2)}, u32[]{:S(2)}) collective-permute-start(bf16[4,128,256]{2,1,0:T(8,128)(2,1)S(1)} %get-tuple-element.30), channel_id=1, source_target_pairs={{0,63},{1,2},{2,1},{3,4},{4,3},{5,6},{6,5},{7,8},{8,7},{9,10},{10,... | collective-permute-start | bytes 786440 | tf_op jit(solution)/shard_map/ppermute | solution.py:401
  106.1 0.8 all-to-all-done.3
  107.0 0.7 broadcast_in_dim.11
  107.6 8.1 %all-to-all-start.4 = ((bf16[16,16,256]{2,1,0:T(8,128)(2,1)}), bf16[16,16,256]{2,1,0:T(8,128)(2,1)S(1)}, u32[]{:S(2)}, u32[]{:S(2)}) async-start(bf16[16,16,256]{2,1,0:T(8,128)(2,1)} %broadcast_in_dim.11), calls=%async_computation.4 | async-start | bytes 262144 | tf_op jit(solution)/shard_map/all_to_all | solution.py:259
  115.7 2.1 %collective-permute-start.5 = (bf16[4,32,256]{2,1,0:T(8,128)(2,1)S(1)}, bf16[4,32,256]{2,1,0:T(8,128)(2,1)S(1)}, u32[]{:S(2)}, u32[]{:S(2)}) collective-permute-start(bf16[4,32,256]{2,1,0:T(8,128)(2,1)S(1)} %get-tuple-element.28), channel_id=1, source_target_pairs={{0,1},{1,0},{2,3},{3,2},{4,5},{5,4},{6,7},{7,6},{8,9},{9,8},{10,11... | collective-permute-start | bytes 196616 | tf_op jit(solution)/shard_map/ppermute | solution.py:255
  117.8 1.0 collective-permute-done.5.passed
  118.8 0.0 collective-permute-done.6.comes
  118.8 0.9 shard_map.118
  119.7 2.2 %all-to-all-done.4.spread = bf16[16,16,256]{2,1,0:T(8,128)(2,1)S(1)} async-done(((bf16[16,16,256]{2,1,0:T(8,128)(2,1)}), bf16[16,16,256]{2,1,0:T(8,128)(2,1)S(1)}, u32[]{:S(2)}, u32[]{:S(2)}) %all-to-all-start.4) | async-done | bytes 131104 | tf_op jit(solution)/shard_map/all_to_all | solution.py:259
  121.9 0.7 shard_map.117
  (14 shorter events, 0.1 us)
Async XLA Ops:
  0.6 21.6 %copy-start = (bf16[4,12,128,128]{3,2,1,0:T(8,128)(2,1)S(1)}, bf16[4,12,128,128]{3,2,1,0:T(8,128)(2,1)}, u32[]{:S(2)}) copy-start(bf16[4,12,128,128]{3,2,1,0:T(8,128)(2,1)} %param.13) | copy-start | bytes 4718596
  0.7 14.0 %copy-start.8 = (s32[4,1]{0,1:T(1,128)S(1)}, s32[4,1]{0,1:T(1,128)}, u32[]{:S(2)}) copy-start(s32[4,1]{0,1:T(1,128)} %param.16) | copy-start | bytes 52
  0.7 14.6 %copy-start.7 = (s32[4,2]{0,1:T(2,128)S(1)}, s32[4,2]{0,1:T(2,128)}, u32[]{:S(2)}) copy-start(s32[4,2]{0,1:T(2,128)} %param.17) | copy-start | bytes 100
  2.8 39.9 %all-to-all-start = ((bf16[16,128,256]{2,1,0:T(8,128)(2,1)}), bf16[16,128,256]{2,1,0:T(8,128)(2,1)}, u32[]{:S(2)}, u32[]{:S(2)}) async-start(bf16[16,128,256]{2,1,0:T(8,128)(2,1)} %bitcast.17), calls=%async_computation | async-start | bytes 2097152 | tf_op jit(solution)/shard_map/all_to_all | solution.py:259
  16.9 10.6 %collective-permute-start = (s32[27]{0:T(128)S(1)}, s32[27]{0:T(128)S(1)}, u32[]{:S(2)}, u32[]{:S(2)}) collective-permute-start(s32[27]{0:T(128)S(1)} %pad_add_fusion), channel_id=1, source_target_pairs={{0,1},{1,0},{2,3},{3,2},{4,5},{5,4},{6,7},{7,6},{8,9},{9,8},{10,11... | collective-permute-start | bytes 332 | tf_op jit(solution)/shard_map/ppermute | solution.py:255
  19.9 7.7 %collective-permute-start.2 = (bf16[384,256]{1,0:T(8,128)(2,1)S(1)}, bf16[384,256]{1,0:T(8,128)(2,1)S(1)}, u32[]{:S(2)}, u32[]{:S(2)}) collective-permute-start(bf16[384,256]{1,0:T(8,128)(2,1)S(1)} %dynamic-slice_bitcast_fusion.1.own_g), channel_id=1, source_target_pairs={{0,1},{1,0},{2,3},{3,2},{4,5},{5,4},{6,7},{7,6},{8,9},{9,8},{10,11... | collective-permute-start | bytes 589832 | tf_op jit(solution)/shard_map/ppermute | solution.py:255
  22.2 7.1 %collective-permute-start.3 = (bf16[12,128,128]{2,1,0:T(8,128)(2,1)S(1)}, bf16[12,128,128]{2,1,0:T(8,128)(2,1)S(1)}, u32[]{:S(2)}, u32[]{:S(2)}) collective-permute-start(bf16[12,128,128]{2,1,0:T(8,128)(2,1)S(1)} %dynamic-slice_bitcast_fusion.own_t), channel_id=1, source_target_pairs={{0,1},{1,0},{2,3},{3,2},{4,5},{5,4},{6,7},{7,6},{8,9},{9,8},{10,11... | collective-permute-start | bytes 1179656 | tf_op jit(solution)/shard_map/ppermute | solution.py:255
  25.3 3.3 %collective-permute-start.1 = (bf16[384,256]{1,0:T(8,128)(2,1)S(1)}, bf16[384,256]{1,0:T(8,128)(2,1)S(1)}, u32[]{:S(2)}, u32[]{:S(2)}) collective-permute-start(bf16[384,256]{1,0:T(8,128)(2,1)S(1)} %dynamic-slice_bitcast_fusion.2.own_x), channel_id=1, source_target_pairs={{0,1},{1,0},{2,3},{3,2},{4,5},{5,4},{6,7},{7,6},{8,9},{9,8},{10,11... | collective-permute-start | bytes 589832 | tf_op jit(solution)/shard_map/ppermute | solution.py:255
  27.7 0.7 copy-start.3
  28.6 0.7 copy-start.5
  29.3 0.7 copy-start.1
  30.0 1.0 copy-start.2
  31.0 0.9 copy-start.4
  32.0 0.9 copy-start.6
  42.7 4.8 %collective-permute-start.4 = (bf16[16,128,256]{2,1,0:T(8,128)(2,1)}, bf16[16,128,256]{2,1,0:T(8,128)(2,1)S(1)}, u32[]{:S(2)}, u32[]{:S(2)}) collective-permute-start(bf16[16,128,256]{2,1,0:T(8,128)(2,1)} %all-to-all-done.mine_far), channel_id=1, source_target_pairs={{0,1},{1,0},{2,3},{3,2},{4,5},{5,4},{6,7},{7,6},{8,9},{9,8},{10,11... | collective-permute-start | bytes 3145736 | tf_op jit(solution)/shard_map/ppermute | solution.py:255
  94.3 12.6 %all-to-all-start.3 = ((bf16[4,16,256]{2,1,0:T(8,128)(2,1)}), bf16[4,16,256]{2,1,0:T(8,128)(2,1)S(1)}, u32[]{:S(2)}, u32[]{:S(2)}) async-start(bf16[4,16,256]{2,1,0:T(8,128)(2,1)} %broadcast_in_dim.10), calls=%async_computation.3 | async-start | bytes 65536 | tf_op jit(solution)/shard_map/all_to_all | solution.py:259
  100.3 18.6 %collective-permute-start.6 = (bf16[4,128,256]{2,1,0:T(8,128)(2,1)S(1)}, bf16[4,128,256]{2,1,0:T(8,128)(2,1)S(1)}, u32[]{:S(2)}, u32[]{:S(2)}) collective-permute-start(bf16[4,128,256]{2,1,0:T(8,128)(2,1)S(1)} %get-tuple-element.30), channel_id=1, source_target_pairs={{0,63},{1,2},{2,1},{3,4},{4,3},{5,6},{6,5},{7,8},{8,7},{9,10},{10,... | collective-permute-start | bytes 786440 | tf_op jit(solution)/shard_map/ppermute | solution.py:401
  107.6 14.3 %all-to-all-start.4 = ((bf16[16,16,256]{2,1,0:T(8,128)(2,1)}), bf16[16,16,256]{2,1,0:T(8,128)(2,1)S(1)}, u32[]{:S(2)}, u32[]{:S(2)}) async-start(bf16[16,16,256]{2,1,0:T(8,128)(2,1)} %broadcast_in_dim.11), calls=%async_computation.4 | async-start | bytes 262144 | tf_op jit(solution)/shard_map/all_to_all | solution.py:259
  115.7 3.1 %collective-permute-start.5 = (bf16[4,32,256]{2,1,0:T(8,128)(2,1)S(1)}, bf16[4,32,256]{2,1,0:T(8,128)(2,1)S(1)}, u32[]{:S(2)}, u32[]{:S(2)}) collective-permute-start(bf16[4,32,256]{2,1,0:T(8,128)(2,1)S(1)} %get-tuple-element.28), channel_id=1, source_target_pairs={{0,1},{1,0},{2,3},{3,2},{4,5},{5,4},{6,7},{7,6},{8,9},{9,8},{10,11... | collective-permute-start | bytes 196616 | tf_op jit(solution)/shard_map/ppermute | solution.py:255
